TPU v7x, 32 devices: a whole 2x2x4 slice. The times are simulated.
32 devices in a mesh: ctx: 8 (over z, y), tp: 4 (over x, core).
Axes of the slice: x: 2, y: 2, z: 4, core: 2. Of those that a mesh axis runs over, the one named last changes fastest.
Arguments:
- queries: bfloat16 [1024, 8192], P('ctx', 'tp'), may hold values from -56 to 56
- suffix_kv: bfloat16 [2, 1024, 1024], P(None, 'ctx', 'tp'), may hold values from -6 to 6
- cache_pool: bfloat16 [2, 128, 128, 1024], P(None, 'ctx', None, 'tp'), may hold values from -6 to 6
- hit_count: int32 [8], replicated, may hold values from 1 to 3, as said below
- hit_slots: int32 [8, 3], P('ctx'), may hold values from 0 to 15, as said below
- out_weight: bfloat16 [8192, 8192], P('tp', 'ctx'), may hold values from -1.1953125 to 1.1953125
Outputs:
- layer_out: bfloat16 [1024, 8192], P('tp', 'ctx')
Inputs may be any that keep to these rules, and one draw needn't show every extreme that they name: hit_count[h] blocks of holder h belong to the prefix; some holder has exactly 3. `hit_slots`: row h names 3 distinct slots of holder h's pool; only its first hit_count[h] entries are hits, the others are unused.
All inputs are finite; a program needn't handle non-finite values.
Results may differ from a plain program's by a relative error of at most 0.024.
Values may be sent and summed in bfloat16 or wider, within the bound.
No kernel may reach another device: no remote copies, remote signals or barrier semaphores. Data moves between devices by JAX's collectives and lax.ppermute only.
A program may use at most 64 MiB of HBM per device.

v0:
```python
import math

import jax
import jax.numpy as jnp
from jax import lax
from jax.sharding import PartitionSpec as P

HD = 128
HCAP = 3


neg_fill = -1e30
blocks_per_turn = 4


def begin_state(query_count, slots_dev, group_size, head_width):
    return (
        jnp.full((query_count, slots_dev, group_size), neg_fill, jnp.float32),
        jnp.zeros((query_count, slots_dev, group_size), jnp.float32),
        jnp.zeros((query_count, slots_dev, group_size, head_width), jnp.float32),
    )


def absorb(softmax_state, query_heads, key_block, visible):
    running_max, running_sum, running_acc = softmax_state
    slots_dev = query_heads.shape[1]
    head_width = query_heads.shape[3]
    key_count = key_block.shape[1]
    key_rows = key_block[0].reshape(key_count, slots_dev, head_width)
    value_rows = key_block[1].reshape(key_count, slots_dev, head_width)
    scores = jnp.einsum(
        "qsgd,ksd->qsgk", query_heads, key_rows, preferred_element_type=jnp.float32
    ) / math.sqrt(head_width)
    mask_all = visible[:, None, None, :]
    scores = jnp.where(mask_all, scores, neg_fill)
    new_max = jnp.maximum(running_max, jnp.max(scores, axis=-1))
    weights = jnp.where(mask_all, jnp.exp(scores - new_max[..., None]), 0.0)
    rescale = jnp.exp(running_max - new_max)
    new_sum = running_sum * rescale + jnp.sum(weights, axis=-1)
    rounded_weights = weights.astype(jnp.bfloat16)
    new_acc = running_acc * rescale[..., None] + jnp.einsum(
        "qsgk,ksd->qsgd", rounded_weights, value_rows, preferred_element_type=jnp.float32
    )
    return (new_max, new_sum, new_acc)


def prefix_visible(slot_index, hit_count):
    holder = slot_index // HCAP
    within = slot_index % HCAP
    holders = jnp.arange(hit_count.shape[0], dtype=jnp.int32)
    counted = jnp.sum(jnp.where(holder[:, None] == holders[None, :], hit_count[None, :], 0), axis=1)
    return within < counted


def body(queries, suffix_kv, cache_pool, hit_count, hit_slots, out_weight):
    tok_rows = queries.shape[0]
    slots_dev = suffix_kv.shape[2] // HD
    heads_dev = queries.shape[1] // HD
    group_size = heads_dev // slots_dev
    query_heads = queries.reshape(tok_rows, slots_dev, group_size, HD)
    my_index = lax.axis_index("ctx")
    query_pos = my_index * tok_rows + jnp.arange(tok_rows, dtype=jnp.int32)
    last_query = my_index * tok_rows + tok_rows - 1
    block_rows = cache_pool.shape[2]
    row_width = cache_pool.shape[3]
    picked = jnp.take(cache_pool, hit_slots[0], axis=1)
    initial = begin_state(tok_rows, slots_dev, group_size, HD)
    fragment = lax.all_gather(picked, "ctx", axis=1, tiled=True)
    slot_count = fragment.shape[1]
    step_size = math.gcd(slot_count, blocks_per_turn * HCAP)
    flattened = fragment.reshape(2, slot_count * block_rows, row_width)

    def advance(position, current):
        key_block = lax.dynamic_slice_in_dim(
            flattened, position * step_size * block_rows, step_size * block_rows, 1
        )
        slot_index = (
            position * step_size + jnp.arange(step_size * block_rows, dtype=jnp.int32) // block_rows
        )
        visible = prefix_visible(slot_index, hit_count)[None, :]
        return absorb(current, query_heads, key_block, visible)

    after_prefix = lax.fori_loop(0, slot_count // step_size, advance, initial)
    fragment = lax.all_gather(suffix_kv, "ctx", axis=1, tiled=True)
    row_count = fragment.shape[1]
    fold_step_size = math.gcd(row_count, blocks_per_turn * tok_rows)

    def advance(position, current):
        first_key = position * fold_step_size

        def include(running):
            key_block = lax.dynamic_slice_in_dim(
                fragment, position * fold_step_size, fold_step_size, 1
            )
            key_pos = first_key + jnp.arange(fold_step_size, dtype=jnp.int32)
            return absorb(running, query_heads, key_block, key_pos[None, :] <= query_pos[:, None])

        return lax.cond(first_key <= last_query, include, lambda running: running, current)

    final_state = lax.fori_loop(0, row_count // fold_step_size, advance, after_prefix)
    running_max, running_sum, running_acc = final_state
    attention = (
        (running_acc / running_sum[..., None])
        .reshape(tok_rows, heads_dev * HD)
        .astype(jnp.bfloat16)
    )
    gathered = lax.all_gather(attention, "ctx", axis=0, tiled=True)
    return lax.psum_scatter(
        jnp.dot(gathered, out_weight, preferred_element_type=jnp.float32).astype(jnp.bfloat16),
        "tp",
        scatter_dimension=0,
        tiled=True,
    )


def solution(mesh):
    placed = (
        P("ctx", "tp"),
        P(None, "ctx", "tp"),
        P(None, "ctx", None, "tp"),
        P(),
        P("ctx", None),
        P("tp", "ctx"),
    )
    return jax.shard_map(
        body, mesh=mesh, in_specs=placed, out_specs=P("tp", "ctx"), check_vma=False
    )
```

profile of v0, /device:TPU:0, one launch (start us, length us, event | category | flops | bytes accessed | tf_op | source)
XLA Modules:
  0.0 262.3 jit_solution(7199013966016222260)
XLA Ops:
  6.5 0.8 fusion.48
  7.3 0.7 compare_and_fusion
  8.1 0.6 gather_fusion
  8.7 0.8 select_bitcast_fusion
  9.6 1.7 copy.46
  11.4 1.3 copy.43
  13.0 59.9 %all-gather.4.cloned.1.call-done = bf16[2,24,128,256]{3,2,0,1:T(8,128)(2,1)} async-done(((bf16[2,3,128,256]{3,2,0,1:T(8,128)(2,1)}), bf16[2,24,128,256]{3,2,0,1:T(8,128)(2,1)}) %all-gather.4.cloned.1.call-update) | async-done | bytes 3145744 | tf_op jit(solution)/shard_map/all_gather | solution.py:68
  72.9 3.9 %copy.42 = bf16[2,24,128,256]{3,2,1,0:T(8,128)(2,1)} copy(bf16[2,24,128,256]{3,2,0,1:T(8,128)(2,1)} %all-gather.4.cloned.1.call-done) | data formatting | bytes 6291456 | tf_op jit(solution)/shard_map/all_gather | solution.py:68
  76.8 52.8 %while.40 = (s32[]{:T(128)}, f32[128,2,8]{0,2,1:T(8,128)S(1)}, f32[128,2,8]{0,2,1:T(8,128)S(1)}, f32[128,2,8,128]{0,3,2,1:T(8,128)}, s32[8]{0:T(128)S(1)}, /*ind...) while((s32[]{:T(128)}, f32[128,2,8]{0,2,1:T(8,128)S(1)}, ...), condition=%wide.region_4.5_spmd.clone, body=%wide.region_0.4_spmd.clone.sunk | while | flops 1652389888 | bytes 51542296 | solution.py:83
  76.8 2.6 constant_dynamic-slice_fusion.5
  79.4 1.4 copy.63
  80.9 6.2 %bitcast_reduce_fusion.2 = (f32[128,2,8]{0,2,1:T(8,128)S(1)}, f32[2,1536,128,8]{2,1,3,0:T(8,128)}) fusion(pred[1536]{0:T(1024)(128)(4,1)S(1)} %fusion.69, bf16[1536,2,128,1]{0,2,3,1:T(8,128)(2,1)S(1)} %bitcast.96, bf16[128,2,8,128]{3,0,2,1:T(8,128)(2,1)S(1)} %get-tuple-element.701), kind=kOutput, calls=%fused_computation.22.clone.1 | convolution fusion | flops 814741504 | bytes 13903360 | tf_op jit(solution)/shard_map/while/body/eval_jaxpr/qsgd,ksd->qsgk/dot_general | solution.py:31
  87.1 6.9 %fusion.70 = f32[128,2,8]{0,2,1:T(8,128)S(1)} fusion(f32[2,1536,128,8]{2,1,3,0:T(8,128)} %get-tuple-element.659, f32[128,2,8]{0,2,1:T(8,128)S(1)} %select_maximum_fusion.2, pred[1536]{0:T(1024)(128)(4,1)S(1)} %fusion.69), kind=kLoop, calls=%fused_computation.27.clone.1 | loop fusion | flops 15726592 | bytes 12600832 | tf_op jit(solution)/shard_map/while/body/eval_jaxpr/reduce_sum | solution.py:39
  94.0 1.2 copy.64
  95.2 7.9 %fusion.72 = f32[128,2,8,128]{0,3,2,1:T(8,128)} fusion(bf16[1536,2,128,1]{0,2,3,1:T(8,128)(2,1)} %bitcast.99, f32[2,1536,128,8]{2,1,3,0:T(8,128)} %get-tuple-element.659, f32[128,2,8]{0,2,1:T(8,128)S(1)} %select_maximum_fusion.2, pred[1536]{0:T(1024)(128)(4,1)S(1)} %fusion.69, f32[128,2,8,128]{0,3,2,1:T(8,128)} %get-tuple-element.685, ...), kind=kOutput, calls=%fused_computation.32.clone.1 | convolution fusion | flops 821821440 | bytes 15484417 | tf_op jit(solution)/shard_map/while/body/eval_jaxpr/qsgk,ksd->qsgd/dot_general | solution.py:41
  103.1 2.6 constant_dynamic-slice_fusion.5
  105.7 1.4 copy.63
  107.3 6.1 %bitcast_reduce_fusion.2 = (f32[128,2,8]{0,2,1:T(8,128)S(1)}, f32[2,1536,128,8]{2,1,3,0:T(8,128)}) fusion(pred[1536]{0:T(1024)(128)(4,1)S(1)} %fusion.69, bf16[1536,2,128,1]{0,2,3,1:T(8,128)(2,1)S(1)} %bitcast.96, bf16[128,2,8,128]{3,0,2,1:T(8,128)(2,1)S(1)} %get-tuple-element.701), kind=kOutput, calls=%fused_computation.22.clone.1 | convolution fusion | flops 814741504 | bytes 13903360 | tf_op jit(solution)/shard_map/while/body/eval_jaxpr/qsgd,ksd->qsgk/dot_general | solution.py:31
  113.4 6.8 %fusion.70 = f32[128,2,8]{0,2,1:T(8,128)S(1)} fusion(f32[2,1536,128,8]{2,1,3,0:T(8,128)} %get-tuple-element.659, f32[128,2,8]{0,2,1:T(8,128)S(1)} %select_maximum_fusion.2, pred[1536]{0:T(1024)(128)(4,1)S(1)} %fusion.69), kind=kLoop, calls=%fused_computation.27.clone.1 | loop fusion | flops 15726592 | bytes 12600832 | tf_op jit(solution)/shard_map/while/body/eval_jaxpr/reduce_sum | solution.py:39
  120.3 1.2 copy.64
  121.5 8.0 %fusion.72 = f32[128,2,8,128]{0,3,2,1:T(8,128)} fusion(bf16[1536,2,128,1]{0,2,3,1:T(8,128)(2,1)} %bitcast.99, f32[2,1536,128,8]{2,1,3,0:T(8,128)} %get-tuple-element.659, f32[128,2,8]{0,2,1:T(8,128)S(1)} %select_maximum_fusion.2, pred[1536]{0:T(1024)(128)(4,1)S(1)} %fusion.69, f32[128,2,8,128]{0,3,2,1:T(8,128)} %get-tuple-element.685, ...), kind=kOutput, calls=%fused_computation.32.clone.1 | convolution fusion | flops 821821440 | bytes 15484417 | tf_op jit(solution)/shard_map/while/body/eval_jaxpr/qsgk,ksd->qsgd/dot_general | solution.py:41
  129.6 5.6 %while.39 = (s32[]{:T(128)}, f32[128,2,8]{0,2,1:T(8,128)S(1)}, f32[128,2,8]{0,2,1:T(8,128)S(1)}, f32[128,2,8,128]{0,3,2,1:T(8,128)}, s32[]{:T(128)}, /*index=5*/...) while((s32[]{:T(128)}, f32[128,2,8]{0,2,1:T(8,128)S(1)}, ...), condition=%wide.region_10.11_spmd.clone, body=%wide.region_5.10_spmd.clone.sunk | while | flops 551096960 | bytes 25565568 | solution.py:100
  129.6 5.6 %conditional.3 = ((f32[128,2,8]{0,2,1:T(8,128)S(1)}, f32[128,2,8]{0,2,1:T(8,128)S(1)}, f32[128,2,8,128]{0,3,2,1:T(8,128)})) conditional(s32[]{:T(128)} %convert_element_type.51, (f32[128,2,8]{0,2,1:T(8,128)S(1)}, f32[128,2,8]{0,2,1:T(8,128)S(1)}, f32[128,2,8,128]{0,3,2,1:T(8,128)}) %tuple.96, (s32[]{:T(128)}, s32[]{:T(128)}, s32[]{:T(128)}, ...), branch_computations={%region_6.6_spmd, %region_7.9_spmd} | conditional | flops 551096960 | bytes 25564834 | solution.py:98
  129.6 1.1 constant_dynamic-slice_fusion.1
  130.8 0.8 fusion.2
  131.7 1.0 fusion.4
  132.7 1.4 fusion.11
  134.2 1.0 copy-done.3
  135.1 2.1 divide_convert_fusion
  137.5 79.0 %all-gather.8.cloned.1.call-done = bf16[1024,2048]{0,1:T(8,128)(2,1)} async-done(((bf16[128,2048]{0,1:T(8,128)(2,1)}), bf16[1024,2048]{0,1:T(8,128)(2,1)}) %all-gather.8.cloned.1.call-update) | async-done | bytes 4194320 | tf_op jit(solution)/shard_map/all_gather | solution.py:107
  216.6 9.4 %convolution_convert_fusion = bf16[1024,1024]{1,0:T(8,128)(2,1)} fusion(bf16[1024,2048]{0,1:T(8,128)(2,1)} %all-gather.8.cloned.1.call-done, bf16[2048,1024]{1,0:T(8,128)(2,1)} %param.17), kind=kOutput, calls=%fused_computation.64 | convolution fusion | flops 4296015872 | bytes 10485760 | tf_op jit(solution)/shard_map/dot_general | solution.py:109
  226.0 29.8 %reduce-scatter.2.cloned.1.call-done = bf16[256,1024]{1,0:T(8,128)(2,1)} async-done(((bf16[1024,1024]{1,0:T(8,128)(2,1)}), bf16[256,1024]{1,0:T(8,128)(2,1)}) %reduce-scatter.2.cloned.1.call-update) | async-done | bytes 524304 | tf_op jit(solution)/shard_map/reduce_scatter | solution.py:108
  (46 shorter events, 1.3 us)
Async XLA Ops:
  6.5 1.6 copy-start
  6.5 66.4 %all-gather.4.cloned.1.call-start = ((), (), s32[]{:S(2)}) async-start(), calls=%async_computation.1 | async-start | bytes 3538944 | tf_op jit(solution)/shard_map/all_gather | solution.py:68
  9.6 120.0 %all-gather.6.cloned.1.call-start = ((), (), s32[]{:S(2)}) async-start(), calls=%async_computation.2 | async-start | bytes 1179648 | tf_op jit(solution)/shard_map/all_gather | solution.py:84
  11.3 205.2 %all-gather.8.cloned.1.call-start = ((), (), s32[]{:S(2)}) async-start(), calls=%async_computation.3 | async-start | bytes 4718592 | tf_op jit(solution)/shard_map/all_gather | solution.py:107
  11.4 65.4 %copy-start.4 = (s32[8]{0:T(128)S(1)}, s32[8]{0:T(128)}, u32[]{:S(2)}) copy-start(s32[8]{0:T(128)} %param.15) | copy-start | bytes 100
  87.1 6.9 %copy-start.1 = (bf16[1,1536,256]{2,1,0:T(8,128)(2,1)S(1)}, bf16[1,1536,256]{2,1,0:T(8,128)(2,1)}, u32[]{:S(2)}) copy-start(bf16[1,1536,256]{2,1,0:T(8,128)(2,1)} %get-tuple-element.661) | copy-start | bytes 2359300 | tf_op jit(solution)/shard_map/while
  113.4 6.9 %copy-start.1 = (bf16[1,1536,256]{2,1,0:T(8,128)(2,1)S(1)}, bf16[1,1536,256]{2,1,0:T(8,128)(2,1)}, u32[]{:S(2)}) copy-start(bf16[1,1536,256]{2,1,0:T(8,128)(2,1)} %get-tuple-element.661) | copy-start | bytes 2359300 | tf_op jit(solution)/shard_map/while
  130.8 1.9 copy-start.2
  134.1 1.0 copy-start.3
  137.3 118.4 %reduce-scatter.2.cloned.1.call-start = ((), (), s32[]{:S(2)}) async-start(), calls=%async_computation.4 | async-start | bytes 2621440 | tf_op jit(solution)/shard_map/reduce_scatter | solution.py:108
Sparse Core Ops, SparseCore 0:
  9.7 63.1 all-gather.3
  74.9 38.1 all-gather.5
  137.4 79.0 all-gather.7
  226.1 29.5 reduce-scatter.1
where the time goes:
time: 263 us; the launch traced here: 262 us
  waiting for transfers between devices  169 us (64%)
  matrix products  39.8 us (15%)
  local copies, waits for them, and re-layouts  20.4 us (8%)
  other arithmetic  19.6 us (7%)
  between operations  13.2 us (5%)
    all_gather x1, waiting for transfers between devices, body(): gathered = lax.all_gather(attention, 'ctx', axis=0, tiled=True)  79 us
    all_gather x1, waiting for transfers between devices, body(): fragment = lax.all_gather(picked, 'ctx', axis=1, tiled=True)  59.9 us
    reduce_scatter x1, waiting for transfers between devices, body(): lax.psum_scatter(jnp.dot(gathered, out_weight, preferred_element_type=jnp...  29.8 us
    dot_general x3, matrix products, absorb(): jnp.einsum('qsgk,ksd->qsgd', rounded_weights, value_rows, preferred_eleme...  17.3 us
    reduce_sum x3, other arithmetic, absorb(): new_sum = running_sum * rescale + jnp.sum(weights, axis=-1)  14.7 us
    dot_general x3, matrix products, absorb(): jnp.einsum('qsgd,ksd->qsgk', query_heads, key_rows, preferred_element_typ...  13.1 us
    dot_general x1, matrix products, body(): jnp.dot(gathered, out_weight, preferred_element_type=jnp.float32)  9.37 us
    slice x3, local copies, waits for them, and re-layouts, absorb(): value_rows = key_block[1].reshape(key_count, slots_dev, head_width)  6.29 us
  transfers between devices with their start and end apart: 4, of which 3 were waited for; matrix products, arithmetic and copies ran while one was open for 23% of the time, Pallas kernels for 0%

commit v1 on v0

v1 whole, which is shorter than its diff:
```python
import functools
import math

import jax
import jax.numpy as jnp
from jax import lax
from jax.experimental import pallas as pl
from jax.experimental.pallas import tpu as pltpu
from jax.sharding import PartitionSpec as P

HD = 128
HCAP = 3
neg_fill = -1e30
score_scale = 1.0 / math.sqrt(HD)
kernel_vmem = 16 * 1024 * 1024

vmem = pl.BlockSpec(memory_space=pltpu.VMEM)
smem = pl.BlockSpec(memory_space=pltpu.SMEM)
hbm = pl.BlockSpec(memory_space=pltpu.HBM)
params = pltpu.CompilerParams(vmem_limit_bytes=kernel_vmem)
light = pl.CostEstimate(flops=1000, bytes_accessed=1000, transcendentals=0)


def ring_order(n):
    return [2 * q if 2 * q < n else 2 * (n - 1 - q) + 1 for q in range(n)]


def owner_of(me, step, n):
    place = jnp.where(me % 2 == 0, me // 2, n - 1 - me // 2)
    place = lax.rem(place + step + n, n)
    return jnp.where(2 * place < n, 2 * place, 2 * (n - 1 - place) + 1)


def pick_kernel(blk, hit_slots, pool_ref, suffix_ref, near_ref, rest_ref, held, slots_ref, slots_sem, sems):
    outs = (near_ref, rest_ref)
    fetch = pltpu.make_async_copy(hit_slots, slots_ref, slots_sem)
    fetch.start()
    fetch.wait()
    copies = []
    for kv in range(2):
        for place in range(HCAP + 1):
            if place == 0:
                src = suffix_ref.at[kv]
            else:
                src = pool_ref.at[kv, slots_ref[0, place - 1]]
            if kv == 0:
                dst = outs[place // 2].at[0, pl.ds(place % 2 * blk, blk), :]
            else:
                dst = held.at[place]
            copies.append(pltpu.make_async_copy(src, dst, sems.at[kv, place]))
    for copy in copies:
        copy.start()
    for copy in copies:
        copy.wait()
    for place in range(HCAP + 1):
        for lane in range(0, held.shape[2], HD):
            at = slice(place % 2 * blk, (place % 2 + 1) * blk)
            outs[place // 2][1, at, lane : lane + HD] = held[place, :, lane : lane + HD].T


def pick(hit_slots, cache_pool, suffix_kv):
    blk, wide = cache_pool.shape[2:]
    return pl.pallas_call(
        functools.partial(pick_kernel, blk),
        out_shape=[jax.ShapeDtypeStruct((2, 2 * blk, wide), jnp.bfloat16)] * 2,
        in_specs=[hbm, hbm, hbm],
        out_specs=[vmem, vmem],
        scratch_shapes=[
            pltpu.VMEM((HCAP + 1, blk, wide), jnp.bfloat16),
            pltpu.SMEM(hit_slots.shape, jnp.int32),
            pltpu.SemaphoreType.DMA,
            pltpu.SemaphoreType.DMA((2, HCAP + 1)),
        ],
        compiler_params=pltpu.CompilerParams(vmem_limit_bytes=60 * 1024 * 1024),
        name="pick",
    )(hit_slots, cache_pool, suffix_kv)


def fold(op, array):
    parts = [array[r : r + 8] for r in range(0, array.shape[0], 8)]
    while len(parts) > 1:
        pairs = [op(a, b) for a, b in zip(parts[::2], parts[1::2])]
        parts = pairs + parts[len(parts) - len(parts) % 2 :]
    return parts[0]


def flash_kernel(n, tok, pieces, first, last, hit_ref, q_ref, *refs):
    count = len(pieces)
    kv_refs, refs = refs[:count], refs[count:]
    me = lax.axis_index("ctx")
    heads = (q_ref.shape[1] if first else q_ref.shape[1] // tok * HD) // HD
    keys, wide = kv_refs[0].shape[1:]
    blk = keys // 2
    slots_dev = wide // HD
    group = heads // slots_dev
    per = 2 if group % 2 == 0 else 1
    rows = per * tok
    biases = []
    for kind, step in pieces:
        owner = owner_of(me, step, n)
        if kind == 0:
            seen = [None if step == 0 else owner < me, None]
        else:
            seen = [hit_ref[owner] > 1, hit_ref[owner] > 2]
        biases.append([0.0 if s is None else jnp.where(s, 0.0, neg_fill) for s in seen])

    def place(j):
        head = j * per
        cols = [slice((head + h) * HD, (head + h + 1) * HD) for h in range(per)]
        slot = head // group
        return cols, slice(head * tok, head * tok + rows), slice(slot * HD, (slot + 1) * HD)

    def score(j):
        cols, at, lanes = place(j)
        if first:
            turned = jnp.concatenate([q_ref[:, c].T for c in cols], axis=1)
            refs[-4][:, at] = turned
        else:
            turned = q_ref[:, at]
        scores = []
        for (kind, step), ref, bias in zip(pieces, kv_refs, biases):
            raw = jnp.dot(ref[0, :, lanes], turned, preferred_element_type=jnp.float32)
            for b in range(2):
                part = raw[b * blk : (b + 1) * blk]
                if (kind, step, b) == (0, 0, 0):
                    key = lax.broadcasted_iota(jnp.int32, part.shape, 0)
                    token = lax.broadcasted_iota(jnp.int32, part.shape, 1) % tok
                    part = jnp.where(key <= token, part, neg_fill)
                scores.append((part, bias[b]))
        return scores

    def weigh(j, scores):
        _, at, _ = place(j)
        tops = [fold(jnp.maximum, part) + bias for part, bias in scores]
        top = jnp.max(functools.reduce(jnp.maximum, tops), axis=0, keepdims=True)
        total = fade = None
        if not first:
            m_in, l_in, _ = refs[:3]
            old_top = m_in[:, at]
            top = jnp.maximum(old_top, top)
            fade = jnp.exp((old_top - top) * score_scale)
            total = l_in[:, at] * fade
        if not last:
            refs[-3][:, at] = jnp.broadcast_to(top, (8, rows))
        offset = top[:1] * score_scale
        probs = []
        for part, bias in scores:
            weights = jnp.exp(part * score_scale - (offset - bias))
            add = fold(jnp.add, weights)
            total = add if total is None else total + add
            probs.append(weights.astype(jnp.bfloat16))
        if not last:
            refs[-2][:, at] = total
        return jnp.concatenate(probs, axis=0), fade, total

    def mix(j, probs, fade, total):
        cols, at, lanes = place(j)
        values = [ref[1, b * blk : (b + 1) * blk, lanes] for ref in kv_refs for b in range(2)]
        mixed = jnp.dot(
            jnp.concatenate(values, axis=1), probs, preferred_element_type=jnp.float32
        )
        if not first:
            mixed = mixed + refs[2][:, at] * fade[:1]
        if not last:
            refs[-1][:, at] = mixed
            return
        result = mixed * (1.0 / jnp.sum(total, axis=0, keepdims=True))
        half = tok // 2
        for h, c in enumerate(cols):
            head_out = result[:, h * tok : (h + 1) * tok].T.astype(jnp.bfloat16)
            for k, out in enumerate(refs[-2:]):
                out[:, c] = head_out[k * half : (k + 1) * half]

    blocks = heads // per
    ahead = min(2, blocks)
    scores = [score(j) for j in range(ahead)]
    for j in range(blocks):
        weighed = weigh(j, scores[j])
        scores[j] = None
        if j + ahead < blocks:
            scores.append(score(j + ahead))
        mix(j, *weighed)


def flash(n, tok, queries, hit_count, pieces, arrays, state, last):
    rows = queries.size // HD
    small = jax.ShapeDtypeStruct((8, rows), jnp.float32)
    if last:
        out_shape = [jax.ShapeDtypeStruct((tok // 2, rows // tok * HD), jnp.bfloat16)] * 2
        aliases = {}
    else:
        out_shape = [small, small, jax.ShapeDtypeStruct((HD, rows), jnp.float32)]
        aliases = {2 + len(arrays) + i: i for i in range(len(state))}
    if not state:
        out_shape = [jax.ShapeDtypeStruct((HD, rows), jnp.bfloat16)] + out_shape
    return pl.pallas_call(
        functools.partial(flash_kernel, n, tok, pieces, not state, last),
        out_shape=out_shape,
        in_specs=[smem] + [vmem] * (1 + len(arrays) + len(state)),
        out_specs=[vmem] * len(out_shape),
        input_output_aliases=aliases,
        compiler_params=params,
        cost_estimate=light,
        name="flash",
    )(hit_count, queries, *arrays, *state)


def project_kernel(count, *refs):
    shard_refs, (w_ref, keep_ref, send_ref) = refs[: 2 * count], refs[2 * count :]
    odd = lax.axis_index("tp") % 2
    rows = jnp.concatenate([ref[...] for ref in shard_refs], axis=0)
    half = rows.shape[0] // (2 * count)
    wide = w_ref.shape[1]
    width = min(256, wide)
    for col in range(0, wide, width):
        at = slice(col, col + width)
        product = jnp.dot(rows, w_ref[:, at], preferred_element_type=jnp.float32)
        product = product.astype(jnp.bfloat16)
        for i in range(count):
            low = product[2 * i * half : (2 * i + 1) * half]
            high = product[(2 * i + 1) * half : (2 * i + 2) * half]

            @pl.when(odd == 0)
            def _():
                keep_ref[i, :, at] = low
                send_ref[i, :, at] = high

            @pl.when(odd == 1)
            def _():
                keep_ref[i, :, at] = high
                send_ref[i, :, at] = low


def project(arrays, out_weight):
    half = arrays[0].shape[0]
    depth, wide = out_weight.shape
    count = len(arrays) // 2
    return pl.pallas_call(
        functools.partial(project_kernel, count),
        out_shape=[jax.ShapeDtypeStruct((count, half, wide), jnp.bfloat16)] * 2,
        in_specs=[vmem] * (len(arrays) + 1),
        out_specs=[vmem, vmem],
        compiler_params=params,
        cost_estimate=light,
        name="project",
    )(*arrays, out_weight)


def sides(n, n_tp, steps):
    me = lax.axis_index("ctx")
    my_tp = lax.axis_index("tp")
    share = n // n_tp
    found, near_count, away_count = [], jnp.int32(0), jnp.int32(0)
    for step in steps:
        owner = owner_of(me, step, n)
        away = lax.bitwise_xor(owner // share, my_tp) // 2 % 2
        found.append((owner, away, jnp.where(away == 1, away_count, near_count)))
        near_count = near_count + 1 - away
        away_count = away_count + away
    return found


def added(a, b):
    return a.astype(jnp.float32) + b.astype(jnp.float32)


def sort_kernel(n, n_tp, steps, *refs):
    *refs, stay_ref, send_ref, last_stay_ref, last_send_ref = refs
    count = len(refs) // 2
    places = [(a, b, i) for a, b in zip(refs[:count], refs[count:]) for i in range(a.shape[0])]
    full = stay_ref.shape[0]
    for (a, b, i), (_, away, rank) in zip(places, sides(n, n_tp, steps)):
        total = added(a[i], b[i]).astype(jnp.bfloat16)
        for side, out, last in ((0, stay_ref, last_stay_ref), (1, send_ref, last_send_ref)):

            @pl.when((away == side) & (rank < full))
            def _():
                out[rank] = total

            @pl.when((away == side) & (rank == full))
            def _():
                last[0] = total


def sort(n, n_tp, steps, sums):
    keeps, gots = zip(*sums)
    half, wide = keeps[0].shape[1:]
    many = jax.ShapeDtypeStruct((n // 2 - 1, half, wide), jnp.bfloat16)
    one = jax.ShapeDtypeStruct((1, half, wide), jnp.bfloat16)
    return pl.pallas_call(
        functools.partial(sort_kernel, n, n_tp, steps),
        out_shape=[many, many, one, one],
        in_specs=[vmem] * (2 * len(sums)),
        out_specs=[vmem] * 4,
        compiler_params=params,
        cost_estimate=light,
        name="sort",
    )(*keeps, *gots)


def last_kernel(n, n_tp, keep_ref, got_ref, stay_in, send_in, stay_ref, send_ref):
    ((_, away, _),) = sides(n, n_tp, (n // 2,))
    total = added(keep_ref[...], got_ref[...]).astype(jnp.bfloat16)
    stay_ref[...] = jnp.where(away == 0, total, stay_in[...])
    send_ref[...] = jnp.where(away == 1, total, send_in[...])


def place_last(n, n_tp, keep, got, stay, send):
    return pl.pallas_call(
        functools.partial(last_kernel, n, n_tp),
        out_shape=[jax.ShapeDtypeStruct(keep.shape, jnp.bfloat16)] * 2,
        in_specs=[vmem] * 4,
        out_specs=[vmem] * 2,
        compiler_params=params,
        cost_estimate=light,
        name="last",
    )(keep, got, stay, send)


def choose_kernel(n, n_tp, steps, *refs):
    stay, got, last_stay, last_got, mine_ref, give_ref = refs
    my_tp = lax.axis_index("tp")
    share = n // n_tp
    found = sides(n, n_tp, steps)
    full = stay.shape[0]
    for r in range(full + 1):
        owner = jnp.int32(0)
        for candidate, away, rank in found:
            owner = jnp.where((away == 0) & (rank == r), candidate, owner)
        if r < full:
            total = added(stay[r], got[r])
        else:
            total = added(last_stay[0], last_got[0])
        for out, block in ((mine_ref, my_tp), (give_ref, lax.bitwise_xor(my_tp, 1))):

            @pl.when(owner // share == block)
            def _():
                out[owner % share] = total.astype(out.dtype)


def choose(n, n_tp, steps, arrays):
    half, wide = arrays[0].shape[1:]
    return pl.pallas_call(
        functools.partial(choose_kernel, n, n_tp, steps),
        out_shape=[jax.ShapeDtypeStruct((n // n_tp, half, wide), jnp.bfloat16)] * 2,
        in_specs=[vmem] * 4,
        out_specs=[vmem, vmem],
        compiler_params=params,
        name="choose",
    )(*arrays)


def join_kernel(mine_ref, got_ref, out_ref):
    odd = lax.axis_index("tp") % 2
    count, half, _ = mine_ref.shape
    for low in range(2):
        first, second = (mine_ref, got_ref) if low == 0 else (got_ref, mine_ref)

        @pl.when(odd == low)
        def _():
            for i in range(count):
                out_ref[2 * i * half : (2 * i + 1) * half] = first[i]
                out_ref[(2 * i + 1) * half : (2 * i + 2) * half] = second[i]


def join(mine, got):
    count, half, wide = mine.shape
    return pl.pallas_call(
        join_kernel,
        out_shape=jax.ShapeDtypeStruct((2 * count * half, wide), jnp.bfloat16),
        in_specs=[vmem, vmem],
        out_specs=vmem,
        compiler_params=params,
        name="join",
    )(mine, got)


def after(array, token):
    return lax.optimization_barrier((array, token))[0]


def body(n, n_tp, queries, suffix_kv, cache_pool, hit_count, hit_slots, out_weight):
    tok = queries.shape[0]
    half = n // 2
    order = ring_order(n)
    right = [(order[i], order[(i + 1) % n]) for i in range(n)]
    left = [(b, a) for a, b in right]

    def send_both(pair, k, token):
        from_left, from_right = pair
        if token is not None:
            from_left = after(from_left, token)
            from_right = after(from_right, token)
        return lax.ppermute(from_left, "ctx", right), lax.ppermute(from_right, "ctx", left)

    def ring(own, visit, token):
        held = [send_both((a, a), k, None) for k, a in enumerate(own)]
        for step in range(1, half):
            token = visit(step - 1, arrived if step > 1 else None, token)
            arrived = held
            if step < half - 1:
                held = [send_both(arrived[k], k, token) for k in range(2)]
            else:
                held = (
                    lax.ppermute(after(arrived[0][0], token), "ctx", right),
                    lax.ppermute(after(arrived[1][1], token), "ctx", left),
                )
        token = visit(half - 1, arrived, token)
        return held, token

    def absorb(step, arrived, state):
        if step == 0:
            return flash(n, tok, queries, hit_count, ((0, 0), (1, 0)), own, (), False)
        turned, state = state[0], state[1:]
        for kind in range(2):
            pieces = ((kind, -step), (kind, step))
            state = flash(n, tok, turned, hit_count, pieces, arrived[kind], state, False)
        return [turned] + list(state)

    own = pick(hit_slots, cache_pool, suffix_kv)
    far, state = ring(own, absorb, None)
    attention = flash(
        n, tok, state[0], hit_count, ((0, half), (1, half)), far, tuple(state[1:]), True
    )

    swap = [(t, t ^ 1) for t in range(n_tp)]
    sums = []

    def reduce(arrays):
        keep, send = project(arrays, out_weight)
        sums.append((keep, lax.ppermute(send, "tp", swap)))
        return send

    def spread(step, arrived, token):
        if step == 0:
            return attention[0]
        (a_left, a_right), (b_left, b_right) = arrived
        arrays = (a_left, b_left, a_right, b_right)
        return reduce(tuple(attention) + arrays if step == 1 else arrays)

    def cross(stay, send):
        got = lax.ppermute(send, "tp", [(t, t ^ 2) for t in range(n_tp)])
        bit = 4
        while bit < n_tp:
            stay = added(stay, got).astype(jnp.bfloat16)
            got = lax.ppermute(stay, "tp", [(t, t ^ bit) for t in range(n_tp)])
            bit *= 2
        return stay, got

    far, _ = ring(attention, spread, None)
    steps = [0] + [s * d for d in range(1, half) for s in (-1, 1)] + [half]
    sums[0] = (after(sums[0][0], far), sums[0][1])
    stay, send, last_stay, last_send = sort(n, n_tp, steps[:-1], sums)
    stay, got = cross(stay, send)
    reduce(far)
    last_stay, last_send = place_last(n, n_tp, *sums[-1], last_stay, last_send)
    last_stay, last_got = cross(last_stay, last_send)
    mine, give = choose(n, n_tp, steps, (stay, got, last_stay, last_got))
    return join(mine, lax.ppermute(give, "tp", swap))


def solution(mesh):
    n, n_tp = mesh.shape["ctx"], mesh.shape["tp"]
    placed = (
        P("ctx", "tp"),
        P(None, "ctx", "tp"),
        P(None, "ctx", None, "tp"),
        P(),
        P("ctx", None),
        P("tp", "ctx"),
    )
    return jax.shard_map(
        functools.partial(body, n, n_tp),
        mesh=mesh,
        in_specs=placed,
        out_specs=P("tp", "ctx"),
        check_vma=False,
    )
```

time: 263 us -> 108 us (0.41)
  waiting for transfers between devices: 169 us -> 36.9 us
  matrix products: 39.8 us -> 0 us
  Pallas kernels: 0 us -> 34.4 us
  starting transfers between devices: 0.31 us -> 32.1 us
  other arithmetic: 19.6 us -> 0 us
  local copies, waits for them, and re-layouts: 20.4 us -> 3.6 us
  between operations: 13.2 us -> 0.23 us
    all_gather x3 -> x0, waiting for transfers between devices: 139 us -> none  [the longest x1 79 us: body(): gathered = lax.all_gather(attention, 'ctx', axis=0, tiled=True)]
    dot_general x7 -> x0, matrix products: 39.8 us -> none  [the longest x3 17.3 us: absorb(): jnp.einsum('qsgk,ksd->qsgd', rounded_weights, value_rows, preferred_eleme...]
    ppermute x0 -> x35, waiting for transfers between devices: none -> 36.9 us  [the longest x12 14.8 us: send_both(): lax.ppermute(from_right, 'ctx', left)]
    pallas_call x0 -> x17, Pallas kernels: none -> 34.4 us  [the longest x8 18.6 us: flash(): pl.pallas_call(functools.partial(flash_kernel, n, tok, pieces, not state,...]
    ppermute x0 -> x35, starting transfers between devices: none -> 32.1 us  [the longest x12 19.8 us: send_both(): lax.ppermute(from_right, 'ctx', left)]
    reduce_scatter x1 -> x0, waiting for transfers between devices: 29.8 us -> none  [body(): lax.psum_scatter(jnp.dot(gathered, out_weight, preferred_element_type=jnp...]
    reduce_sum x5 -> x0, other arithmetic: 14.9 us -> none  [the longest x3 14.7 us: absorb(): new_sum = running_sum * rescale + jnp.sum(weights, axis=-1)]
    slice x3 -> x0, local copies, waits for them, and re-layouts: 6.29 us -> none  [absorb(): value_rows = key_block[1].reshape(key_count, slots_dev, head_width)]
  transfers between devices with their start and end apart: 4 -> 35, of which waited for: 3 -> 15; matrix products, arithmetic and copies ran while one was open for 23% -> 0% of each run, Pallas kernels for 0% -> 26%
where the time goes in v1:
time: 108 us; the launch traced here: 107 us
  waiting for transfers between devices  36.9 us (34%)
  Pallas kernels  34.4 us (32%)
  starting transfers between devices  32.1 us (30%)
  local copies, waits for them, and re-layouts  3.6 us (3%)
    ppermute x12, starting transfers between devices, send_both(): lax.ppermute(from_right, 'ctx', left)  19.8 us
    pallas_call x8, Pallas kernels, flash(): pl.pallas_call(functools.partial(flash_kernel, n, tok, pieces, not state,...  18.6 us
    ppermute x12, waiting for transfers between devices, send_both(): lax.ppermute(from_right, 'ctx', left)  14.8 us
    pallas_call x4, Pallas kernels, project(): pl.pallas_call(functools.partial(project_kernel, count), out_shape=[jax.S...  11.2 us
    ppermute x12, waiting for transfers between devices, send_both(): lax.ppermute(from_left, 'ctx', right)  8.57 us
    ppermute x2, waiting for transfers between devices, cross(): got = lax.ppermute(send, 'tp', [(t, t ^ 2) for t in range(n_tp)])  7.62 us
    ppermute x12, starting transfers between devices, send_both(): lax.ppermute(from_left, 'ctx', right)  5.89 us
    unnamed x12, local copies, waits for them, and re-layouts  3.6 us
  transfers between devices with their start and end apart: 35, of which 15 were waited for; matrix products, arithmetic and copies ran while one was open for 0% of the time, Pallas kernels for 26%

profile of v1, /device:TPU:0, one launch (start us, length us, event | category | flops | bytes accessed | tf_op | source)
XLA Modules:
  0.0 107.2 jit_solution(7579837092121397508)
XLA Ops:
  0.0 2.8 %pick.1 = (bf16[2,256,256]{2,1,0:T(8,128)(2,1)}, bf16[2,256,256]{2,1,0:T(8,128)(2,1)}) custom-call(s32[1,3]{1,0:T(1,128)} %hit_slots.1, bf16[2,16,128,256]{3,2,1,0:T(8,128)(2,1)} %pool_ref.1, bf16[2,128,256]{2,1,0:T(8,128)(2,1)} %suffix_ref.1), custom_call_target="tpu_custom_call" | custom-call | tf_op jit(solution)/shard_map/pick/pallas_call | solution.py:63
  2.8 3.0 %collective-permute-start.3 = (bf16[2,256,256]{2,1,0:T(8,128)(2,1)}, bf16[2,256,256]{2,1,0:T(8,128)(2,1)S(1)}, u32[]{:S(2)}, u32[]{:S(2)}) collective-permute-start(bf16[2,256,256]{2,1,0:T(8,128)(2,1)} %get-tuple-element.69.refs_1_), channel_id=1, source_target_pairs={{8,0},{16,8},{24,16},{28,24},{20,28},{12,20},{4,12},{0,4},{9,1},{1... | collective-permute-start | bytes 786440 | tf_op jit(solution)/shard_map/ppermute | solution.py:394
  6.0 2.0 %collective-permute-start.2 = (bf16[2,256,256]{2,1,0:T(8,128)(2,1)}, bf16[2,256,256]{2,1,0:T(8,128)(2,1)S(1)}, u32[]{:S(2)}, u32[]{:S(2)}) collective-permute-start(bf16[2,256,256]{2,1,0:T(8,128)(2,1)} %get-tuple-element.69.refs_1_), channel_id=1, source_target_pairs={{0,8},{8,16},{16,24},{24,28},{28,20},{20,12},{12,4},{4,0},{1,9},{9... | collective-permute-start | bytes 786440 | tf_op jit(solution)/shard_map/ppermute | solution.py:394
  11.6 2.4 %flash.8 = (bf16[128,2048]{1,0:T(8,128)(2,1)S(1)}, f32[8,2048]{1,0:T(8,128)S(1)}, f32[8,2048]{1,0:T(8,128)S(1)}, f32[128,2048]{1,0:T(8,128)S(1)}) custom-call(s32[8]{0:T(128)S(1)} %copy-done.4, bf16[128,2048]{1,0:T(8,128)(2,1)S(1)} %copy-done.1, bf16[2,256,256]{2,1,0:T(8,128)(2,1)S(1)} %copy-done.2, bf16[2,256,256]{2,1,0:T(8,128)(2,1)S(1)} %copy-done.3), custom_call_target="tpu_custom_call" | custom-call | flops 1000 | bytes 1000 | tf_op jit(solution)/shard_map/flash/pallas_call | solution.py:196
  14.0 2.0 %collective-permute-start.7 = (bf16[2,256,256]{2,1,0:T(8,128)(2,1)S(1)}, bf16[2,256,256]{2,1,0:T(8,128)(2,1)S(1)}, u32[]{:S(2)}, u32[]{:S(2)}) collective-permute-start(bf16[2,256,256]{2,1,0:T(8,128)(2,1)S(1)} %collective-permute-done.3.refs_1_), channel_id=1, source_target_pairs={{8,0},{16,8},{24,16},{28,24},{20,28},{12,20},{4,12},{0,4},{9,1},{1... | collective-permute-start | bytes 786440 | tf_op jit(solution)/shard_map/ppermute | solution.py:394
  16.1 4.8 %collective-permute-done.2.refs_0_ = bf16[2,256,256]{2,1,0:T(8,128)(2,1)S(1)} collective-permute-done((bf16[2,256,256]{2,1,0:T(8,128)(2,1)}, bf16[2,256,256]{2,1,0:T(8,128)(2,1)S(1)}, u32[]{:S(2)}, u32[]{:S(2)}) %collective-permute-start.2) | collective-permute-done | bytes 262176 | tf_op jit(solution)/shard_map/ppermute | solution.py:394
  21.0 1.9 %collective-permute-start.8 = (bf16[2,256,256]{2,1,0:T(8,128)(2,1)S(1)}, bf16[2,256,256]{2,1,0:T(8,128)(2,1)S(1)}, u32[]{:S(2)}, u32[]{:S(2)}) collective-permute-start(bf16[2,256,256]{2,1,0:T(8,128)(2,1)S(1)} %collective-permute-done.4.refs_1_), channel_id=1, source_target_pairs={{8,0},{16,8},{24,16},{28,24},{20,28},{12,20},{4,12},{0,4},{9,1},{1... | collective-permute-start | bytes 786440 | tf_op jit(solution)/shard_map/ppermute | solution.py:394
  22.9 2.4 %flash.9 = (f32[8,2048]{1,0:T(8,128)S(1)}, f32[8,2048]{1,0:T(8,128)S(1)}, f32[128,2048]{1,0:T(8,128)S(1)}) custom-call(s32[8]{0:T(128)S(1)} %copy-done.4, bf16[128,2048]{1,0:T(8,128)(2,1)S(1)} %get-tuple-element.70.q_ref, bf16[2,256,256]{2,1,0:T(8,128)(2,1)S(1)} %collective-permute-done.refs_0_, ...), custom_call_target="tpu_custom_call", output_to_operand_aliasing={{0}: (4, {}), {1}: (5, {}), {2}: (6, {})} | custom-call | flops 1000 | bytes 1000 | tf_op jit(solution)/shard_map/flash/pallas_call | solution.py:196
  25.3 2.3 %flash.10 = (f32[8,2048]{1,0:T(8,128)S(1)}, f32[8,2048]{1,0:T(8,128)S(1)}, f32[128,2048]{1,0:T(8,128)S(1)}) custom-call(s32[8]{0:T(128)S(1)} %copy-done.4, bf16[128,2048]{1,0:T(8,128)(2,1)S(1)} %get-tuple-element.70.q_ref, bf16[2,256,256]{2,1,0:T(8,128)(2,1)S(1)} %collective-permute-done.2.refs_0_, ...), custom_call_target="tpu_custom_call", output_to_operand_aliasing={{0}: (4, {}), {1}: (5, {}), {2}: (6, {})} | custom-call | flops 1000 | bytes 1000 | tf_op jit(solution)/shard_map/flash/pallas_call | solution.py:196
  27.6 1.6 %collective-permute-start.10 = (bf16[2,256,256]{2,1,0:T(8,128)(2,1)S(1)}, bf16[2,256,256]{2,1,0:T(8,128)(2,1)S(1)}, u32[]{:S(2)}, u32[]{:S(2)}) collective-permute-start(bf16[2,256,256]{2,1,0:T(8,128)(2,1)S(1)} %collective-permute-done.7.refs_1_), channel_id=1, source_target_pairs={{8,0},{16,8},{24,16},{28,24},{20,28},{12,20},{4,12},{0,4},{9,1},{1... | collective-permute-start | bytes 786440 | tf_op jit(solution)/shard_map/ppermute | solution.py:394
  29.7 2.4 %collective-permute-done.6.refs_0_ = bf16[2,256,256]{2,1,0:T(8,128)(2,1)S(1)} collective-permute-done((bf16[2,256,256]{2,1,0:T(8,128)(2,1)S(1)}, bf16[2,256,256]{2,1,0:T(8,128)(2,1)S(1)}, u32[]{:S(2)}, u32[]{:S(2)}) %collective-permute-start.6) | collective-permute-done | bytes 262176 | tf_op jit(solution)/shard_map/ppermute | solution.py:394
  32.1 1.6 %collective-permute-start.13 = (bf16[2,256,256]{2,1,0:T(8,128)(2,1)S(1)}, bf16[2,256,256]{2,1,0:T(8,128)(2,1)S(1)}, u32[]{:S(2)}, u32[]{:S(2)}) collective-permute-start(bf16[2,256,256]{2,1,0:T(8,128)(2,1)S(1)} %collective-permute-done.8.refs_1_), channel_id=1, source_target_pairs={{8,0},{16,8},{24,16},{28,24},{20,28},{12,20},{4,12},{0,4},{9,1},{1... | collective-permute-start | bytes 786440 | tf_op jit(solution)/shard_map/ppermute | solution.py:394
  34.2 2.4 %flash.11 = (f32[8,2048]{1,0:T(8,128)S(1)}, f32[8,2048]{1,0:T(8,128)S(1)}, f32[128,2048]{1,0:T(8,128)S(1)}) custom-call(s32[8]{0:T(128)S(1)} %copy-done.5, bf16[128,2048]{1,0:T(8,128)(2,1)S(1)} %get-tuple-element.70.q_ref, bf16[2,256,256]{2,1,0:T(8,128)(2,1)S(1)} %collective-permute-done.1.refs_0_, ...), custom_call_target="tpu_custom_call", output_to_operand_aliasing={{0}: (4, {}), {1}: (5, {}), {2}: (6, {})} | custom-call | flops 1000 | bytes 1000 | tf_op jit(solution)/shard_map/flash/pallas_call | solution.py:196
  36.6 2.3 %flash.12 = (f32[8,2048]{1,0:T(8,128)S(1)}, f32[8,2048]{1,0:T(8,128)S(1)}, f32[128,2048]{1,0:T(8,128)S(1)}) custom-call(s32[8]{0:T(128)S(1)} %copy-done.5, bf16[128,2048]{1,0:T(8,128)(2,1)S(1)} %get-tuple-element.70.q_ref, bf16[2,256,256]{2,1,0:T(8,128)(2,1)S(1)} %collective-permute-done.6.refs_0_, ...), custom_call_target="tpu_custom_call", output_to_operand_aliasing={{0}: (4, {}), {1}: (5, {}), {2}: (6, {})} | custom-call | flops 1000 | bytes 1000 | tf_op jit(solution)/shard_map/flash/pallas_call | solution.py:196
  38.9 1.6 %collective-permute-start.11 = (bf16[2,256,256]{2,1,0:T(8,128)(2,1)S(1)}, bf16[2,256,256]{2,1,0:T(8,128)(2,1)S(1)}, u32[]{:S(2)}, u32[]{:S(2)}) collective-permute-start(bf16[2,256,256]{2,1,0:T(8,128)(2,1)S(1)} %collective-permute-done.10.refs_1_), channel_id=1, source_target_pairs={{8,0},{16,8},{24,16},{28,24},{20,28},{12,20},{4,12},{0,4},{9,1},{1... | collective-permute-start | bytes 786440 | tf_op jit(solution)/shard_map/ppermute | solution.py:406
  42.5 2.4 %flash.13 = (f32[8,2048]{1,0:T(8,128)S(1)}, f32[8,2048]{1,0:T(8,128)S(1)}, f32[128,2048]{1,0:T(8,128)S(1)}) custom-call(s32[8]{0:T(128)S(1)} %copy-done.5, bf16[128,2048]{1,0:T(8,128)(2,1)S(1)} %get-tuple-element.70.q_ref, bf16[2,256,256]{2,1,0:T(8,128)(2,1)S(1)} %collective-permute-done.5.refs_0_, ...), custom_call_target="tpu_custom_call", output_to_operand_aliasing={{0}: (4, {}), {1}: (5, {}), {2}: (6, {})} | custom-call | flops 1000 | bytes 1000 | tf_op jit(solution)/shard_map/flash/pallas_call | solution.py:196
  44.9 2.3 %flash.14 = (f32[8,2048]{1,0:T(8,128)S(1)}, f32[8,2048]{1,0:T(8,128)S(1)}, f32[128,2048]{1,0:T(8,128)S(1)}) custom-call(s32[8]{0:T(128)S(1)} %copy-done.5, bf16[128,2048]{1,0:T(8,128)(2,1)S(1)} %get-tuple-element.70.q_ref, bf16[2,256,256]{2,1,0:T(8,128)(2,1)S(1)} %collective-permute-done.12.refs_0_, ...), custom_call_target="tpu_custom_call", output_to_operand_aliasing={{0}: (4, {}), {1}: (5, {}), {2}: (6, {})} | custom-call | flops 1000 | bytes 1000 | tf_op jit(solution)/shard_map/flash/pallas_call | solution.py:196
  47.5 2.3 %flash.15 = (bf16[64,2048]{1,0:T(8,128)(2,1)S(1)}, bf16[64,2048]{1,0:T(8,128)(2,1)S(1)}) custom-call(s32[8]{0:T(128)S(1)} %copy-done.5, bf16[128,2048]{1,0:T(8,128)(2,1)S(1)} %get-tuple-element.70.q_ref, bf16[2,256,256]{2,1,0:T(8,128)(2,1)S(1)} %collective-permute-done.9.refs_0_, bf16[2,256,256]{2,1,0:T(8,128)(2,1)S(1)} %collective-permute-done.11.refs_1_, ...), custom_call_target="tpu_custom_call" | custom-call | flops 1000 | bytes 1000 | tf_op jit(solution)/shard_map/flash/pallas_call | solution.py:196
  49.8 1.6 %collective-permute-start.17 = (bf16[64,2048]{1,0:T(8,128)(2,1)S(1)}, bf16[64,2048]{1,0:T(8,128)(2,1)S(1)}, u32[]{:S(2)}, u32[]{:S(2)}) collective-permute-start(bf16[64,2048]{1,0:T(8,128)(2,1)S(1)} %get-tuple-element.103.refs_1_), channel_id=1, source_target_pairs={{8,0},{16,8},{24,16},{28,24},{20,28},{12,20},{4,12},{0,4},{9,1},{1... | collective-permute-start | bytes 786440 | tf_op jit(solution)/shard_map/ppermute | solution.py:394
  51.9 1.6 %collective-permute-start.16 = (bf16[64,2048]{1,0:T(8,128)(2,1)S(1)}, bf16[64,2048]{1,0:T(8,128)(2,1)S(1)}, u32[]{:S(2)}, u32[]{:S(2)}) collective-permute-start(bf16[64,2048]{1,0:T(8,128)(2,1)S(1)} %get-tuple-element.102.refs_0_), channel_id=1, source_target_pairs={{8,0},{16,8},{24,16},{28,24},{20,28},{12,20},{4,12},{0,4},{9,1},{1... | collective-permute-start | bytes 786440 | tf_op jit(solution)/shard_map/ppermute | solution.py:394
  53.9 5.2 %collective-permute-done.17.refs_5_ = bf16[64,2048]{1,0:T(8,128)(2,1)S(1)} collective-permute-done((bf16[64,2048]{1,0:T(8,128)(2,1)S(1)}, bf16[64,2048]{1,0:T(8,128)(2,1)S(1)}, u32[]{:S(2)}, u32[]{:S(2)}) %collective-permute-start.17) | collective-permute-done | bytes 262176 | tf_op jit(solution)/shard_map/ppermute | solution.py:394
  59.1 1.6 %collective-permute-start.22 = (bf16[64,2048]{1,0:T(8,128)(2,1)S(1)}, bf16[64,2048]{1,0:T(8,128)(2,1)S(1)}, u32[]{:S(2)}, u32[]{:S(2)}) collective-permute-start(bf16[64,2048]{1,0:T(8,128)(2,1)S(1)} %collective-permute-done.17.refs_5_), channel_id=1, source_target_pairs={{8,0},{16,8},{24,16},{28,24},{20,28},{12,20},{4,12},{0,4},{9,1},{1... | collective-permute-start | bytes 786440 | tf_op jit(solution)/shard_map/ppermute | solution.py:394
  61.1 3.6 %collective-permute-done.16.refs_4_ = bf16[64,2048]{1,0:T(8,128)(2,1)S(1)} collective-permute-done((bf16[64,2048]{1,0:T(8,128)(2,1)S(1)}, bf16[64,2048]{1,0:T(8,128)(2,1)S(1)}, u32[]{:S(2)}, u32[]{:S(2)}) %collective-permute-start.16) | collective-permute-done | bytes 262176 | tf_op jit(solution)/shard_map/ppermute | solution.py:394
  64.7 1.6 %collective-permute-start.21 = (bf16[64,2048]{1,0:T(8,128)(2,1)S(1)}, bf16[64,2048]{1,0:T(8,128)(2,1)S(1)}, u32[]{:S(2)}, u32[]{:S(2)}) collective-permute-start(bf16[64,2048]{1,0:T(8,128)(2,1)S(1)} %collective-permute-done.16.refs_4_), channel_id=1, source_target_pairs={{8,0},{16,8},{24,16},{28,24},{20,28},{12,20},{4,12},{0,4},{9,1},{1... | collective-permute-start | bytes 786440 | tf_op jit(solution)/shard_map/ppermute | solution.py:394
  66.7 3.9 %project.4 = (bf16[3,64,1024]{2,1,0:T(8,128)(2,1)S(1)}, bf16[3,64,1024]{2,1,0:T(8,128)(2,1)S(1)}) custom-call(bf16[64,2048]{1,0:T(8,128)(2,1)S(1)} %get-tuple-element.102.refs_0_, bf16[64,2048]{1,0:T(8,128)(2,1)S(1)} %get-tuple-element.103.refs_1_, bf16[64,2048]{1,0:T(8,128)(2,1)S(1)} %collective-permute-done.14.refs_2_, ...), custom_call_target="tpu_custom_call" | custom-call | flops 1000 | bytes 1000 | tf_op jit(solution)/shard_map/project/pallas_call | solution.py:238
  70.7 1.6 %collective-permute-start.24 = (bf16[64,2048]{1,0:T(8,128)(2,1)S(1)}, bf16[64,2048]{1,0:T(8,128)(2,1)S(1)}, u32[]{:S(2)}, u32[]{:S(2)}) collective-permute-start(bf16[64,2048]{1,0:T(8,128)(2,1)S(1)} %collective-permute-done.22.refs_3_), channel_id=1, source_target_pairs={{8,0},{16,8},{24,16},{28,24},{20,28},{12,20},{4,12},{0,4},{9,1},{1... | collective-permute-start | bytes 786440 | tf_op jit(solution)/shard_map/ppermute | solution.py:394
  72.8 3.2 %collective-permute-done.21.refs_2_ = bf16[64,2048]{1,0:T(8,128)(2,1)S(1)} collective-permute-done((bf16[64,2048]{1,0:T(8,128)(2,1)S(1)}, bf16[64,2048]{1,0:T(8,128)(2,1)S(1)}, u32[]{:S(2)}, u32[]{:S(2)}) %collective-permute-start.21) | collective-permute-done | bytes 262176 | tf_op jit(solution)/shard_map/ppermute | solution.py:394
  75.9 1.6 %collective-permute-start.27 = (bf16[64,2048]{1,0:T(8,128)(2,1)S(1)}, bf16[64,2048]{1,0:T(8,128)(2,1)S(1)}, u32[]{:S(2)}, u32[]{:S(2)}) collective-permute-start(bf16[64,2048]{1,0:T(8,128)(2,1)S(1)} %collective-permute-done.21.refs_2_), channel_id=1, source_target_pairs={{8,0},{16,8},{24,16},{28,24},{20,28},{12,20},{4,12},{0,4},{9,1},{1... | collective-permute-start | bytes 786440 | tf_op jit(solution)/shard_map/ppermute | solution.py:394
  78.0 2.8 %project.5 = (bf16[2,64,1024]{2,1,0:T(8,128)(2,1)S(1)}, bf16[2,64,1024]{2,1,0:T(8,128)(2,1)S(1)}) custom-call(bf16[64,2048]{1,0:T(8,128)(2,1)S(1)} %collective-permute-done.18.refs_0_, bf16[64,2048]{1,0:T(8,128)(2,1)S(1)} %collective-permute-done.20.refs_1_, bf16[64,2048]{1,0:T(8,128)(2,1)S(1)} %collective-permute-done.21.refs_2_, ...), custom_call_target="tpu_custom_call" | custom-call | flops 1000 | bytes 1000 | tf_op jit(solution)/shard_map/project/pallas_call | solution.py:238
  85.4 2.8 %project.6 = (bf16[2,64,1024]{2,1,0:T(8,128)(2,1)S(1)}, bf16[2,64,1024]{2,1,0:T(8,128)(2,1)S(1)}) custom-call(bf16[64,2048]{1,0:T(8,128)(2,1)S(1)} %collective-permute-done.19.refs_0_, bf16[64,2048]{1,0:T(8,128)(2,1)S(1)} %collective-permute-done.26.refs_1_, bf16[64,2048]{1,0:T(8,128)(2,1)S(1)} %collective-permute-done.27.refs_2_, ...), custom_call_target="tpu_custom_call" | custom-call | flops 1000 | bytes 1000 | tf_op jit(solution)/shard_map/project/pallas_call | solution.py:238
  93.1 1.7 %project.7 = (bf16[1,64,1024]{2,1,0:T(8,128)(2,1)S(1)}, bf16[1,64,1024]{2,1,0:T(8,128)(2,1)S(1)}) custom-call(bf16[64,2048]{1,0:T(8,128)(2,1)S(1)} %collective-permute-done.23.refs_0_, bf16[64,2048]{1,0:T(8,128)(2,1)S(1)} %collective-permute-done.25.refs_1_, bf16[2048,1024]{1,0:T(8,128)(2,1)S(1)} %copy-done), custom_call_target="tpu_custom_call" | custom-call | flops 1000 | bytes 1000 | tf_op jit(solution)/shard_map/project/pallas_call | solution.py:238
  96.8 7.6 %collective-permute-done.33.refs_3_ = bf16[1,64,1024]{2,1,0:T(8,128)(2,1)S(1)} collective-permute-done((bf16[1,64,1024]{2,1,0:T(8,128)(2,1)S(1)}, bf16[1,64,1024]{2,1,0:T(8,128)(2,1)S(1)}, u32[]{:S(2)}, u32[]{:S(2)}) %collective-permute-start.33) | collective-permute-done | bytes 131104 | tf_op jit(solution)/shard_map/ppermute | solution.py:442
  (67 shorter events, 24.3 us)
Async XLA Ops:
  2.8 11.2 %collective-permute-start.3 = (bf16[2,256,256]{2,1,0:T(8,128)(2,1)}, bf16[2,256,256]{2,1,0:T(8,128)(2,1)S(1)}, u32[]{:S(2)}, u32[]{:S(2)}) collective-permute-start(bf16[2,256,256]{2,1,0:T(8,128)(2,1)} %get-tuple-element.69.refs_1_), channel_id=1, source_target_pairs={{8,0},{16,8},{24,16},{28,24},{20,28},{12,20},{4,12},{0,4},{9,1},{1... | collective-permute-start | bytes 786440 | tf_op jit(solution)/shard_map/ppermute | solution.py:394
  5.8 10.1 %collective-permute-start = (bf16[2,256,256]{2,1,0:T(8,128)(2,1)}, bf16[2,256,256]{2,1,0:T(8,128)(2,1)S(1)}, u32[]{:S(2)}, u32[]{:S(2)}) collective-permute-start(bf16[2,256,256]{2,1,0:T(8,128)(2,1)} %get-tuple-element.68.refs_0_), channel_id=1, source_target_pairs={{0,8},{8,16},{16,24},{24,28},{28,20},{20,12},{12,4},{4,0},{1,9},{9... | collective-permute-start | bytes 786440 | tf_op jit(solution)/shard_map/ppermute | solution.py:394
  6.0 14.9 %collective-permute-start.2 = (bf16[2,256,256]{2,1,0:T(8,128)(2,1)}, bf16[2,256,256]{2,1,0:T(8,128)(2,1)S(1)}, u32[]{:S(2)}, u32[]{:S(2)}) collective-permute-start(bf16[2,256,256]{2,1,0:T(8,128)(2,1)} %get-tuple-element.69.refs_1_), channel_id=1, source_target_pairs={{0,8},{8,16},{16,24},{24,28},{28,20},{20,12},{12,4},{4,0},{1,9},{9... | collective-permute-start | bytes 786440 | tf_op jit(solution)/shard_map/ppermute | solution.py:394
  7.9 13.0 %collective-permute-start.4 = (bf16[2,256,256]{2,1,0:T(8,128)(2,1)}, bf16[2,256,256]{2,1,0:T(8,128)(2,1)S(1)}, u32[]{:S(2)}, u32[]{:S(2)}) collective-permute-start(bf16[2,256,256]{2,1,0:T(8,128)(2,1)} %get-tuple-element.68.refs_0_), channel_id=1, source_target_pairs={{8,0},{16,8},{24,16},{28,24},{20,28},{12,20},{4,12},{0,4},{9,1},{1... | collective-permute-start | bytes 786440 | tf_op jit(solution)/shard_map/ppermute | solution.py:394
  14.0 13.6 %collective-permute-start.7 = (bf16[2,256,256]{2,1,0:T(8,128)(2,1)S(1)}, bf16[2,256,256]{2,1,0:T(8,128)(2,1)S(1)}, u32[]{:S(2)}, u32[]{:S(2)}) collective-permute-start(bf16[2,256,256]{2,1,0:T(8,128)(2,1)S(1)} %collective-permute-done.3.refs_1_), channel_id=1, source_target_pairs={{8,0},{16,8},{24,16},{28,24},{20,28},{12,20},{4,12},{0,4},{9,1},{1... | collective-permute-start | bytes 786440 | tf_op jit(solution)/shard_map/ppermute | solution.py:394
  16.0 13.3 %collective-permute-start.1 = (bf16[2,256,256]{2,1,0:T(8,128)(2,1)S(1)}, bf16[2,256,256]{2,1,0:T(8,128)(2,1)S(1)}, u32[]{:S(2)}, u32[]{:S(2)}) collective-permute-start(bf16[2,256,256]{2,1,0:T(8,128)(2,1)S(1)} %collective-permute-done.refs_0_), channel_id=1, source_target_pairs={{0,8},{8,16},{16,24},{24,28},{28,20},{20,12},{12,4},{4,0},{1,9},{9... | collective-permute-start | bytes 786440 | tf_op jit(solution)/shard_map/ppermute | solution.py:394
  20.9 11.2 %collective-permute-start.6 = (bf16[2,256,256]{2,1,0:T(8,128)(2,1)S(1)}, bf16[2,256,256]{2,1,0:T(8,128)(2,1)S(1)}, u32[]{:S(2)}, u32[]{:S(2)}) collective-permute-start(bf16[2,256,256]{2,1,0:T(8,128)(2,1)S(1)} %collective-permute-done.2.refs_0_), channel_id=1, source_target_pairs={{0,8},{8,16},{16,24},{24,28},{28,20},{20,12},{12,4},{4,0},{1,9},{9... | collective-permute-start | bytes 786440 | tf_op jit(solution)/shard_map/ppermute | solution.py:394
  21.0 11.2 %collective-permute-start.8 = (bf16[2,256,256]{2,1,0:T(8,128)(2,1)S(1)}, bf16[2,256,256]{2,1,0:T(8,128)(2,1)S(1)}, u32[]{:S(2)}, u32[]{:S(2)}) collective-permute-start(bf16[2,256,256]{2,1,0:T(8,128)(2,1)S(1)} %collective-permute-done.4.refs_1_), channel_id=1, source_target_pairs={{8,0},{16,8},{24,16},{28,24},{20,28},{12,20},{4,12},{0,4},{9,1},{1... | collective-permute-start | bytes 786440 | tf_op jit(solution)/shard_map/ppermute | solution.py:394
  27.6 11.2 %collective-permute-start.10 = (bf16[2,256,256]{2,1,0:T(8,128)(2,1)S(1)}, bf16[2,256,256]{2,1,0:T(8,128)(2,1)S(1)}, u32[]{:S(2)}, u32[]{:S(2)}) collective-permute-start(bf16[2,256,256]{2,1,0:T(8,128)(2,1)S(1)} %collective-permute-done.7.refs_1_), channel_id=1, source_target_pairs={{8,0},{16,8},{24,16},{28,24},{20,28},{12,20},{4,12},{0,4},{9,1},{1... | collective-permute-start | bytes 786440 | tf_op jit(solution)/shard_map/ppermute | solution.py:394
  29.2 9.6 %collective-permute-start.5 = (bf16[2,256,256]{2,1,0:T(8,128)(2,1)S(1)}, bf16[2,256,256]{2,1,0:T(8,128)(2,1)S(1)}, u32[]{:S(2)}, u32[]{:S(2)}) collective-permute-start(bf16[2,256,256]{2,1,0:T(8,128)(2,1)S(1)} %collective-permute-done.1.refs_0_), channel_id=1, source_target_pairs={{0,8},{8,16},{16,24},{24,28},{28,20},{20,12},{12,4},{4,0},{1,9},{9... | collective-permute-start | bytes 786440 | tf_op jit(solution)/shard_map/ppermute | solution.py:394
  32.1 10.4 %collective-permute-start.13 = (bf16[2,256,256]{2,1,0:T(8,128)(2,1)S(1)}, bf16[2,256,256]{2,1,0:T(8,128)(2,1)S(1)}, u32[]{:S(2)}, u32[]{:S(2)}) collective-permute-start(bf16[2,256,256]{2,1,0:T(8,128)(2,1)S(1)} %collective-permute-done.8.refs_1_), channel_id=1, source_target_pairs={{8,0},{16,8},{24,16},{28,24},{20,28},{12,20},{4,12},{0,4},{9,1},{1... | collective-permute-start | bytes 786440 | tf_op jit(solution)/shard_map/ppermute | solution.py:394
  33.7 11.2 %collective-permute-start.12 = (bf16[2,256,256]{2,1,0:T(8,128)(2,1)S(1)}, bf16[2,256,256]{2,1,0:T(8,128)(2,1)S(1)}, u32[]{:S(2)}, u32[]{:S(2)}) collective-permute-start(bf16[2,256,256]{2,1,0:T(8,128)(2,1)S(1)} %collective-permute-done.6.refs_0_), channel_id=1, source_target_pairs={{0,8},{8,16},{16,24},{24,28},{28,20},{20,12},{12,4},{4,0},{1,9},{9... | collective-permute-start | bytes 786440 | tf_op jit(solution)/shard_map/ppermute | solution.py:394
  38.9 8.3 %collective-permute-start.11 = (bf16[2,256,256]{2,1,0:T(8,128)(2,1)S(1)}, bf16[2,256,256]{2,1,0:T(8,128)(2,1)S(1)}, u32[]{:S(2)}, u32[]{:S(2)}) collective-permute-start(bf16[2,256,256]{2,1,0:T(8,128)(2,1)S(1)} %collective-permute-done.10.refs_1_), channel_id=1, source_target_pairs={{8,0},{16,8},{24,16},{28,24},{20,28},{12,20},{4,12},{0,4},{9,1},{1... | collective-permute-start | bytes 786440 | tf_op jit(solution)/shard_map/ppermute | solution.py:406
  40.5 7.0 %collective-permute-start.9 = (bf16[2,256,256]{2,1,0:T(8,128)(2,1)S(1)}, bf16[2,256,256]{2,1,0:T(8,128)(2,1)S(1)}, u32[]{:S(2)}, u32[]{:S(2)}) collective-permute-start(bf16[2,256,256]{2,1,0:T(8,128)(2,1)S(1)} %collective-permute-done.5.refs_0_), channel_id=1, source_target_pairs={{0,8},{8,16},{16,24},{24,28},{28,20},{20,12},{12,4},{4,0},{1,9},{9... | collective-permute-start | bytes 786440 | tf_op jit(solution)/shard_map/ppermute | solution.py:405
  49.8 9.3 %collective-permute-start.17 = (bf16[64,2048]{1,0:T(8,128)(2,1)S(1)}, bf16[64,2048]{1,0:T(8,128)(2,1)S(1)}, u32[]{:S(2)}, u32[]{:S(2)}) collective-permute-start(bf16[64,2048]{1,0:T(8,128)(2,1)S(1)} %get-tuple-element.103.refs_1_), channel_id=1, source_target_pairs={{8,0},{16,8},{24,16},{28,24},{20,28},{12,20},{4,12},{0,4},{9,1},{1... | collective-permute-start | bytes 786440 | tf_op jit(solution)/shard_map/ppermute | solution.py:394
  51.4 9.2 %collective-permute-start.14 = (bf16[64,2048]{1,0:T(8,128)(2,1)S(1)}, bf16[64,2048]{1,0:T(8,128)(2,1)S(1)}, u32[]{:S(2)}, u32[]{:S(2)}) collective-permute-start(bf16[64,2048]{1,0:T(8,128)(2,1)S(1)} %get-tuple-element.102.refs_0_), channel_id=1, source_target_pairs={{0,8},{8,16},{16,24},{24,28},{28,20},{20,12},{12,4},{4,0},{1,9},{9... | collective-permute-start | bytes 786440 | tf_op jit(solution)/shard_map/ppermute | solution.py:394
  51.9 12.8 %collective-permute-start.16 = (bf16[64,2048]{1,0:T(8,128)(2,1)S(1)}, bf16[64,2048]{1,0:T(8,128)(2,1)S(1)}, u32[]{:S(2)}, u32[]{:S(2)}) collective-permute-start(bf16[64,2048]{1,0:T(8,128)(2,1)S(1)} %get-tuple-element.102.refs_0_), channel_id=1, source_target_pairs={{8,0},{16,8},{24,16},{28,24},{20,28},{12,20},{4,12},{0,4},{9,1},{1... | collective-permute-start | bytes 786440 | tf_op jit(solution)/shard_map/ppermute | solution.py:394
  53.4 12.8 %collective-permute-start.15 = (bf16[64,2048]{1,0:T(8,128)(2,1)S(1)}, bf16[64,2048]{1,0:T(8,128)(2,1)S(1)}, u32[]{:S(2)}, u32[]{:S(2)}) collective-permute-start(bf16[64,2048]{1,0:T(8,128)(2,1)S(1)} %get-tuple-element.103.refs_1_), channel_id=1, source_target_pairs={{0,8},{8,16},{16,24},{24,28},{28,20},{20,12},{12,4},{4,0},{1,9},{9... | collective-permute-start | bytes 786440 | tf_op jit(solution)/shard_map/ppermute | solution.py:394
  59.1 11.6 %collective-permute-start.22 = (bf16[64,2048]{1,0:T(8,128)(2,1)S(1)}, bf16[64,2048]{1,0:T(8,128)(2,1)S(1)}, u32[]{:S(2)}, u32[]{:S(2)}) collective-permute-start(bf16[64,2048]{1,0:T(8,128)(2,1)S(1)} %collective-permute-done.17.refs_5_), channel_id=1, source_target_pairs={{8,0},{16,8},{24,16},{28,24},{20,28},{12,20},{4,12},{0,4},{9,1},{1... | collective-permute-start | bytes 786440 | tf_op jit(solution)/shard_map/ppermute | solution.py:394
  60.7 11.6 %collective-permute-start.18 = (bf16[64,2048]{1,0:T(8,128)(2,1)S(1)}, bf16[64,2048]{1,0:T(8,128)(2,1)S(1)}, u32[]{:S(2)}, u32[]{:S(2)}) collective-permute-start(bf16[64,2048]{1,0:T(8,128)(2,1)S(1)} %collective-permute-done.14.refs_2_), channel_id=1, source_target_pairs={{0,8},{8,16},{16,24},{24,28},{28,20},{20,12},{12,4},{4,0},{1,9},{9... | collective-permute-start | bytes 786440 | tf_op jit(solution)/shard_map/ppermute | solution.py:394
  64.7 11.2 %collective-permute-start.21 = (bf16[64,2048]{1,0:T(8,128)(2,1)S(1)}, bf16[64,2048]{1,0:T(8,128)(2,1)S(1)}, u32[]{:S(2)}, u32[]{:S(2)}) collective-permute-start(bf16[64,2048]{1,0:T(8,128)(2,1)S(1)} %collective-permute-done.16.refs_4_), channel_id=1, source_target_pairs={{8,0},{16,8},{24,16},{28,24},{20,28},{12,20},{4,12},{0,4},{9,1},{1... | collective-permute-start | bytes 786440 | tf_op jit(solution)/shard_map/ppermute | solution.py:394
  66.3 11.2 %collective-permute-start.20 = (bf16[64,2048]{1,0:T(8,128)(2,1)S(1)}, bf16[64,2048]{1,0:T(8,128)(2,1)S(1)}, u32[]{:S(2)}, u32[]{:S(2)}) collective-permute-start(bf16[64,2048]{1,0:T(8,128)(2,1)S(1)} %collective-permute-done.15.refs_3_), channel_id=1, source_target_pairs={{0,8},{8,16},{16,24},{24,28},{28,20},{20,12},{12,4},{4,0},{1,9},{9... | collective-permute-start | bytes 786440 | tf_op jit(solution)/shard_map/ppermute | solution.py:394
  70.7 10.6 %collective-permute-start.24 = (bf16[64,2048]{1,0:T(8,128)(2,1)S(1)}, bf16[64,2048]{1,0:T(8,128)(2,1)S(1)}, u32[]{:S(2)}, u32[]{:S(2)}) collective-permute-start(bf16[64,2048]{1,0:T(8,128)(2,1)S(1)} %collective-permute-done.22.refs_3_), channel_id=1, source_target_pairs={{8,0},{16,8},{24,16},{28,24},{20,28},{12,20},{4,12},{0,4},{9,1},{1... | collective-permute-start | bytes 786440 | tf_op jit(solution)/shard_map/ppermute | solution.py:394
  72.3 10.5 %collective-permute-start.19 = (bf16[64,2048]{1,0:T(8,128)(2,1)S(1)}, bf16[64,2048]{1,0:T(8,128)(2,1)S(1)}, u32[]{:S(2)}, u32[]{:S(2)}) collective-permute-start(bf16[64,2048]{1,0:T(8,128)(2,1)S(1)} %collective-permute-done.18.refs_0_), channel_id=1, source_target_pairs={{0,8},{8,16},{16,24},{24,28},{28,20},{20,12},{12,4},{4,0},{1,9},{9... | collective-permute-start | bytes 786440 | tf_op jit(solution)/shard_map/ppermute | solution.py:394
  75.9 8.1 %collective-permute-start.27 = (bf16[64,2048]{1,0:T(8,128)(2,1)S(1)}, bf16[64,2048]{1,0:T(8,128)(2,1)S(1)}, u32[]{:S(2)}, u32[]{:S(2)}) collective-permute-start(bf16[64,2048]{1,0:T(8,128)(2,1)S(1)} %collective-permute-done.21.refs_2_), channel_id=1, source_target_pairs={{8,0},{16,8},{24,16},{28,24},{20,28},{12,20},{4,12},{0,4},{9,1},{1... | collective-permute-start | bytes 786440 | tf_op jit(solution)/shard_map/ppermute | solution.py:394
  77.5 7.9 %collective-permute-start.26 = (bf16[64,2048]{1,0:T(8,128)(2,1)S(1)}, bf16[64,2048]{1,0:T(8,128)(2,1)S(1)}, u32[]{:S(2)}, u32[]{:S(2)}) collective-permute-start(bf16[64,2048]{1,0:T(8,128)(2,1)S(1)} %collective-permute-done.20.refs_1_), channel_id=1, source_target_pairs={{0,8},{8,16},{16,24},{24,28},{28,20},{20,12},{12,4},{4,0},{1,9},{9... | collective-permute-start | bytes 786440 | tf_op jit(solution)/shard_map/ppermute | solution.py:394
  78.0 13.0 %collective-permute-start.28 = (bf16[3,64,1024]{2,1,0:T(8,128)(2,1)S(1)}, bf16[3,64,1024]{2,1,0:T(8,128)(2,1)S(1)}, u32[]{:S(2)}, u32[]{:S(2)}) collective-permute-start(bf16[3,64,1024]{2,1,0:T(8,128)(2,1)S(1)} %get-tuple-element.106), channel_id=1, source_target_pairs={{0,1},{1,0},{2,3},{3,2},{4,5},{5,4},{6,7},{7,6},{8,9},{9,8},{10,11... | collective-permute-start | bytes 1179656 | tf_op jit(solution)/shard_map/ppermute | solution.py:431
  81.2 8.4 %collective-permute-start.25 = (bf16[64,2048]{1,0:T(8,128)(2,1)S(1)}, bf16[64,2048]{1,0:T(8,128)(2,1)S(1)}, u32[]{:S(2)}, u32[]{:S(2)}) collective-permute-start(bf16[64,2048]{1,0:T(8,128)(2,1)S(1)} %collective-permute-done.24.refs_3_), channel_id=1, source_target_pairs={{8,0},{16,8},{24,16},{28,24},{20,28},{12,20},{4,12},{0,4},{9,1},{1... | collective-permute-start | bytes 786440 | tf_op jit(solution)/shard_map/ppermute | solution.py:406
  82.8 8.1 %collective-permute-start.23 = (bf16[64,2048]{1,0:T(8,128)(2,1)S(1)}, bf16[64,2048]{1,0:T(8,128)(2,1)S(1)}, u32[]{:S(2)}, u32[]{:S(2)}) collective-permute-start(bf16[64,2048]{1,0:T(8,128)(2,1)S(1)} %collective-permute-done.19.refs_0_), channel_id=1, source_target_pairs={{0,8},{8,16},{16,24},{24,28},{28,20},{20,12},{12,4},{4,0},{1,9},{9... | collective-permute-start | bytes 786440 | tf_op jit(solution)/shard_map/ppermute | solution.py:405
  84.1 6.9 %collective-permute-start.29 = (bf16[2,64,1024]{2,1,0:T(8,128)(2,1)S(1)}, bf16[2,64,1024]{2,1,0:T(8,128)(2,1)S(1)}, u32[]{:S(2)}, u32[]{:S(2)}) collective-permute-start(bf16[2,64,1024]{2,1,0:T(8,128)(2,1)S(1)} %get-tuple-element.111), channel_id=1, source_target_pairs={{0,1},{1,0},{2,3},{3,2},{4,5},{5,4},{6,7},{7,6},{8,9},{9,8},{10,11... | collective-permute-start | bytes 786440 | tf_op jit(solution)/shard_map/ppermute | solution.py:431
  91.5 13.0 %collective-permute-start.31 = (bf16[3,64,1024]{2,1,0:T(8,128)(2,1)S(1)}, bf16[3,64,1024]{2,1,0:T(8,128)(2,1)S(1)}, u32[]{:S(2)}, u32[]{:S(2)}) collective-permute-start(bf16[3,64,1024]{2,1,0:T(8,128)(2,1)S(1)} %get-tuple-element.122), channel_id=1, source_target_pairs={{0,2},{1,3},{2,0},{3,1},{4,6},{5,7},{6,4},{7,5},{8,10},{9,11},{10,... | collective-permute-start | bytes 1179656 | tf_op jit(solution)/shard_map/ppermute | solution.py:442
  96.2 8.2 %collective-permute-start.33 = (bf16[1,64,1024]{2,1,0:T(8,128)(2,1)S(1)}, bf16[1,64,1024]{2,1,0:T(8,128)(2,1)S(1)}, u32[]{:S(2)}, u32[]{:S(2)}) collective-permute-start(bf16[1,64,1024]{2,1,0:T(8,128)(2,1)S(1)} %get-tuple-element.128), channel_id=1, source_target_pairs={{0,2},{1,3},{2,0},{3,1},{4,6},{5,7},{6,4},{7,5},{8,10},{9,11},{10,... | collective-permute-start | bytes 393224 | tf_op jit(solution)/shard_map/ppermute | solution.py:442
  (9 other events, 73.8 us)

commit v2 on v1

--- a/solution.py
+++ b/solution.py
@@ -459,6 +459,466 @@
     return join(mine, lax.ppermute(give, "tp", swap))
 
 
+def pair_pick_kernel(blk, hit_slots, pool_ref, suffix_ref, mine_ref, other_ref, held, slots_ref, slots_sem, sems):
+    fetch = pltpu.make_async_copy(hit_slots, slots_ref, slots_sem)
+    fetch.start()
+    fetch.wait()
+    copies = []
+    for kv in range(2):
+        for place in range(HCAP + 1):
+            if place == 0:
+                src = suffix_ref.at[kv]
+            else:
+                src = pool_ref.at[kv, slots_ref[0, place - 1]]
+            copies.append(pltpu.make_async_copy(src, held.at[kv, place], sems.at[kv, place]))
+    for copy in copies:
+        copy.start()
+    for copy in copies:
+        copy.wait()
+    parity = lax.axis_index("ctx") % 2
+    for place in range(HCAP + 1):
+        at = slice(place * blk, (place + 1) * blk)
+        keys = [held[0, place, :, s * HD : (s + 1) * HD] for s in range(2)]
+        values = [held[1, place, :, s * HD : (s + 1) * HD].T for s in range(2)]
+        mine_ref[0, at, :] = jnp.where(parity == 0, keys[0], keys[1])
+        mine_ref[1, at, :] = jnp.where(parity == 0, values[0], values[1])
+        other_ref[0, at, :] = jnp.where(parity == 0, keys[1], keys[0])
+        other_ref[1, at, :] = jnp.where(parity == 0, values[1], values[0])
+
+
+def pair_pick(hit_slots, cache_pool, suffix_kv):
+    blk, wide = cache_pool.shape[2:]
+    return pl.pallas_call(
+        functools.partial(pair_pick_kernel, blk),
+        out_shape=[jax.ShapeDtypeStruct((2, (HCAP + 1) * blk, HD), jnp.bfloat16)] * 2,
+        in_specs=[hbm, hbm, hbm],
+        out_specs=[vmem, vmem],
+        scratch_shapes=[
+            pltpu.VMEM((2, HCAP + 1, blk, wide), jnp.bfloat16),
+            pltpu.SMEM(hit_slots.shape, jnp.int32),
+            pltpu.SemaphoreType.DMA,
+            pltpu.SemaphoreType.DMA((2, HCAP + 1)),
+        ],
+        compiler_params=pltpu.CompilerParams(vmem_limit_bytes=60 * 1024 * 1024),
+        name="pick",
+    )(hit_slots, cache_pool, suffix_kv)
+
+
+def attend(blocks, score, biases, values, old, store):
+    def weigh(j, scores):
+        tops = [fold(jnp.maximum, part) + bias for part, bias in zip(scores, biases)]
+        top = jnp.max(functools.reduce(jnp.maximum, tops), axis=0, keepdims=True)
+        total = fade = mixed = None
+        if old is not None:
+            old_top, old_total, old_mixed = old(j)
+            top = jnp.maximum(old_top, top)
+            fade = jnp.exp((old_top - top) * score_scale)
+            total, mixed = old_total * fade, old_mixed
+        else:
+            top = jnp.broadcast_to(top, (8, top.shape[1]))
+        offset = top[:1] * score_scale
+        probs = []
+        for part, bias in zip(scores, biases):
+            weights = jnp.exp(part * score_scale - (offset - bias))
+            add = fold(jnp.add, weights)
+            total = add if total is None else total + add
+            probs.append(weights.astype(jnp.bfloat16))
+        return jnp.concatenate(probs, axis=0), top, total, fade, mixed
+
+    def mix(j, probs, top, total, fade, mixed):
+        add = jnp.dot(values, probs, preferred_element_type=jnp.float32)
+        store(j, top, total, add if mixed is None else mixed * fade[:1] + add)
+
+    ahead = min(2, blocks)
+    scores = [score(j) for j in range(ahead)]
+    for j in range(blocks):
+        weighed = weigh(j, scores[j])
+        scores[j] = None
+        if j + ahead < blocks:
+            scores.append(score(j + ahead))
+        mix(j, *weighed)
+
+
+def squares(values, blk):
+    return jnp.concatenate(
+        [values[r : r + blk] for r in range(0, values.shape[0], blk)], axis=1
+    )
+
+
+def hit_biases(hits, suffix_seen):
+    seen = [suffix_seen, None] + [hits > h for h in range(1, HCAP)]
+    return [0.0 if s is None else jnp.where(s, 0.0, neg_fill) for s in seen]
+
+
+def causal(parts, owner, tok):
+    key = lax.broadcasted_iota(jnp.int32, parts[0].shape, 0) + owner % 2 * tok
+    token = lax.broadcasted_iota(jnp.int32, parts[0].shape, 1)
+    return [jnp.where(key <= token, parts[0], neg_fill)] + parts[1:]
+
+
+def pair_first_kernel(tok, hit_ref, q_ref, q_got_ref, mine_ref, turned_ref, *state):
+    me = lax.axis_index("ctx")
+    parity = me % 2
+    heads = q_got_ref.shape[1] // HD
+    rows = 2 * tok
+    blk = tok
+    biases = hit_biases(hit_ref[me], None)
+    values = squares(mine_ref[1], blk)
+
+    def score(j):
+        own = q_ref[:, pl.ds(pl.multiple_of((parity * heads + j) * HD, HD), HD)].T
+        got = q_got_ref[:, j * HD : (j + 1) * HD].T
+        low = jnp.where(parity == 0, own, got)
+        high = jnp.where(parity == 0, got, own)
+        turned = jnp.concatenate([low, high], axis=1)
+        turned_ref[:, j * rows : (j + 1) * rows] = turned
+        raw = jnp.dot(mine_ref[0], turned, preferred_element_type=jnp.float32)
+        return causal([raw[r : r + blk] for r in range(0, raw.shape[0], blk)], me, tok)
+
+    def store(j, *new):
+        for ref, array in zip(state, new):
+            ref[:, j * rows : (j + 1) * rows] = array
+
+    attend(heads, score, biases, values, None, store)
+
+
+def pair_step_kernel(n, tok, step, part, last, hit_ref, turned_ref, left_ref, right_ref, *refs):
+    old_refs, out_refs = refs[:3], refs[3:]
+    me = lax.axis_index("ctx")
+    level, levels = me // 2, n // 2
+    home = lax.bitwise_xor(me, part)
+    rows = 2 * tok
+    blk = tok
+    heads = turned_ref.shape[1] // rows
+    reach = jnp.where(me % 2 == 0, step, -step)
+    from_left = (level - reach >= 0) & (level - reach < levels)
+    from_right = (level + reach >= 0) & (level + reach < levels)
+
+    def at(j):
+        return slice(j * rows, (j + 1) * rows)
+
+    def old(j):
+        return tuple(ref[:, at(j)] for ref in old_refs)
+
+    def store(j, top, total, mixed):
+        if last:
+            result = mixed * (1.0 / jnp.sum(total, axis=0, keepdims=True))
+            for k, out in enumerate(out_refs):
+                square = result[:, k * tok : (k + 1) * tok]
+                out[:, j * HD : (j + 1) * HD] = square.T.astype(jnp.bfloat16)
+        else:
+            for ref, array in zip(out_refs, (top, total, mixed)):
+                ref[:, at(j)] = array
+
+    def run(keys, values, biases):
+        def score(j):
+            scores = []
+            for block in keys:
+                raw = jnp.dot(block, turned_ref[:, at(j)], preferred_element_type=jnp.float32)
+                scores += [raw[r : r + blk] for r in range(0, raw.shape[0], blk)]
+            return causal(scores, home, tok) if step == 0 else scores
+
+        attend(heads, score, biases, values, old, store)
+
+    if step == 0:
+        run([left_ref[0]], squares(left_ref[1], blk), hit_biases(hit_ref[home], None))
+        return
+
+    @pl.when(from_left != from_right)
+    def _():
+        keys = jnp.where(from_left, left_ref[0], right_ref[0])
+        values = jnp.where(from_left, left_ref[1], right_ref[1])
+        owner = home - 2 * jnp.where(from_left, reach, -reach)
+        run([keys], squares(values, blk), hit_biases(hit_ref[owner], owner < home))
+
+    if 2 * step < levels:
+
+        @pl.when(from_left & from_right)
+        def _():
+            values = [squares(ref[1], blk) for ref in (left_ref, right_ref)]
+            biases = hit_biases(hit_ref[home - 2 * reach], reach > 0)
+            biases += hit_biases(hit_ref[home + 2 * reach], reach < 0)
+            run([left_ref[0], right_ref[0]], jnp.concatenate(values, axis=1), biases)
+
+    if 2 * step > levels:
+
+        @pl.when(jnp.logical_not(from_left | from_right))
+        def _():
+            for j in range(heads):
+                store(j, *old(j))
+
+
+def pair_flash(kernel, tok, rows, operands, states, last):
+    small = jax.ShapeDtypeStruct((8, rows), jnp.float32)
+    shapes = [small, small, jax.ShapeDtypeStruct((HD, rows), jnp.float32)]
+    aliases = {len(operands) + i: i for i in range(len(states))}
+    if not states:
+        shapes = [jax.ShapeDtypeStruct((HD, rows), jnp.bfloat16)] + shapes
+    if last:
+        shapes = [jax.ShapeDtypeStruct((tok, rows // (2 * tok) * HD), jnp.bfloat16)] * 2
+        aliases = {}
+    return pl.pallas_call(
+        kernel,
+        out_shape=shapes,
+        in_specs=[smem] + [vmem] * (len(operands) - 1 + len(states)),
+        out_specs=[vmem] * len(shapes),
+        input_output_aliases=aliases,
+        compiler_params=params,
+        cost_estimate=light,
+        name="flash",
+    )(*operands, *states)
+
+
+def times_weight(me, step, n, low, high, w_ref, at):
+    depth = w_ref.shape[0] // 2
+    owner = owner_of(me, step, n)
+    rows = jnp.concatenate([low[...], high[...]], axis=0)
+    side = w_ref[pl.ds(pl.multiple_of(owner % 2 * depth, depth), depth), at]
+    return owner, jnp.dot(rows, side, preferred_element_type=jnp.float32)
+
+
+def pair_project_kernel(n, steps, *refs):
+    arrays, w_ref, out_ref = refs[: 2 * len(steps)], refs[2 * len(steps)], refs[-1]
+    me = lax.axis_index("ctx")
+    wide = w_ref.shape[1]
+    width = min(256, wide)
+    for col in range(0, wide, width):
+        at = slice(col, col + width)
+        for i, step in enumerate(steps):
+            owner, product = times_weight(
+                me, step, n, arrays[2 * i], arrays[2 * i + 1], w_ref, at
+            )
+            out_ref[owner, :, at] = product.astype(jnp.bfloat16)
+
+
+def pair_project(n, steps, arrays, out_weight, buffer):
+    shape = (n, 2 * arrays[0].shape[0], out_weight.shape[1])
+    return pl.pallas_call(
+        functools.partial(pair_project_kernel, n, steps),
+        out_shape=jax.ShapeDtypeStruct(shape, jnp.bfloat16),
+        in_specs=[vmem] * (len(arrays) + 1 + len(buffer)),
+        out_specs=vmem,
+        input_output_aliases={len(arrays) + 1: 0} if buffer else {},
+        compiler_params=params,
+        cost_estimate=light,
+        name="project",
+    )(*arrays, out_weight, *buffer)
+
+
+def levels_of(n):
+    me = lax.axis_index("ctx")
+    side = lax.axis_index("tp") // 2
+    far = owner_of(me, n // 2, n) // 2
+    stay = jnp.where(far == 2 * side, 2 * side + 1, 2 * side)
+    away = 2 * (1 - side)
+    send = jnp.where(far == away, away + 1, away)
+    other = jnp.where(far // 2 == side, away + 1, 2 * side + 1)
+    return stay, send, other, far
+
+
+def split_halves(total, keep, send, i, at):
+    odd = lax.axis_index("tp") % 2
+    half = total.shape[0] // 2
+    low, high = total[:half], total[half:]
+    keep[i, :, at] = jnp.where(odd == 0, low, high).astype(jnp.bfloat16)
+    send[i, :, at] = jnp.where(odd == 0, high, low).astype(jnp.bfloat16)
+
+
+def pair_add_kernel(n, buffer_ref, keep_ref, *send_refs):
+    odd = lax.axis_index("tp") % 2
+    pieces = len(send_refs) // 3
+    for i, level in enumerate(levels_of(n)[:3]):
+        total = added(buffer_ref[2 * level], buffer_ref[2 * level + 1]).astype(jnp.bfloat16)
+        half = total.shape[0] // 2
+        size = half // pieces
+        low, high = total[:half], total[half:]
+        keep_ref[i] = jnp.where(odd == 0, low, high)
+        send = jnp.where(odd == 0, high, low)
+        for k in range(pieces):
+            send_refs[i * pieces + k][0] = send[k * size : (k + 1) * size]
+
+
+def pair_add(n, buffer, pieces=2):
+    _, rows, wide = buffer.shape
+    return pl.pallas_call(
+        functools.partial(pair_add_kernel, n),
+        out_shape=[jax.ShapeDtypeStruct((3, rows // 2, wide), jnp.bfloat16)]
+        + [jax.ShapeDtypeStruct((1, rows // 2 // pieces, wide), jnp.bfloat16)] * (3 * pieces),
+        in_specs=[vmem],
+        out_specs=[vmem] * (1 + 3 * pieces),
+        compiler_params=params,
+        cost_estimate=light,
+        name="add",
+    )(buffer)
+
+
+def pair_far_kernel(n, low, high, w_ref, buffer_ref, keep_ref, send_ref):
+    me = lax.axis_index("ctx")
+    wide = w_ref.shape[1]
+    width = min(256, wide)
+    for col in range(0, wide, width):
+        at = slice(col, col + width)
+        owner, product = times_weight(me, n // 2, n, low, high, w_ref, at)
+        total = product + buffer_ref[lax.bitwise_xor(owner, 1), :, at].astype(jnp.float32)
+        split_halves(total, keep_ref, send_ref, 0, at)
+
+
+def pair_far(n, arrays, out_weight, buffer):
+    _, rows, wide = buffer.shape
+    return pl.pallas_call(
+        functools.partial(pair_far_kernel, n),
+        out_shape=[jax.ShapeDtypeStruct((1, rows // 2, wide), jnp.bfloat16)] * 2,
+        in_specs=[vmem] * 4,
+        out_specs=[vmem, vmem],
+        compiler_params=params,
+        cost_estimate=light,
+        name="project",
+    )(*arrays, out_weight, buffer)
+
+
+def pair_sort_kernel(keep_ref, *refs):
+    got_refs, outs = refs[:-3], refs[-3:]
+    pieces = len(got_refs) // 3
+    size = keep_ref.shape[1] // pieces
+    for i, out in enumerate(outs):
+        for k in range(pieces):
+            at = slice(k * size, (k + 1) * size)
+            got = got_refs[i * pieces + k][0]
+            out[0, at, :] = added(keep_ref[i, at, :], got).astype(jnp.bfloat16)
+
+
+def pair_sort(keep, got):
+    shape = jax.ShapeDtypeStruct((1,) + keep.shape[1:], jnp.bfloat16)
+    return pl.pallas_call(
+        pair_sort_kernel,
+        out_shape=[shape] * 3,
+        in_specs=[vmem] * (1 + len(got)),
+        out_specs=[vmem] * 3,
+        compiler_params=params,
+        cost_estimate=light,
+        name="sort",
+    )(keep, *got)
+
+
+def pair_last_kernel(n, keep_ref, got_ref, other_ref, stay_ref, send_ref):
+    far = levels_of(n)[3]
+    stays = far // 2 == lax.axis_index("tp") // 2
+    total = added(keep_ref[...], got_ref[...]).astype(jnp.bfloat16)
+    stay_ref[...] = jnp.where(stays, total, other_ref[...])
+    send_ref[...] = jnp.where(stays, other_ref[...], total)
+
+
+def pair_last(n, keep, got, other):
+    return pl.pallas_call(
+        functools.partial(pair_last_kernel, n),
+        out_shape=[jax.ShapeDtypeStruct(keep.shape, jnp.bfloat16)] * 2,
+        in_specs=[vmem] * 3,
+        out_specs=[vmem] * 2,
+        compiler_params=params,
+        cost_estimate=light,
+        name="last",
+    )(keep, got, other)
+
+
+def pair_choose_kernel(n, stay_ref, got_ref, last_stay_ref, last_got_ref, mine_ref, give_ref):
+    first = levels_of(n)[0] == lax.axis_index("tp")
+    early = added(stay_ref[...], got_ref[...]).astype(jnp.bfloat16)
+    late = added(last_stay_ref[...], last_got_ref[...]).astype(jnp.bfloat16)
+    mine_ref[...] = jnp.where(first, early, late)
+    give_ref[...] = jnp.where(first, late, early)
+
+
+def pair_choose(n, *arrays):
+    return pl.pallas_call(
+        functools.partial(pair_choose_kernel, n),
+        out_shape=[jax.ShapeDtypeStruct(arrays[0].shape, jnp.bfloat16)] * 2,
+        in_specs=[vmem] * 4,
+        out_specs=[vmem, vmem],
+        compiler_params=params,
+        cost_estimate=light,
+        name="choose",
+    )(*arrays)
+
+
+def pair_body(n, n_tp, queries, suffix_kv, cache_pool, hit_count, hit_slots, out_weight):
+    tok, wide = queries.shape
+    half, levels = n // 2, n // 2
+    order = ring_order(n)
+    right = [(order[i], order[(i + 1) % n]) for i in range(n)]
+    left = [(b, a) for a, b in right]
+    swap = [(t, t ^ 1) for t in range(n_tp)]
+    over = [(t, t ^ 2) for t in range(n_tp)]
+    flip = [(i, i ^ 1) for i in range(n)]
+    parity = lax.axis_index("ctx") % 2
+
+    def both(pair, ways, token):
+        if token is not None:
+            pair = [after(a, token) for a in pair]
+        return tuple(lax.ppermute(a, "ctx", way) for a, way in zip(pair, ways))
+
+    mine, other = pair_pick(hit_slots, cache_pool, suffix_kv)
+    near = [both((mine, mine), (right, left), None)]
+    q_other = lax.dynamic_slice_in_dim(queries, (1 - parity) * (wide // 2), wide // 2, 1)
+    q_got = lax.ppermute(q_other, "ctx", flip)
+    got = lax.ppermute(other, "ctx", flip)
+    far = [both((got, got), (right, left), None)]
+    rows = wide // 2 // HD * 2 * tok
+    turned, *state = pair_flash(
+        functools.partial(pair_first_kernel, tok),
+        tok, rows, (hit_count, queries, q_got, mine), (), False,
+    )
+
+    def absorb(step, part, pair, state):
+        last = (step, part) == (levels - 1, 1)
+        kernel = functools.partial(pair_step_kernel, n, tok, step, part, last)
+        return pair_flash(kernel, tok, rows, (hit_count, turned, *pair), state, last)
+
+    first = near_state = middle = state[0]
+    for step in range(1, levels):
+        if step == 2:
+            near.append(both(near[-1], (right, left), None))
+            far.append(both(far[-1], (right, left), first))
+        elif step > 2:
+            near.append(both(near[-1], (right, left), first))
+            far.append(both(far[-1], (right, left), mid))
+        state = absorb(step, 0, near[step - 1], state)
+        near_state = state[0]
+        if step == 1:
+            state = absorb(0, 1, (got, got), state)
+        middle = state[0]
+        if step == 1:
+            early, mid = near_state, middle
+        state = absorb(step, 1, far[step - 1], state)
+    attention = state
+
+    held = [both((a, a), (right, left), None) for a in attention]
+    buffer, token = (), None
+    for step in range(1, half):
+        arrived = held
+        if step < half - 1:
+            held = [both(pair, (right, left), token) for pair in arrived]
+        else:
+            held = [
+                lax.ppermute(after(arrived[0][0], token), "ctx", right),
+                lax.ppermute(after(arrived[1][1], token), "ctx", left),
+            ]
+        arrays = [arrived[k][side] for side in range(2) for k in range(2)]
+        steps = (-step, step)
+        if step == 1:
+            arrays, steps = list(attention) + arrays, (0, -1, 1)
+        buffer = (pair_project(n, steps, arrays, out_weight, buffer),)
+        token = buffer[0]
+    keep, *sends = pair_add(n, token)
+    got = [lax.ppermute(send, "tp", swap) for send in sends]
+    stay, send, other = pair_sort(after(keep, tuple(held)), got)
+    got = lax.ppermute(send, "tp", over)
+    keep, send = pair_far(n, held, out_weight, token)
+    last_stay, last_send = pair_last(n, keep, lax.ppermute(send, "tp", swap), other)
+    last_got = lax.ppermute(last_send, "tp", over)
+    mine, give = pair_choose(n, stay, got, last_stay, last_got)
+    return join(mine, lax.ppermute(give, "tp", swap))
+
+
 def solution(mesh):
     n, n_tp = mesh.shape["ctx"], mesh.shape["tp"]
     placed = (
@@ -469,8 +929,14 @@
         P("ctx", None),
         P("tp", "ctx"),
     )
+
+    def run(*arrays):
+        slots_dev = arrays[1].shape[2] // HD
+        paired = slots_dev == 2 and n_tp == 4 and n == 2 * n_tp
+        return (pair_body if paired else body)(n, n_tp, *arrays)
+
     return jax.shard_map(
-        functools.partial(body, n, n_tp),
+        run,
         mesh=mesh,
         in_specs=placed,
         out_specs=P("tp", "ctx"),

time: 108 us -> 120 us (1.11)
  waiting for transfers between devices: 36.9 us -> 48.5 us
  Pallas kernels: 34.4 us -> 29.9 us
  starting transfers between devices: 32.1 us -> 36.4 us
    ppermute x35 -> x38, waiting for transfers between devices: 36.9 us -> 48.5 us  [the longest x24 23.7 us: both(): return tuple((lax.ppermute(a, 'ctx', way) for a, way in zip(pair, ways)))]
    pallas_call x16 -> x17, Pallas kernels: 33.6 us -> 29.1 us  [the longest x8 20 us: pair_flash(): pl.pallas_call(kernel, out_shape=shapes, in_specs=[smem] + [vmem] * (len(...]
    ppermute x35 -> x38, starting transfers between devices: 32.1 us -> 36.4 us  [the longest x24 26.3 us: both(): return tuple((lax.ppermute(a, 'ctx', way) for a, way in zip(pair, ways)))]
    unnamed x12 -> x10, local copies, waits for them, and re-layouts: 3.6 us -> 3.31 us
  transfers between devices with their start and end apart: 35 -> 38, of which waited for: 15 -> 22; matrix products, arithmetic and copies ran while one was open for 0% -> 1% of each run, Pallas kernels for 26% -> 20%
where the time goes in v2:
time: 120 us; the launch traced here: 119 us
  waiting for transfers between devices  48.5 us (40%)
  starting transfers between devices  36.4 us (30%)
  Pallas kernels  29.9 us (25%)
  local copies, waits for them, and re-layouts  4.27 us (4%)
    ppermute x24, starting transfers between devices, both(): return tuple((lax.ppermute(a, 'ctx', way) for a, way in zip(pair, ways)))  26.3 us
    ppermute x24, waiting for transfers between devices, both(): return tuple((lax.ppermute(a, 'ctx', way) for a, way in zip(pair, ways)))  23.7 us
    pallas_call x8, Pallas kernels, pair_flash(): pl.pallas_call(kernel, out_shape=shapes, in_specs=[smem] + [vmem] * (len(...  20 us
    ppermute x1, waiting for transfers between devices, pair_body(): got = lax.ppermute(send, 'tp', over)  6.92 us
    ppermute x1, waiting for transfers between devices, pair_body(): last_got = lax.ppermute(last_send, 'tp', over)  4.87 us
    pallas_call x3, Pallas kernels, pair_project(): pl.pallas_call(functools.partial(pair_project_kernel, n, steps), out_shap...  4.63 us
    ppermute x1, waiting for transfers between devices, pair_body(): got = lax.ppermute(other, 'ctx', flip)  4.22 us
    ppermute x1, waiting for transfers between devices, pair_body(): q_got = lax.ppermute(q_other, 'ctx', flip)  3.56 us
  transfers between devices with their start and end apart: 38, of which 22 were waited for; matrix products, arithmetic and copies ran while one was open for 1% of the time, Pallas kernels for 20%

profile of v2, /device:TPU:0, one launch (start us, length us, event | category | flops | bytes accessed | tf_op | source)
XLA Modules:
  0.0 119.3 jit_solution(16592217790140476966)
XLA Ops:
  0.0 2.7 %pick.1 = (bf16[2,512,128]{2,1,0:T(8,128)(2,1)}, bf16[2,512,128]{2,1,0:T(8,128)(2,1)}) custom-call(s32[1,3]{1,0:T(1,128)} %hit_slots.1, bf16[2,16,128,256]{3,2,1,0:T(8,128)(2,1)} %pool_ref.1, bf16[2,128,256]{2,1,0:T(8,128)(2,1)} %suffix_ref.1), custom_call_target="tpu_custom_call" | custom-call | tf_op jit(solution)/shard_map/pick/pallas_call | solution.py:491
  2.7 3.0 %collective-permute-start.1 = (bf16[2,512,128]{2,1,0:T(8,128)(2,1)}, bf16[2,512,128]{2,1,0:T(8,128)(2,1)S(1)}, u32[]{:S(2)}, u32[]{:S(2)}) collective-permute-start(bf16[2,512,128]{2,1,0:T(8,128)(2,1)} %get-tuple-element.62), channel_id=1, source_target_pairs={{0,4},{4,0},{8,12},{12,8},{16,20},{20,16},{24,28},{28,24},{1,5},{5... | collective-permute-start | bytes 786440 | tf_op jit(solution)/shard_map/ppermute | solution.py:863
  8.9 4.2 %collective-permute-done.1.left_ref.right_ref = bf16[2,512,128]{2,1,0:T(8,128)(2,1)S(1)} collective-permute-done((bf16[2,512,128]{2,1,0:T(8,128)(2,1)}, bf16[2,512,128]{2,1,0:T(8,128)(2,1)S(1)}, u32[]{:S(2)}, u32[]{:S(2)}) %collective-permute-start.1) | collective-permute-done | bytes 262176 | tf_op jit(solution)/shard_map/ppermute | solution.py:863
  13.1 2.1 %collective-permute-start.7 = (bf16[2,512,128]{2,1,0:T(8,128)(2,1)S(1)}, bf16[2,512,128]{2,1,0:T(8,128)(2,1)S(1)}, u32[]{:S(2)}, u32[]{:S(2)}) collective-permute-start(bf16[2,512,128]{2,1,0:T(8,128)(2,1)S(1)} %collective-permute-done.1.left_ref.right_ref), channel_id=1, source_target_pairs={{8,0},{16,8},{24,16},{28,24},{20,28},{12,20},{4,12},{0,4},{9,1},{1... | collective-permute-start | bytes 786440 | tf_op jit(solution)/shard_map/ppermute | solution.py:857
  15.2 3.5 %collective-permute-done.4.left_ref = bf16[2,512,128]{2,1,0:T(8,128)(2,1)S(1)} collective-permute-done((bf16[2,512,128]{2,1,0:T(8,128)(2,1)}, bf16[2,512,128]{2,1,0:T(8,128)(2,1)S(1)}, u32[]{:S(2)}, u32[]{:S(2)}) %collective-permute-start.4) | collective-permute-done | bytes 262176 | tf_op jit(solution)/shard_map/ppermute | solution.py:857
  18.7 2.1 %collective-permute-start.12 = (bf16[2,512,128]{2,1,0:T(8,128)(2,1)S(1)}, bf16[2,512,128]{2,1,0:T(8,128)(2,1)S(1)}, u32[]{:S(2)}, u32[]{:S(2)}) collective-permute-start(bf16[2,512,128]{2,1,0:T(8,128)(2,1)S(1)} %collective-permute-done.5.right_ref), channel_id=1, source_target_pairs={{8,0},{16,8},{24,16},{28,24},{20,28},{12,20},{4,12},{0,4},{9,1},{1... | collective-permute-start | bytes 786440 | tf_op jit(solution)/shard_map/ppermute | solution.py:857
  20.8 3.6 %collective-permute-done.q_got_ref = bf16[128,1024]{1,0:T(8,128)(2,1)S(1)} collective-permute-done((bf16[128,1024]{1,0:T(8,128)(2,1)S(1)}, bf16[128,1024]{1,0:T(8,128)(2,1)S(1)}, u32[]{:S(2)}, u32[]{:S(2)}) %collective-permute-start) | collective-permute-done | bytes 262176 | tf_op jit(solution)/shard_map/ppermute | solution.py:862
  27.0 2.6 %flash.8 = (bf16[128,2048]{1,0:T(8,128)(2,1)S(1)}, f32[8,2048]{1,0:T(8,128)S(1)}, f32[8,2048]{1,0:T(8,128)S(1)}, f32[128,2048]{1,0:T(8,128)S(1)}) custom-call(s32[8]{0:T(128)S(1)} %copy-done.3, bf16[128,2048]{1,0:T(8,128)(2,1)S(1)} %copy-done.1, bf16[128,1024]{1,0:T(8,128)(2,1)S(1)} %collective-permute-done.q_got_ref, bf16[2,512,128]{2,1,0:T(8,128)(2,1)S(1)} %copy-done.2), custom_call_target="tpu_custom_call" | custom-call | flops 1000 | bytes 1000 | tf_op jit(solution)/shard_map/flash/pallas_call | solution.py:660
  29.6 2.5 %collective-permute-start.8 = (bf16[2,512,128]{2,1,0:T(8,128)(2,1)S(1)}, bf16[2,512,128]{2,1,0:T(8,128)(2,1)S(1)}, u32[]{:S(2)}, u32[]{:S(2)}) collective-permute-start(bf16[2,512,128]{2,1,0:T(8,128)(2,1)S(1)} %collective-permute-done.7.right_ref), channel_id=1, source_target_pairs={{8,0},{16,8},{24,16},{28,24},{20,28},{12,20},{4,12},{0,4},{9,1},{1... | collective-permute-start | bytes 786440 | tf_op jit(solution)/shard_map/ppermute | solution.py:857
  32.0 3.6 %collective-permute-done.10.left_ref = bf16[2,512,128]{2,1,0:T(8,128)(2,1)S(1)} collective-permute-done((bf16[2,512,128]{2,1,0:T(8,128)(2,1)S(1)}, bf16[2,512,128]{2,1,0:T(8,128)(2,1)S(1)}, u32[]{:S(2)}, u32[]{:S(2)}) %collective-permute-start.10) | collective-permute-done | bytes 262176 | tf_op jit(solution)/shard_map/ppermute | solution.py:857
  35.6 2.1 %collective-permute-start.13 = (bf16[2,512,128]{2,1,0:T(8,128)(2,1)S(1)}, bf16[2,512,128]{2,1,0:T(8,128)(2,1)S(1)}, u32[]{:S(2)}, u32[]{:S(2)}) collective-permute-start(bf16[2,512,128]{2,1,0:T(8,128)(2,1)S(1)} %collective-permute-done.12.right_ref), channel_id=1, source_target_pairs={{8,0},{16,8},{24,16},{28,24},{20,28},{12,20},{4,12},{0,4},{9,1},{1... | collective-permute-start | bytes 786440 | tf_op jit(solution)/shard_map/ppermute | solution.py:857
  38.3 2.5 %flash.9 = (f32[8,2048]{1,0:T(8,128)S(1)}, f32[8,2048]{1,0:T(8,128)S(1)}, f32[128,2048]{1,0:T(8,128)S(1)}) custom-call(s32[8]{0:T(128)S(1)} %copy-done.4, bf16[128,2048]{1,0:T(8,128)(2,1)S(1)} %get-tuple-element.61.turned_ref, bf16[2,512,128]{2,1,0:T(8,128)(2,1)S(1)} %collective-permute-done.4.left_ref, ...), custom_call_target="tpu_custom_call", output_to_operand_aliasing={{0}: (4, {}), {1}: (5, {}), {2}: (6, {})} | custom-call | flops 1000 | bytes 1000 | tf_op jit(solution)/shard_map/flash/pallas_call | solution.py:660
  40.8 2.5 %flash.10 = (f32[8,2048]{1,0:T(8,128)S(1)}, f32[8,2048]{1,0:T(8,128)S(1)}, f32[128,2048]{1,0:T(8,128)S(1)}) custom-call(s32[8]{0:T(128)S(1)} %copy-done.4, bf16[128,2048]{1,0:T(8,128)(2,1)S(1)} %get-tuple-element.61.turned_ref, ...), custom_call_target="tpu_custom_call", output_to_operand_aliasing={{0}: (4, {}), {1}: (5, {}), {2}: (6, {})} | custom-call | flops 1000 | bytes 1000 | tf_op jit(solution)/shard_map/flash/pallas_call | solution.py:660
  43.3 2.1 %collective-permute-start.9 = (bf16[2,512,128]{2,1,0:T(8,128)(2,1)S(1)}, bf16[2,512,128]{2,1,0:T(8,128)(2,1)S(1)}, u32[]{:S(2)}, u32[]{:S(2)}) collective-permute-start(bf16[2,512,128]{2,1,0:T(8,128)(2,1)S(1)} %collective-permute-done.8.right_ref), channel_id=1, source_target_pairs={{8,0},{16,8},{24,16},{28,24},{20,28},{12,20},{4,12},{0,4},{9,1},{1... | collective-permute-start | bytes 786440 | tf_op jit(solution)/shard_map/ppermute | solution.py:857
  45.4 2.6 %flash.11 = (f32[8,2048]{1,0:T(8,128)S(1)}, f32[8,2048]{1,0:T(8,128)S(1)}, f32[128,2048]{1,0:T(8,128)S(1)}) custom-call(s32[8]{0:T(128)S(1)} %copy-done.4, bf16[128,2048]{1,0:T(8,128)(2,1)S(1)} %get-tuple-element.61.turned_ref, bf16[2,512,128]{2,1,0:T(8,128)(2,1)S(1)} %collective-permute-done.2.left_ref, ...), custom_call_target="tpu_custom_call", output_to_operand_aliasing={{0}: (4, {}), {1}: (5, {}), {2}: (6, {})} | custom-call | flops 1000 | bytes 1000 | tf_op jit(solution)/shard_map/flash/pallas_call | solution.py:660
  48.0 2.5 %flash.12 = (f32[8,2048]{1,0:T(8,128)S(1)}, f32[8,2048]{1,0:T(8,128)S(1)}, f32[128,2048]{1,0:T(8,128)S(1)}) custom-call(s32[8]{0:T(128)S(1)} %copy-done.4, bf16[128,2048]{1,0:T(8,128)(2,1)S(1)} %get-tuple-element.61.turned_ref, bf16[2,512,128]{2,1,0:T(8,128)(2,1)S(1)} %collective-permute-done.10.left_ref, ...), custom_call_target="tpu_custom_call", output_to_operand_aliasing={{0}: (4, {}), {1}: (5, {}), {2}: (6, {})} | custom-call | flops 1000 | bytes 1000 | tf_op jit(solution)/shard_map/flash/pallas_call | solution.py:660
  50.5 2.5 %flash.13 = (f32[8,2048]{1,0:T(8,128)S(1)}, f32[8,2048]{1,0:T(8,128)S(1)}, f32[128,2048]{1,0:T(8,128)S(1)}) custom-call(s32[8]{0:T(128)S(1)} %copy-done.4, bf16[128,2048]{1,0:T(8,128)(2,1)S(1)} %get-tuple-element.61.turned_ref, bf16[2,512,128]{2,1,0:T(8,128)(2,1)S(1)} %collective-permute-done.3.left_ref, ...), custom_call_target="tpu_custom_call", output_to_operand_aliasing={{0}: (4, {}), {1}: (5, {}), {2}: (6, {})} | custom-call | flops 1000 | bytes 1000 | tf_op jit(solution)/shard_map/flash/pallas_call | solution.py:660
  53.0 2.5 %flash.14 = (f32[8,2048]{1,0:T(8,128)S(1)}, f32[8,2048]{1,0:T(8,128)S(1)}, f32[128,2048]{1,0:T(8,128)S(1)}) custom-call(s32[8]{0:T(128)S(1)} %copy-done.4, bf16[128,2048]{1,0:T(8,128)(2,1)S(1)} %get-tuple-element.61.turned_ref, bf16[2,512,128]{2,1,0:T(8,128)(2,1)S(1)} %collective-permute-done.11.left_ref, ...), custom_call_target="tpu_custom_call", output_to_operand_aliasing={{0}: (4, {}), {1}: (5, {}), {2}: (6, {})} | custom-call | flops 1000 | bytes 1000 | tf_op jit(solution)/shard_map/flash/pallas_call | solution.py:660
  55.5 2.4 %flash.15 = (bf16[128,1024]{1,0:T(8,128)(2,1)S(1)}, bf16[128,1024]{1,0:T(8,128)(2,1)S(1)}) custom-call(s32[8]{0:T(128)S(1)} %copy-done.4, bf16[128,2048]{1,0:T(8,128)(2,1)S(1)} %get-tuple-element.61.turned_ref, bf16[2,512,128]{2,1,0:T(8,128)(2,1)S(1)} %collective-permute-done.6.left_ref, bf16[2,512,128]{2,1,0:T(8,128)(2,1)S(1)} %collective-permute-done.9.right_ref, ...), custom_call_target="tpu_custom_call" | custom-call | flops 1000 | bytes 1000 | tf_op jit(solution)/shard_map/flash/pallas_call | solution.py:660
  58.1 1.9 %collective-permute-start.18 = (bf16[128,1024]{1,0:T(8,128)(2,1)S(1)}, bf16[128,1024]{1,0:T(8,128)(2,1)S(1)}, u32[]{:S(2)}, u32[]{:S(2)}) collective-permute-start(bf16[128,1024]{1,0:T(8,128)(2,1)S(1)} %get-tuple-element.91.refs_1_), channel_id=1, source_target_pairs={{8,0},{16,8},{24,16},{28,24},{20,28},{12,20},{4,12},{0,4},{9,1},{1... | collective-permute-start | bytes 786440 | tf_op jit(solution)/shard_map/ppermute | solution.py:857
  60.1 1.9 %collective-permute-start.17 = (bf16[128,1024]{1,0:T(8,128)(2,1)S(1)}, bf16[128,1024]{1,0:T(8,128)(2,1)S(1)}, u32[]{:S(2)}, u32[]{:S(2)}) collective-permute-start(bf16[128,1024]{1,0:T(8,128)(2,1)S(1)} %get-tuple-element.90.refs_0_), channel_id=1, source_target_pairs={{8,0},{16,8},{24,16},{28,24},{20,28},{12,20},{4,12},{0,4},{9,1},{1... | collective-permute-start | bytes 786440 | tf_op jit(solution)/shard_map/ppermute | solution.py:857
  62.1 5.1 %collective-permute-done.14.refs_2_ = bf16[128,1024]{1,0:T(8,128)(2,1)S(1)} collective-permute-done((bf16[128,1024]{1,0:T(8,128)(2,1)S(1)}, bf16[128,1024]{1,0:T(8,128)(2,1)S(1)}, u32[]{:S(2)}, u32[]{:S(2)}) %collective-permute-start.14) | collective-permute-done | bytes 262176 | tf_op jit(solution)/shard_map/ppermute | solution.py:857
  67.4 1.9 %collective-permute-start.24 = (bf16[128,1024]{1,0:T(8,128)(2,1)S(1)}, bf16[128,1024]{1,0:T(8,128)(2,1)S(1)}, u32[]{:S(2)}, u32[]{:S(2)}) collective-permute-start(bf16[128,1024]{1,0:T(8,128)(2,1)S(1)} %collective-permute-done.18.refs_5_), channel_id=1, source_target_pairs={{8,0},{16,8},{24,16},{28,24},{20,28},{12,20},{4,12},{0,4},{9,1},{1... | collective-permute-start | bytes 786440 | tf_op jit(solution)/shard_map/ppermute | solution.py:857
  69.3 3.5 %collective-permute-done.16.refs_3_ = bf16[128,1024]{1,0:T(8,128)(2,1)S(1)} collective-permute-done((bf16[128,1024]{1,0:T(8,128)(2,1)S(1)}, bf16[128,1024]{1,0:T(8,128)(2,1)S(1)}, u32[]{:S(2)}, u32[]{:S(2)}) %collective-permute-start.16) | collective-permute-done | bytes 262176 | tf_op jit(solution)/shard_map/ppermute | solution.py:857
  73.0 1.9 %collective-permute-start.22 = (bf16[128,1024]{1,0:T(8,128)(2,1)S(1)}, bf16[128,1024]{1,0:T(8,128)(2,1)S(1)}, u32[]{:S(2)}, u32[]{:S(2)}) collective-permute-start(bf16[128,1024]{1,0:T(8,128)(2,1)S(1)} %collective-permute-done.17.refs_4_), channel_id=1, source_target_pairs={{8,0},{16,8},{24,16},{28,24},{20,28},{12,20},{4,12},{0,4},{9,1},{1... | collective-permute-start | bytes 786440 | tf_op jit(solution)/shard_map/ppermute | solution.py:857
  74.9 2.0 %project.4.refs_5_ = bf16[8,256,1024]{2,1,0:T(8,128)(2,1)S(1)} custom-call(bf16[128,1024]{1,0:T(8,128)(2,1)S(1)} %get-tuple-element.90.refs_0_, bf16[128,1024]{1,0:T(8,128)(2,1)S(1)} %get-tuple-element.91.refs_1_, bf16[128,1024]{1,0:T(8,128)(2,1)S(1)} %collective-permute-done.14.refs_2_, bf16[128,1024]{1,0:T(8,128)(2,1)S(1)} %collective-permute-done.16.refs_3_, ...), custom_call_target="tpu_custom_call" | custom-call | flops 1000 | bytes 1000 | tf_op jit(solution)/shard_map/project/pallas_call | solution.py:696
  80.5 3.5 %collective-permute-done.20.refs_1_ = bf16[128,1024]{1,0:T(8,128)(2,1)S(1)} collective-permute-done((bf16[128,1024]{1,0:T(8,128)(2,1)S(1)}, bf16[128,1024]{1,0:T(8,128)(2,1)S(1)}, u32[]{:S(2)}, u32[]{:S(2)}) %collective-permute-start.20) | collective-permute-done | bytes 262176 | tf_op jit(solution)/shard_map/ppermute | solution.py:857
  84.2 3.1 %collective-permute-start.21 = (bf16[128,1024]{1,0:T(8,128)(2,1)S(1)}, bf16[128,1024]{1,0:T(8,128)(2,1)S(1)}, u32[]{:S(2)}, u32[]{:S(2)}) collective-permute-start(bf16[128,1024]{1,0:T(8,128)(2,1)S(1)} %collective-permute-done.20.refs_1_), channel_id=1, source_target_pairs={{0,8},{8,16},{16,24},{24,28},{28,20},{20,12},{12,4},{4,0},{1,9},{9... | collective-permute-start | bytes 786440 | tf_op jit(solution)/shard_map/ppermute | solution.py:857
  89.8 3.1 %collective-permute-start.26 = (bf16[128,1024]{1,0:T(8,128)(2,1)S(1)}, bf16[128,1024]{1,0:T(8,128)(2,1)S(1)}, u32[]{:S(2)}, u32[]{:S(2)}) collective-permute-start(bf16[128,1024]{1,0:T(8,128)(2,1)S(1)} %collective-permute-done.19.refs_0_), channel_id=1, source_target_pairs={{0,8},{8,16},{16,24},{24,28},{28,20},{20,12},{12,4},{4,0},{1,9},{9... | collective-permute-start | bytes 786440 | tf_op jit(solution)/shard_map/ppermute | solution.py:902
  97.2 2.1 %collective-permute-done.27.high = bf16[128,1024]{1,0:T(8,128)(2,1)S(1)} collective-permute-done((bf16[128,1024]{1,0:T(8,128)(2,1)S(1)}, bf16[128,1024]{1,0:T(8,128)(2,1)S(1)}, u32[]{:S(2)}, u32[]{:S(2)}) %collective-permute-start.27) | collective-permute-done | bytes 262176 | tf_op jit(solution)/shard_map/ppermute | solution.py:903
  105.0 6.9 %collective-permute-done.34.got_ref = bf16[1,128,1024]{2,1,0:T(8,128)(2,1)S(1)} collective-permute-done((bf16[1,128,1024]{2,1,0:T(8,128)(2,1)S(1)}, bf16[1,128,1024]{2,1,0:T(8,128)(2,1)S(1)}, u32[]{:S(2)}, u32[]{:S(2)}) %collective-permute-start.34) | collective-permute-done | bytes 262176 | tf_op jit(solution)/shard_map/ppermute | solution.py:914
  111.9 4.9 %collective-permute-done.36.last_got_ref = bf16[1,128,1024]{2,1,0:T(8,128)(2,1)S(1)} collective-permute-done((bf16[1,128,1024]{2,1,0:T(8,128)(2,1)S(1)}, bf16[1,128,1024]{2,1,0:T(8,128)(2,1)S(1)}, u32[]{:S(2)}, u32[]{:S(2)}) %collective-permute-start.36) | collective-permute-done | bytes 262176 | tf_op jit(solution)/shard_map/ppermute | solution.py:917
  (73 shorter events, 26.0 us)
Async XLA Ops:
  2.7 10.4 %collective-permute-start.1 = (bf16[2,512,128]{2,1,0:T(8,128)(2,1)}, bf16[2,512,128]{2,1,0:T(8,128)(2,1)S(1)}, u32[]{:S(2)}, u32[]{:S(2)}) collective-permute-start(bf16[2,512,128]{2,1,0:T(8,128)(2,1)} %get-tuple-element.62), channel_id=1, source_target_pairs={{0,4},{4,0},{8,12},{12,8},{16,20},{20,16},{24,28},{28,24},{1,5},{5... | collective-permute-start | bytes 786440 | tf_op jit(solution)/shard_map/ppermute | solution.py:863
  5.8 13.0 %collective-permute-start.4 = (bf16[2,512,128]{2,1,0:T(8,128)(2,1)}, bf16[2,512,128]{2,1,0:T(8,128)(2,1)S(1)}, u32[]{:S(2)}, u32[]{:S(2)}) collective-permute-start(bf16[2,512,128]{2,1,0:T(8,128)(2,1)} %get-tuple-element.60.mine_ref), channel_id=1, source_target_pairs={{0,8},{8,16},{16,24},{24,28},{28,20},{20,12},{12,4},{4,0},{1,9},{9... | collective-permute-start | bytes 786440 | tf_op jit(solution)/shard_map/ppermute | solution.py:857
  7.3 11.4 %collective-permute-start.5 = (bf16[2,512,128]{2,1,0:T(8,128)(2,1)}, bf16[2,512,128]{2,1,0:T(8,128)(2,1)S(1)}, u32[]{:S(2)}, u32[]{:S(2)}) collective-permute-start(bf16[2,512,128]{2,1,0:T(8,128)(2,1)} %get-tuple-element.60.mine_ref), channel_id=1, source_target_pairs={{8,0},{16,8},{24,16},{28,24},{20,28},{12,20},{4,12},{0,4},{9,1},{1... | collective-permute-start | bytes 786440 | tf_op jit(solution)/shard_map/ppermute | solution.py:857
  8.8 15.6 %collective-permute-start = (bf16[128,1024]{1,0:T(8,128)(2,1)S(1)}, bf16[128,1024]{1,0:T(8,128)(2,1)S(1)}, u32[]{:S(2)}, u32[]{:S(2)}) collective-permute-start(bf16[128,1024]{1,0:T(8,128)(2,1)S(1)} %constant_dynamic-slice_fusion), channel_id=1, source_target_pairs={{0,4},{4,0},{8,12},{12,8},{16,20},{20,16},{24,28},{28,24},{1,5},{5... | collective-permute-start | bytes 786440 | tf_op jit(solution)/shard_map/ppermute | solution.py:862
  13.1 16.4 %collective-permute-start.7 = (bf16[2,512,128]{2,1,0:T(8,128)(2,1)S(1)}, bf16[2,512,128]{2,1,0:T(8,128)(2,1)S(1)}, u32[]{:S(2)}, u32[]{:S(2)}) collective-permute-start(bf16[2,512,128]{2,1,0:T(8,128)(2,1)S(1)} %collective-permute-done.1.left_ref.right_ref), channel_id=1, source_target_pairs={{8,0},{16,8},{24,16},{28,24},{20,28},{12,20},{4,12},{0,4},{9,1},{1... | collective-permute-start | bytes 786440 | tf_op jit(solution)/shard_map/ppermute | solution.py:857
  15.2 16.9 %collective-permute-start.2 = (bf16[2,512,128]{2,1,0:T(8,128)(2,1)S(1)}, bf16[2,512,128]{2,1,0:T(8,128)(2,1)S(1)}, u32[]{:S(2)}, u32[]{:S(2)}) collective-permute-start(bf16[2,512,128]{2,1,0:T(8,128)(2,1)S(1)} %collective-permute-done.1.left_ref.right_ref), channel_id=1, source_target_pairs={{0,8},{8,16},{16,24},{24,28},{28,20},{20,12},{12,4},{4,0},{1,9},{9... | collective-permute-start | bytes 786440 | tf_op jit(solution)/shard_map/ppermute | solution.py:857
  18.7 16.9 %collective-permute-start.10 = (bf16[2,512,128]{2,1,0:T(8,128)(2,1)S(1)}, bf16[2,512,128]{2,1,0:T(8,128)(2,1)S(1)}, u32[]{:S(2)}, u32[]{:S(2)}) collective-permute-start(bf16[2,512,128]{2,1,0:T(8,128)(2,1)S(1)} %collective-permute-done.4.left_ref), channel_id=1, source_target_pairs={{0,8},{8,16},{16,24},{24,28},{28,20},{20,12},{12,4},{4,0},{1,9},{9... | collective-permute-start | bytes 786440 | tf_op jit(solution)/shard_map/ppermute | solution.py:857
  18.7 16.8 %collective-permute-start.12 = (bf16[2,512,128]{2,1,0:T(8,128)(2,1)S(1)}, bf16[2,512,128]{2,1,0:T(8,128)(2,1)S(1)}, u32[]{:S(2)}, u32[]{:S(2)}) collective-permute-start(bf16[2,512,128]{2,1,0:T(8,128)(2,1)S(1)} %collective-permute-done.5.right_ref), channel_id=1, source_target_pairs={{8,0},{16,8},{24,16},{28,24},{20,28},{12,20},{4,12},{0,4},{9,1},{1... | collective-permute-start | bytes 786440 | tf_op jit(solution)/shard_map/ppermute | solution.py:857
  29.6 13.7 %collective-permute-start.8 = (bf16[2,512,128]{2,1,0:T(8,128)(2,1)S(1)}, bf16[2,512,128]{2,1,0:T(8,128)(2,1)S(1)}, u32[]{:S(2)}, u32[]{:S(2)}) collective-permute-start(bf16[2,512,128]{2,1,0:T(8,128)(2,1)S(1)} %collective-permute-done.7.right_ref), channel_id=1, source_target_pairs={{8,0},{16,8},{24,16},{28,24},{20,28},{12,20},{4,12},{0,4},{9,1},{1... | collective-permute-start | bytes 786440 | tf_op jit(solution)/shard_map/ppermute | solution.py:857
  32.0 11.2 %collective-permute-start.3 = (bf16[2,512,128]{2,1,0:T(8,128)(2,1)S(1)}, bf16[2,512,128]{2,1,0:T(8,128)(2,1)S(1)}, u32[]{:S(2)}, u32[]{:S(2)}) collective-permute-start(bf16[2,512,128]{2,1,0:T(8,128)(2,1)S(1)} %collective-permute-done.2.left_ref), channel_id=1, source_target_pairs={{0,8},{8,16},{16,24},{24,28},{28,20},{20,12},{12,4},{4,0},{1,9},{9... | collective-permute-start | bytes 786440 | tf_op jit(solution)/shard_map/ppermute | solution.py:857
  35.6 17.4 %collective-permute-start.11 = (bf16[2,512,128]{2,1,0:T(8,128)(2,1)S(1)}, bf16[2,512,128]{2,1,0:T(8,128)(2,1)S(1)}, u32[]{:S(2)}, u32[]{:S(2)}) collective-permute-start(bf16[2,512,128]{2,1,0:T(8,128)(2,1)S(1)} %collective-permute-done.10.left_ref), channel_id=1, source_target_pairs={{0,8},{8,16},{16,24},{24,28},{28,20},{20,12},{12,4},{4,0},{1,9},{9... | collective-permute-start | bytes 786440 | tf_op jit(solution)/shard_map/ppermute | solution.py:857
  35.6 17.4 %collective-permute-start.13 = (bf16[2,512,128]{2,1,0:T(8,128)(2,1)S(1)}, bf16[2,512,128]{2,1,0:T(8,128)(2,1)S(1)}, u32[]{:S(2)}, u32[]{:S(2)}) collective-permute-start(bf16[2,512,128]{2,1,0:T(8,128)(2,1)S(1)} %collective-permute-done.12.right_ref), channel_id=1, source_target_pairs={{8,0},{16,8},{24,16},{28,24},{20,28},{12,20},{4,12},{0,4},{9,1},{1... | collective-permute-start | bytes 786440 | tf_op jit(solution)/shard_map/ppermute | solution.py:857
  43.3 12.2 %collective-permute-start.9 = (bf16[2,512,128]{2,1,0:T(8,128)(2,1)S(1)}, bf16[2,512,128]{2,1,0:T(8,128)(2,1)S(1)}, u32[]{:S(2)}, u32[]{:S(2)}) collective-permute-start(bf16[2,512,128]{2,1,0:T(8,128)(2,1)S(1)} %collective-permute-done.8.right_ref), channel_id=1, source_target_pairs={{8,0},{16,8},{24,16},{28,24},{20,28},{12,20},{4,12},{0,4},{9,1},{1... | collective-permute-start | bytes 786440 | tf_op jit(solution)/shard_map/ppermute | solution.py:857
  45.4 10.1 %collective-permute-start.6 = (bf16[2,512,128]{2,1,0:T(8,128)(2,1)S(1)}, bf16[2,512,128]{2,1,0:T(8,128)(2,1)S(1)}, u32[]{:S(2)}, u32[]{:S(2)}) collective-permute-start(bf16[2,512,128]{2,1,0:T(8,128)(2,1)S(1)} %collective-permute-done.3.left_ref), channel_id=1, source_target_pairs={{0,8},{8,16},{16,24},{24,28},{28,20},{20,12},{12,4},{4,0},{1,9},{9... | collective-permute-start | bytes 786440 | tf_op jit(solution)/shard_map/ppermute | solution.py:857
  57.9 9.3 %collective-permute-start.14 = (bf16[128,1024]{1,0:T(8,128)(2,1)S(1)}, bf16[128,1024]{1,0:T(8,128)(2,1)S(1)}, u32[]{:S(2)}, u32[]{:S(2)}) collective-permute-start(bf16[128,1024]{1,0:T(8,128)(2,1)S(1)} %get-tuple-element.90.refs_0_), channel_id=1, source_target_pairs={{0,8},{8,16},{16,24},{24,28},{28,20},{20,12},{12,4},{4,0},{1,9},{9... | collective-permute-start | bytes 786440 | tf_op jit(solution)/shard_map/ppermute | solution.py:857
  58.1 9.2 %collective-permute-start.18 = (bf16[128,1024]{1,0:T(8,128)(2,1)S(1)}, bf16[128,1024]{1,0:T(8,128)(2,1)S(1)}, u32[]{:S(2)}, u32[]{:S(2)}) collective-permute-start(bf16[128,1024]{1,0:T(8,128)(2,1)S(1)} %get-tuple-element.91.refs_1_), channel_id=1, source_target_pairs={{8,0},{16,8},{24,16},{28,24},{20,28},{12,20},{4,12},{0,4},{9,1},{1... | collective-permute-start | bytes 786440 | tf_op jit(solution)/shard_map/ppermute | solution.py:857
  60.1 12.8 %collective-permute-start.16 = (bf16[128,1024]{1,0:T(8,128)(2,1)S(1)}, bf16[128,1024]{1,0:T(8,128)(2,1)S(1)}, u32[]{:S(2)}, u32[]{:S(2)}) collective-permute-start(bf16[128,1024]{1,0:T(8,128)(2,1)S(1)} %get-tuple-element.91.refs_1_), channel_id=1, source_target_pairs={{0,8},{8,16},{16,24},{24,28},{28,20},{20,12},{12,4},{4,0},{1,9},{9... | collective-permute-start | bytes 786440 | tf_op jit(solution)/shard_map/ppermute | solution.py:857
  60.1 12.8 %collective-permute-start.17 = (bf16[128,1024]{1,0:T(8,128)(2,1)S(1)}, bf16[128,1024]{1,0:T(8,128)(2,1)S(1)}, u32[]{:S(2)}, u32[]{:S(2)}) collective-permute-start(bf16[128,1024]{1,0:T(8,128)(2,1)S(1)} %get-tuple-element.90.refs_0_), channel_id=1, source_target_pairs={{8,0},{16,8},{24,16},{28,24},{20,28},{12,20},{4,12},{0,4},{9,1},{1... | collective-permute-start | bytes 786440 | tf_op jit(solution)/shard_map/ppermute | solution.py:857
  67.2 11.2 %collective-permute-start.15 = (bf16[128,1024]{1,0:T(8,128)(2,1)S(1)}, bf16[128,1024]{1,0:T(8,128)(2,1)S(1)}, u32[]{:S(2)}, u32[]{:S(2)}) collective-permute-start(bf16[128,1024]{1,0:T(8,128)(2,1)S(1)} %collective-permute-done.14.refs_2_), channel_id=1, source_target_pairs={{0,8},{8,16},{16,24},{24,28},{28,20},{20,12},{12,4},{4,0},{1,9},{9... | collective-permute-start | bytes 786440 | tf_op jit(solution)/shard_map/ppermute | solution.py:857
  67.4 11.2 %collective-permute-start.24 = (bf16[128,1024]{1,0:T(8,128)(2,1)S(1)}, bf16[128,1024]{1,0:T(8,128)(2,1)S(1)}, u32[]{:S(2)}, u32[]{:S(2)}) collective-permute-start(bf16[128,1024]{1,0:T(8,128)(2,1)S(1)} %collective-permute-done.18.refs_5_), channel_id=1, source_target_pairs={{8,0},{16,8},{24,16},{28,24},{20,28},{12,20},{4,12},{0,4},{9,1},{1... | collective-permute-start | bytes 786440 | tf_op jit(solution)/shard_map/ppermute | solution.py:857
  72.8 11.2 %collective-permute-start.20 = (bf16[128,1024]{1,0:T(8,128)(2,1)S(1)}, bf16[128,1024]{1,0:T(8,128)(2,1)S(1)}, u32[]{:S(2)}, u32[]{:S(2)}) collective-permute-start(bf16[128,1024]{1,0:T(8,128)(2,1)S(1)} %collective-permute-done.16.refs_3_), channel_id=1, source_target_pairs={{0,8},{8,16},{16,24},{24,28},{28,20},{20,12},{12,4},{4,0},{1,9},{9... | collective-permute-start | bytes 786440 | tf_op jit(solution)/shard_map/ppermute | solution.py:857
  73.0 11.2 %collective-permute-start.22 = (bf16[128,1024]{1,0:T(8,128)(2,1)S(1)}, bf16[128,1024]{1,0:T(8,128)(2,1)S(1)}, u32[]{:S(2)}, u32[]{:S(2)}) collective-permute-start(bf16[128,1024]{1,0:T(8,128)(2,1)S(1)} %collective-permute-done.17.refs_4_), channel_id=1, source_target_pairs={{8,0},{16,8},{24,16},{28,24},{20,28},{12,20},{4,12},{0,4},{9,1},{1... | collective-permute-start | bytes 786440 | tf_op jit(solution)/shard_map/ppermute | solution.py:857
  78.5 11.2 %collective-permute-start.19 = (bf16[128,1024]{1,0:T(8,128)(2,1)S(1)}, bf16[128,1024]{1,0:T(8,128)(2,1)S(1)}, u32[]{:S(2)}, u32[]{:S(2)}) collective-permute-start(bf16[128,1024]{1,0:T(8,128)(2,1)S(1)} %collective-permute-done.15.refs_0_), channel_id=1, source_target_pairs={{0,8},{8,16},{16,24},{24,28},{28,20},{20,12},{12,4},{4,0},{1,9},{9... | collective-permute-start | bytes 786440 | tf_op jit(solution)/shard_map/ppermute | solution.py:857
  78.6 11.2 %collective-permute-start.25 = (bf16[128,1024]{1,0:T(8,128)(2,1)S(1)}, bf16[128,1024]{1,0:T(8,128)(2,1)S(1)}, u32[]{:S(2)}, u32[]{:S(2)}) collective-permute-start(bf16[128,1024]{1,0:T(8,128)(2,1)S(1)} %collective-permute-done.24.refs_3_), channel_id=1, source_target_pairs={{8,0},{16,8},{24,16},{28,24},{20,28},{12,20},{4,12},{0,4},{9,1},{1... | collective-permute-start | bytes 786440 | tf_op jit(solution)/shard_map/ppermute | solution.py:857
  84.2 10.2 %collective-permute-start.21 = (bf16[128,1024]{1,0:T(8,128)(2,1)S(1)}, bf16[128,1024]{1,0:T(8,128)(2,1)S(1)}, u32[]{:S(2)}, u32[]{:S(2)}) collective-permute-start(bf16[128,1024]{1,0:T(8,128)(2,1)S(1)} %collective-permute-done.20.refs_1_), channel_id=1, source_target_pairs={{0,8},{8,16},{16,24},{24,28},{28,20},{20,12},{12,4},{4,0},{1,9},{9... | collective-permute-start | bytes 786440 | tf_op jit(solution)/shard_map/ppermute | solution.py:857
  87.3 7.2 %collective-permute-start.23 = (bf16[128,1024]{1,0:T(8,128)(2,1)S(1)}, bf16[128,1024]{1,0:T(8,128)(2,1)S(1)}, u32[]{:S(2)}, u32[]{:S(2)}) collective-permute-start(bf16[128,1024]{1,0:T(8,128)(2,1)S(1)} %collective-permute-done.22.refs_2_), channel_id=1, source_target_pairs={{8,0},{16,8},{24,16},{28,24},{20,28},{12,20},{4,12},{0,4},{9,1},{1... | collective-permute-start | bytes 786440 | tf_op jit(solution)/shard_map/ppermute | solution.py:857
  89.8 7.4 %collective-permute-start.26 = (bf16[128,1024]{1,0:T(8,128)(2,1)S(1)}, bf16[128,1024]{1,0:T(8,128)(2,1)S(1)}, u32[]{:S(2)}, u32[]{:S(2)}) collective-permute-start(bf16[128,1024]{1,0:T(8,128)(2,1)S(1)} %collective-permute-done.19.refs_0_), channel_id=1, source_target_pairs={{0,8},{8,16},{16,24},{24,28},{28,20},{20,12},{12,4},{4,0},{1,9},{9... | collective-permute-start | bytes 786440 | tf_op jit(solution)/shard_map/ppermute | solution.py:902
  92.9 6.4 %collective-permute-start.27 = (bf16[128,1024]{1,0:T(8,128)(2,1)S(1)}, bf16[128,1024]{1,0:T(8,128)(2,1)S(1)}, u32[]{:S(2)}, u32[]{:S(2)}) collective-permute-start(bf16[128,1024]{1,0:T(8,128)(2,1)S(1)} %collective-permute-done.25.refs_3_), channel_id=1, source_target_pairs={{8,0},{16,8},{24,16},{28,24},{20,28},{12,20},{4,12},{0,4},{9,1},{1... | collective-permute-start | bytes 786440 | tf_op jit(solution)/shard_map/ppermute | solution.py:903
  96.3 4.4 %collective-permute-start.28 = (bf16[1,64,1024]{2,1,0:T(8,128)(2,1)S(1)}, bf16[1,64,1024]{2,1,0:T(8,128)(2,1)S(1)}, u32[]{:S(2)}, u32[]{:S(2)}) collective-permute-start(bf16[1,64,1024]{2,1,0:T(8,128)(2,1)S(1)} %get-tuple-element.100), channel_id=1, source_target_pairs={{0,1},{1,0},{2,3},{3,2},{4,5},{5,4},{6,7},{7,6},{8,9},{9,8},{10,11... | collective-permute-start | bytes 393224 | tf_op jit(solution)/shard_map/ppermute | solution.py:912
  96.4 4.8 %collective-permute-start.29 = (bf16[1,64,1024]{2,1,0:T(8,128)(2,1)S(1)}, bf16[1,64,1024]{2,1,0:T(8,128)(2,1)S(1)}, u32[]{:S(2)}, u32[]{:S(2)}) collective-permute-start(bf16[1,64,1024]{2,1,0:T(8,128)(2,1)S(1)} %get-tuple-element.101), channel_id=1, source_target_pairs={{0,1},{1,0},{2,3},{3,2},{4,5},{5,4},{6,7},{7,6},{8,9},{9,8},{10,11... | collective-permute-start | bytes 393224 | tf_op jit(solution)/shard_map/ppermute | solution.py:912
  102.7 9.2 %collective-permute-start.34 = (bf16[1,128,1024]{2,1,0:T(8,128)(2,1)S(1)}, bf16[1,128,1024]{2,1,0:T(8,128)(2,1)S(1)}, u32[]{:S(2)}, u32[]{:S(2)}) collective-permute-start(bf16[1,128,1024]{2,1,0:T(8,128)(2,1)S(1)} %get-tuple-element.107), channel_id=1, source_target_pairs={{0,2},{1,3},{2,0},{3,1},{4,6},{5,7},{6,4},{7,5},{8,10},{9,11},{10,... | collective-permute-start | bytes 786440 | tf_op jit(solution)/shard_map/ppermute | solution.py:914
  104.4 12.4 %collective-permute-start.36 = (bf16[1,128,1024]{2,1,0:T(8,128)(2,1)S(1)}, bf16[1,128,1024]{2,1,0:T(8,128)(2,1)S(1)}, u32[]{:S(2)}, u32[]{:S(2)}) collective-permute-start(bf16[1,128,1024]{2,1,0:T(8,128)(2,1)S(1)} %get-tuple-element.112), channel_id=1, source_target_pairs={{0,2},{1,3},{2,0},{3,1},{4,6},{5,7},{6,4},{7,5},{8,10},{9,11},{10,... | collective-permute-start | bytes 786440 | tf_op jit(solution)/shard_map/ppermute | solution.py:917
  (11 other events, 42.0 us)

commit v3 on v1

--- a/solution.py
+++ b/solution.py
@@ -212,9 +212,13 @@
     half = rows.shape[0] // (2 * count)
     wide = w_ref.shape[1]
     width = min(256, wide)
+    deep = w_ref.shape[0] // 2
+    depths = (slice(0, deep), slice(deep, 2 * deep))
     for col in range(0, wide, width):
         at = slice(col, col + width)
-        product = jnp.dot(rows, w_ref[:, at], preferred_element_type=jnp.float32)
+        product = sum(
+            jnp.dot(rows[:, k], w_ref[k, at], preferred_element_type=jnp.float32) for k in depths
+        )
         product = product.astype(jnp.bfloat16)
         for i in range(count):
             low = product[2 * i * half : (2 * i + 1) * half]
@@ -266,11 +270,12 @@
 
 def sort_kernel(n, n_tp, steps, *refs):
     *refs, stay_ref, send_ref, last_stay_ref, last_send_ref = refs
-    count = len(refs) // 2
-    places = [(a, b, i) for a, b in zip(refs[:count], refs[count:]) for i in range(a.shape[0])]
+    count = len(refs) - len(steps)
+    places = [(a, i) for a in refs[:count] for i in range(a.shape[0])]
+    places = [(a, b, i) for (a, i), b in zip(places, refs[count:])]
     full = stay_ref.shape[0]
     for (a, b, i), (_, away, rank) in zip(places, sides(n, n_tp, steps)):
-        total = added(a[i], b[i]).astype(jnp.bfloat16)
+        total = added(a[i], b[0]).astype(jnp.bfloat16)
         for side, out, last in ((0, stay_ref, last_stay_ref), (1, send_ref, last_send_ref)):
 
             @pl.when((away == side) & (rank < full))
@@ -283,14 +288,15 @@
 
 
 def sort(n, n_tp, steps, sums):
-    keeps, gots = zip(*sums)
+    keeps = [keep for keep, _ in sums]
+    gots = [piece for _, pieces in sums for piece in pieces]
     half, wide = keeps[0].shape[1:]
     many = jax.ShapeDtypeStruct((n // 2 - 1, half, wide), jnp.bfloat16)
     one = jax.ShapeDtypeStruct((1, half, wide), jnp.bfloat16)
     return pl.pallas_call(
         functools.partial(sort_kernel, n, n_tp, steps),
         out_shape=[many, many, one, one],
-        in_specs=[vmem] * (2 * len(sums)),
+        in_specs=[vmem] * (len(keeps) + len(gots)),
         out_specs=[vmem] * 4,
         compiler_params=params,
         cost_estimate=light,
@@ -428,7 +434,8 @@
 
     def reduce(arrays):
         keep, send = project(arrays, out_weight)
-        sums.append((keep, lax.ppermute(send, "tp", swap)))
+        pieces = [send[i : i + 1] for i in range(send.shape[0])]
+        sums.append((keep, [lax.ppermute(piece, "tp", swap) for piece in pieces]))
         return send
 
     def spread(step, arrived, token):
@@ -449,11 +456,11 @@
 
     far, _ = ring(attention, spread, None)
     steps = [0] + [s * d for d in range(1, half) for s in (-1, 1)] + [half]
-    sums[0] = (after(sums[0][0], far), sums[0][1])
     stay, send, last_stay, last_send = sort(n, n_tp, steps[:-1], sums)
     stay, got = cross(stay, send)
     reduce(far)
-    last_stay, last_send = place_last(n, n_tp, *sums[-1], last_stay, last_send)
+    keep, (piece,) = sums[-1]
+    last_stay, last_send = place_last(n, n_tp, keep, piece, last_stay, last_send)
     last_stay, last_got = cross(last_stay, last_send)
     mine, give = choose(n, n_tp, steps, (stay, got, last_stay, last_got))
     return join(mine, lax.ppermute(give, "tp", swap))

time: 108 us -> 111 us (1.028)
  starting transfers between devices: 32.1 us -> 34.1 us
    ppermute x2, waiting for transfers between devices: 7.62 us -> 4.06 us  [cross(): got = lax.ppermute(send, 'tp', [(t, t ^ 2) for t in range(n_tp)])]
    ppermute x2, waiting for transfers between devices: 1.41 us -> 2.84 us  [ring(): lax.ppermute(after(arrived[1][1], token), 'ctx', left)]
    ppermute x4 -> x8, waiting for transfers between devices: 1.34 us -> 2.42 us  [reduce(): sums.append((keep, [lax.ppermute(piece, 'tp', swap) for piece in pieces]))]
  transfers between devices with their start and end apart: 35 -> 39, of which waited for: 15 -> 18; matrix products, arithmetic and copies ran while one was open for 0% -> 0% of each run, Pallas kernels for 26% -> 25%
where the time goes in v3:
time: 111 us; the launch traced here: 110 us
  waiting for transfers between devices  38 us (34%)
  Pallas kernels  34.4 us (31%)
  starting transfers between devices  34.1 us (31%)
  local copies, waits for them, and re-layouts  3.67 us (3%)
    ppermute x12, starting transfers between devices, send_both(): lax.ppermute(from_right, 'ctx', left)  19.8 us
    pallas_call x8, Pallas kernels, flash(): pl.pallas_call(functools.partial(flash_kernel, n, tok, pieces, not state,...  18.6 us
    ppermute x12, waiting for transfers between devices, send_both(): lax.ppermute(from_right, 'ctx', left)  15.4 us
    pallas_call x4, Pallas kernels, project(): pl.pallas_call(functools.partial(project_kernel, count), out_shape=[jax.S...  11.2 us
    ppermute x12, waiting for transfers between devices, send_both(): lax.ppermute(from_left, 'ctx', right)  9.62 us
    ppermute x12, starting transfers between devices, send_both(): lax.ppermute(from_left, 'ctx', right)  5.89 us
    ppermute x2, waiting for transfers between devices, cross(): got = lax.ppermute(send, 'tp', [(t, t ^ 2) for t in range(n_tp)])  4.06 us
    ppermute x2, starting transfers between devices, ring(): lax.ppermute(after(arrived[1][1], token), 'ctx', left)  3.82 us
  transfers between devices with their start and end apart: 39, of which 18 were waited for; matrix products, arithmetic and copies ran while one was open for 0% of the time, Pallas kernels for 25%

profile of v3, /device:TPU:0, one launch (start us, length us, event | category | flops | bytes accessed | tf_op | source)
XLA Modules:
  0.0 110.5 jit_solution(17690775892690612330)
XLA Ops:
  0.0 2.8 %pick.1 = (bf16[2,256,256]{2,1,0:T(8,128)(2,1)}, bf16[2,256,256]{2,1,0:T(8,128)(2,1)}) custom-call(s32[1,3]{1,0:T(1,128)} %hit_slots.1, bf16[2,16,128,256]{3,2,1,0:T(8,128)(2,1)} %pool_ref.1, bf16[2,128,256]{2,1,0:T(8,128)(2,1)} %suffix_ref.1), custom_call_target="tpu_custom_call" | custom-call | tf_op jit(solution)/shard_map/pick/pallas_call | solution.py:63
  2.8 3.0 %collective-permute-start.3 = (bf16[2,256,256]{2,1,0:T(8,128)(2,1)}, bf16[2,256,256]{2,1,0:T(8,128)(2,1)S(1)}, u32[]{:S(2)}, u32[]{:S(2)}) collective-permute-start(bf16[2,256,256]{2,1,0:T(8,128)(2,1)} %get-tuple-element.68.refs_1_), channel_id=1, source_target_pairs={{8,0},{16,8},{24,16},{28,24},{20,28},{12,20},{4,12},{0,4},{9,1},{1... | collective-permute-start | bytes 786440 | tf_op jit(solution)/shard_map/ppermute | solution.py:400
  6.0 2.0 %collective-permute-start.2 = (bf16[2,256,256]{2,1,0:T(8,128)(2,1)}, bf16[2,256,256]{2,1,0:T(8,128)(2,1)S(1)}, u32[]{:S(2)}, u32[]{:S(2)}) collective-permute-start(bf16[2,256,256]{2,1,0:T(8,128)(2,1)} %get-tuple-element.68.refs_1_), channel_id=1, source_target_pairs={{0,8},{8,16},{16,24},{24,28},{28,20},{20,12},{12,4},{4,0},{1,9},{9... | collective-permute-start | bytes 786440 | tf_op jit(solution)/shard_map/ppermute | solution.py:400
  11.6 2.4 %flash.8 = (bf16[128,2048]{1,0:T(8,128)(2,1)S(1)}, f32[8,2048]{1,0:T(8,128)S(1)}, f32[8,2048]{1,0:T(8,128)S(1)}, f32[128,2048]{1,0:T(8,128)S(1)}) custom-call(s32[8]{0:T(128)S(1)} %copy-done.4, bf16[128,2048]{1,0:T(8,128)(2,1)S(1)} %copy-done.1, bf16[2,256,256]{2,1,0:T(8,128)(2,1)S(1)} %copy-done.2, bf16[2,256,256]{2,1,0:T(8,128)(2,1)S(1)} %copy-done.3), custom_call_target="tpu_custom_call" | custom-call | flops 1000 | bytes 1000 | tf_op jit(solution)/shard_map/flash/pallas_call | solution.py:196
  14.0 2.0 %collective-permute-start.7 = (bf16[2,256,256]{2,1,0:T(8,128)(2,1)S(1)}, bf16[2,256,256]{2,1,0:T(8,128)(2,1)S(1)}, u32[]{:S(2)}, u32[]{:S(2)}) collective-permute-start(bf16[2,256,256]{2,1,0:T(8,128)(2,1)S(1)} %collective-permute-done.3.refs_1_), channel_id=1, source_target_pairs={{8,0},{16,8},{24,16},{28,24},{20,28},{12,20},{4,12},{0,4},{9,1},{1... | collective-permute-start | bytes 786440 | tf_op jit(solution)/shard_map/ppermute | solution.py:400
  16.1 4.8 %collective-permute-done.2.refs_0_ = bf16[2,256,256]{2,1,0:T(8,128)(2,1)S(1)} collective-permute-done((bf16[2,256,256]{2,1,0:T(8,128)(2,1)}, bf16[2,256,256]{2,1,0:T(8,128)(2,1)S(1)}, u32[]{:S(2)}, u32[]{:S(2)}) %collective-permute-start.2) | collective-permute-done | bytes 262176 | tf_op jit(solution)/shard_map/ppermute | solution.py:400
  21.0 1.9 %collective-permute-start.8 = (bf16[2,256,256]{2,1,0:T(8,128)(2,1)S(1)}, bf16[2,256,256]{2,1,0:T(8,128)(2,1)S(1)}, u32[]{:S(2)}, u32[]{:S(2)}) collective-permute-start(bf16[2,256,256]{2,1,0:T(8,128)(2,1)S(1)} %collective-permute-done.4.refs_1_), channel_id=1, source_target_pairs={{8,0},{16,8},{24,16},{28,24},{20,28},{12,20},{4,12},{0,4},{9,1},{1... | collective-permute-start | bytes 786440 | tf_op jit(solution)/shard_map/ppermute | solution.py:400
  22.9 2.4 %flash.9 = (f32[8,2048]{1,0:T(8,128)S(1)}, f32[8,2048]{1,0:T(8,128)S(1)}, f32[128,2048]{1,0:T(8,128)S(1)}) custom-call(s32[8]{0:T(128)S(1)} %copy-done.4, bf16[128,2048]{1,0:T(8,128)(2,1)S(1)} %get-tuple-element.69.q_ref, bf16[2,256,256]{2,1,0:T(8,128)(2,1)S(1)} %collective-permute-done.refs_0_, ...), custom_call_target="tpu_custom_call", output_to_operand_aliasing={{0}: (4, {}), {1}: (5, {}), {2}: (6, {})} | custom-call | flops 1000 | bytes 1000 | tf_op jit(solution)/shard_map/flash/pallas_call | solution.py:196
  25.3 2.3 %flash.10 = (f32[8,2048]{1,0:T(8,128)S(1)}, f32[8,2048]{1,0:T(8,128)S(1)}, f32[128,2048]{1,0:T(8,128)S(1)}) custom-call(s32[8]{0:T(128)S(1)} %copy-done.4, bf16[128,2048]{1,0:T(8,128)(2,1)S(1)} %get-tuple-element.69.q_ref, bf16[2,256,256]{2,1,0:T(8,128)(2,1)S(1)} %collective-permute-done.2.refs_0_, ...), custom_call_target="tpu_custom_call", output_to_operand_aliasing={{0}: (4, {}), {1}: (5, {}), {2}: (6, {})} | custom-call | flops 1000 | bytes 1000 | tf_op jit(solution)/shard_map/flash/pallas_call | solution.py:196
  27.6 1.6 %collective-permute-start.10 = (bf16[2,256,256]{2,1,0:T(8,128)(2,1)S(1)}, bf16[2,256,256]{2,1,0:T(8,128)(2,1)S(1)}, u32[]{:S(2)}, u32[]{:S(2)}) collective-permute-start(bf16[2,256,256]{2,1,0:T(8,128)(2,1)S(1)} %collective-permute-done.7.refs_1_), channel_id=1, source_target_pairs={{8,0},{16,8},{24,16},{28,24},{20,28},{12,20},{4,12},{0,4},{9,1},{1... | collective-permute-start | bytes 786440 | tf_op jit(solution)/shard_map/ppermute | solution.py:400
  29.7 2.4 %collective-permute-done.6.refs_0_ = bf16[2,256,256]{2,1,0:T(8,128)(2,1)S(1)} collective-permute-done((bf16[2,256,256]{2,1,0:T(8,128)(2,1)S(1)}, bf16[2,256,256]{2,1,0:T(8,128)(2,1)S(1)}, u32[]{:S(2)}, u32[]{:S(2)}) %collective-permute-start.6) | collective-permute-done | bytes 262176 | tf_op jit(solution)/shard_map/ppermute | solution.py:400
  34.2 2.4 %flash.11 = (f32[8,2048]{1,0:T(8,128)S(1)}, f32[8,2048]{1,0:T(8,128)S(1)}, f32[128,2048]{1,0:T(8,128)S(1)}) custom-call(s32[8]{0:T(128)S(1)} %copy-done.5, bf16[128,2048]{1,0:T(8,128)(2,1)S(1)} %get-tuple-element.69.q_ref, bf16[2,256,256]{2,1,0:T(8,128)(2,1)S(1)} %collective-permute-done.1.refs_0_, ...), custom_call_target="tpu_custom_call", output_to_operand_aliasing={{0}: (4, {}), {1}: (5, {}), {2}: (6, {})} | custom-call | flops 1000 | bytes 1000 | tf_op jit(solution)/shard_map/flash/pallas_call | solution.py:196
  36.6 2.3 %flash.12 = (f32[8,2048]{1,0:T(8,128)S(1)}, f32[8,2048]{1,0:T(8,128)S(1)}, f32[128,2048]{1,0:T(8,128)S(1)}) custom-call(s32[8]{0:T(128)S(1)} %copy-done.5, bf16[128,2048]{1,0:T(8,128)(2,1)S(1)} %get-tuple-element.69.q_ref, bf16[2,256,256]{2,1,0:T(8,128)(2,1)S(1)} %collective-permute-done.6.refs_0_, ...), custom_call_target="tpu_custom_call", output_to_operand_aliasing={{0}: (4, {}), {1}: (5, {}), {2}: (6, {})} | custom-call | flops 1000 | bytes 1000 | tf_op jit(solution)/shard_map/flash/pallas_call | solution.py:196
  38.9 1.6 %collective-permute-start.11 = (bf16[2,256,256]{2,1,0:T(8,128)(2,1)S(1)}, bf16[2,256,256]{2,1,0:T(8,128)(2,1)S(1)}, u32[]{:S(2)}, u32[]{:S(2)}) collective-permute-start(bf16[2,256,256]{2,1,0:T(8,128)(2,1)S(1)} %collective-permute-done.10.refs_1_), channel_id=1, source_target_pairs={{8,0},{16,8},{24,16},{28,24},{20,28},{12,20},{4,12},{0,4},{9,1},{1... | collective-permute-start | bytes 786440 | tf_op jit(solution)/shard_map/ppermute | solution.py:412
  42.5 2.4 %flash.13 = (f32[8,2048]{1,0:T(8,128)S(1)}, f32[8,2048]{1,0:T(8,128)S(1)}, f32[128,2048]{1,0:T(8,128)S(1)}) custom-call(s32[8]{0:T(128)S(1)} %copy-done.5, bf16[128,2048]{1,0:T(8,128)(2,1)S(1)} %get-tuple-element.69.q_ref, bf16[2,256,256]{2,1,0:T(8,128)(2,1)S(1)} %collective-permute-done.5.refs_0_, ...), custom_call_target="tpu_custom_call", output_to_operand_aliasing={{0}: (4, {}), {1}: (5, {}), {2}: (6, {})} | custom-call | flops 1000 | bytes 1000 | tf_op jit(solution)/shard_map/flash/pallas_call | solution.py:196
  44.9 2.3 %flash.14 = (f32[8,2048]{1,0:T(8,128)S(1)}, f32[8,2048]{1,0:T(8,128)S(1)}, f32[128,2048]{1,0:T(8,128)S(1)}) custom-call(s32[8]{0:T(128)S(1)} %copy-done.5, bf16[128,2048]{1,0:T(8,128)(2,1)S(1)} %get-tuple-element.69.q_ref, bf16[2,256,256]{2,1,0:T(8,128)(2,1)S(1)} %collective-permute-done.12.refs_0_, ...), custom_call_target="tpu_custom_call", output_to_operand_aliasing={{0}: (4, {}), {1}: (5, {}), {2}: (6, {})} | custom-call | flops 1000 | bytes 1000 | tf_op jit(solution)/shard_map/flash/pallas_call | solution.py:196
  47.5 2.3 %flash.15 = (bf16[64,2048]{1,0:T(8,128)(2,1)S(1)}, bf16[64,2048]{1,0:T(8,128)(2,1)S(1)}) custom-call(s32[8]{0:T(128)S(1)} %copy-done.5, bf16[128,2048]{1,0:T(8,128)(2,1)S(1)} %get-tuple-element.69.q_ref, bf16[2,256,256]{2,1,0:T(8,128)(2,1)S(1)} %collective-permute-done.9.refs_0_, bf16[2,256,256]{2,1,0:T(8,128)(2,1)S(1)} %collective-permute-done.11.refs_1_, ...), custom_call_target="tpu_custom_call" | custom-call | flops 1000 | bytes 1000 | tf_op jit(solution)/shard_map/flash/pallas_call | solution.py:196
  49.8 1.6 %collective-permute-start.17 = (bf16[64,2048]{1,0:T(8,128)(2,1)S(1)}, bf16[64,2048]{1,0:T(8,128)(2,1)S(1)}, u32[]{:S(2)}, u32[]{:S(2)}) collective-permute-start(bf16[64,2048]{1,0:T(8,128)(2,1)S(1)} %get-tuple-element.102.refs_1_), channel_id=1, source_target_pairs={{8,0},{16,8},{24,16},{28,24},{20,28},{12,20},{4,12},{0,4},{9,1},{1... | collective-permute-start | bytes 786440 | tf_op jit(solution)/shard_map/ppermute | solution.py:400
  51.9 1.6 %collective-permute-start.16 = (bf16[64,2048]{1,0:T(8,128)(2,1)S(1)}, bf16[64,2048]{1,0:T(8,128)(2,1)S(1)}, u32[]{:S(2)}, u32[]{:S(2)}) collective-permute-start(bf16[64,2048]{1,0:T(8,128)(2,1)S(1)} %get-tuple-element.101.refs_0_), channel_id=1, source_target_pairs={{8,0},{16,8},{24,16},{28,24},{20,28},{12,20},{4,12},{0,4},{9,1},{1... | collective-permute-start | bytes 786440 | tf_op jit(solution)/shard_map/ppermute | solution.py:400
  53.9 5.2 %collective-permute-done.17.refs_5_ = bf16[64,2048]{1,0:T(8,128)(2,1)S(1)} collective-permute-done((bf16[64,2048]{1,0:T(8,128)(2,1)S(1)}, bf16[64,2048]{1,0:T(8,128)(2,1)S(1)}, u32[]{:S(2)}, u32[]{:S(2)}) %collective-permute-start.17) | collective-permute-done | bytes 262176 | tf_op jit(solution)/shard_map/ppermute | solution.py:400
  61.1 3.6 %collective-permute-done.16.refs_4_ = bf16[64,2048]{1,0:T(8,128)(2,1)S(1)} collective-permute-done((bf16[64,2048]{1,0:T(8,128)(2,1)S(1)}, bf16[64,2048]{1,0:T(8,128)(2,1)S(1)}, u32[]{:S(2)}, u32[]{:S(2)}) %collective-permute-start.16) | collective-permute-done | bytes 262176 | tf_op jit(solution)/shard_map/ppermute | solution.py:400
  64.7 1.6 %collective-permute-start.20 = (bf16[64,2048]{1,0:T(8,128)(2,1)S(1)}, bf16[64,2048]{1,0:T(8,128)(2,1)S(1)}, u32[]{:S(2)}, u32[]{:S(2)}) collective-permute-start(bf16[64,2048]{1,0:T(8,128)(2,1)S(1)} %collective-permute-done.16.refs_4_), channel_id=1, source_target_pairs={{8,0},{16,8},{24,16},{28,24},{20,28},{12,20},{4,12},{0,4},{9,1},{1... | collective-permute-start | bytes 786440 | tf_op jit(solution)/shard_map/ppermute | solution.py:400
  66.7 3.9 %project.4 = (bf16[3,64,1024]{2,1,0:T(8,128)(2,1)S(1)}, bf16[3,64,1024]{2,1,0:T(8,128)(2,1)S(1)}) custom-call(bf16[64,2048]{1,0:T(8,128)(2,1)S(1)} %get-tuple-element.101.refs_0_, bf16[64,2048]{1,0:T(8,128)(2,1)S(1)} %get-tuple-element.102.refs_1_, bf16[64,2048]{1,0:T(8,128)(2,1)S(1)} %collective-permute-done.14.refs_2_, ...), custom_call_target="tpu_custom_call" | custom-call | flops 1000 | bytes 1000 | tf_op jit(solution)/shard_map/project/pallas_call | solution.py:242
  70.7 1.6 %collective-permute-start.25 = (bf16[64,2048]{1,0:T(8,128)(2,1)S(1)}, bf16[64,2048]{1,0:T(8,128)(2,1)S(1)}, u32[]{:S(2)}, u32[]{:S(2)}) collective-permute-start(bf16[64,2048]{1,0:T(8,128)(2,1)S(1)} %collective-permute-done.21.refs_3_), channel_id=1, source_target_pairs={{8,0},{16,8},{24,16},{28,24},{20,28},{12,20},{4,12},{0,4},{9,1},{1... | collective-permute-start | bytes 786440 | tf_op jit(solution)/shard_map/ppermute | solution.py:400
  72.8 3.2 %collective-permute-done.20.refs_2_ = bf16[64,2048]{1,0:T(8,128)(2,1)S(1)} collective-permute-done((bf16[64,2048]{1,0:T(8,128)(2,1)S(1)}, bf16[64,2048]{1,0:T(8,128)(2,1)S(1)}, u32[]{:S(2)}, u32[]{:S(2)}) %collective-permute-start.20) | collective-permute-done | bytes 262176 | tf_op jit(solution)/shard_map/ppermute | solution.py:400
  78.1 2.8 %project.5 = (bf16[2,64,1024]{2,1,0:T(8,128)(2,1)S(1)}, bf16[2,64,1024]{2,1,0:T(8,128)(2,1)S(1)}) custom-call(bf16[64,2048]{1,0:T(8,128)(2,1)S(1)} %collective-permute-done.18.refs_0_, bf16[64,2048]{1,0:T(8,128)(2,1)S(1)} %collective-permute-done.19.refs_1_, bf16[64,2048]{1,0:T(8,128)(2,1)S(1)} %collective-permute-done.20.refs_2_, ...), custom_call_target="tpu_custom_call" | custom-call | flops 1000 | bytes 1000 | tf_op jit(solution)/shard_map/project/pallas_call | solution.py:242
  85.4 2.8 %project.6 = (bf16[2,64,1024]{2,1,0:T(8,128)(2,1)S(1)}, bf16[2,64,1024]{2,1,0:T(8,128)(2,1)S(1)}) custom-call(bf16[64,2048]{1,0:T(8,128)(2,1)S(1)} %collective-permute-done.22.refs_0_, bf16[64,2048]{1,0:T(8,128)(2,1)S(1)} %collective-permute-done.23.refs_1_, bf16[64,2048]{1,0:T(8,128)(2,1)S(1)} %collective-permute-done.24.refs_2_, ...), custom_call_target="tpu_custom_call" | custom-call | flops 1000 | bytes 1000 | tf_op jit(solution)/shard_map/project/pallas_call | solution.py:242
  88.2 2.2 %collective-permute-start.35 = (bf16[64,2048]{1,0:T(8,128)(2,1)S(1)}, bf16[64,2048]{1,0:T(8,128)(2,1)S(1)}, u32[]{:S(2)}, u32[]{:S(2)}) collective-permute-start(bf16[64,2048]{1,0:T(8,128)(2,1)S(1)} %collective-permute-done.25.refs_3_), channel_id=1, source_target_pairs={{8,0},{16,8},{24,16},{28,24},{20,28},{12,20},{4,12},{0,4},{9,1},{1... | collective-permute-start | bytes 786440 | tf_op jit(solution)/shard_map/ppermute | solution.py:412
  94.2 2.8 %collective-permute-done.35.refs_1_ = bf16[64,2048]{1,0:T(8,128)(2,1)S(1)} collective-permute-done((bf16[64,2048]{1,0:T(8,128)(2,1)S(1)}, bf16[64,2048]{1,0:T(8,128)(2,1)S(1)}, u32[]{:S(2)}, u32[]{:S(2)}) %collective-permute-start.35) | collective-permute-done | bytes 262176 | tf_op jit(solution)/shard_map/ppermute | solution.py:412
  97.0 1.9 %collective-permute-done.34.refs_0_ = bf16[64,2048]{1,0:T(8,128)(2,1)S(1)} collective-permute-done((bf16[64,2048]{1,0:T(8,128)(2,1)S(1)}, bf16[64,2048]{1,0:T(8,128)(2,1)S(1)}, u32[]{:S(2)}, u32[]{:S(2)}) %collective-permute-start.34) | collective-permute-done | bytes 262176 | tf_op jit(solution)/shard_map/ppermute | solution.py:411
  98.9 1.7 %project.7 = (bf16[1,64,1024]{2,1,0:T(8,128)(2,1)S(1)}, bf16[1,64,1024]{2,1,0:T(8,128)(2,1)S(1)}) custom-call(bf16[64,2048]{1,0:T(8,128)(2,1)S(1)} %collective-permute-done.34.refs_0_, bf16[64,2048]{1,0:T(8,128)(2,1)S(1)} %collective-permute-done.35.refs_1_, bf16[2048,1024]{1,0:T(8,128)(2,1)S(1)} %copy-done), custom_call_target="tpu_custom_call" | custom-call | flops 1000 | bytes 1000 | tf_op jit(solution)/shard_map/project/pallas_call | solution.py:242
  103.6 4.1 %collective-permute-done.37.refs_3_ = bf16[1,64,1024]{2,1,0:T(8,128)(2,1)S(1)} collective-permute-done((bf16[1,64,1024]{2,1,0:T(8,128)(2,1)S(1)}, bf16[1,64,1024]{2,1,0:T(8,128)(2,1)S(1)}, u32[]{:S(2)}, u32[]{:S(2)}) %collective-permute-start.37) | collective-permute-done | bytes 131104 | tf_op jit(solution)/shard_map/ppermute | solution.py:449
  (78 shorter events, 28.8 us)
Async XLA Ops:
  2.8 11.2 %collective-permute-start.3 = (bf16[2,256,256]{2,1,0:T(8,128)(2,1)}, bf16[2,256,256]{2,1,0:T(8,128)(2,1)S(1)}, u32[]{:S(2)}, u32[]{:S(2)}) collective-permute-start(bf16[2,256,256]{2,1,0:T(8,128)(2,1)} %get-tuple-element.68.refs_1_), channel_id=1, source_target_pairs={{8,0},{16,8},{24,16},{28,24},{20,28},{12,20},{4,12},{0,4},{9,1},{1... | collective-permute-start | bytes 786440 | tf_op jit(solution)/shard_map/ppermute | solution.py:400
  5.9 10.1 %collective-permute-start = (bf16[2,256,256]{2,1,0:T(8,128)(2,1)}, bf16[2,256,256]{2,1,0:T(8,128)(2,1)S(1)}, u32[]{:S(2)}, u32[]{:S(2)}) collective-permute-start(bf16[2,256,256]{2,1,0:T(8,128)(2,1)} %get-tuple-element.67.refs_0_), channel_id=1, source_target_pairs={{0,8},{8,16},{16,24},{24,28},{28,20},{20,12},{12,4},{4,0},{1,9},{9... | collective-permute-start | bytes 786440 | tf_op jit(solution)/shard_map/ppermute | solution.py:400
  6.0 14.9 %collective-permute-start.2 = (bf16[2,256,256]{2,1,0:T(8,128)(2,1)}, bf16[2,256,256]{2,1,0:T(8,128)(2,1)S(1)}, u32[]{:S(2)}, u32[]{:S(2)}) collective-permute-start(bf16[2,256,256]{2,1,0:T(8,128)(2,1)} %get-tuple-element.68.refs_1_), channel_id=1, source_target_pairs={{0,8},{8,16},{16,24},{24,28},{28,20},{20,12},{12,4},{4,0},{1,9},{9... | collective-permute-start | bytes 786440 | tf_op jit(solution)/shard_map/ppermute | solution.py:400
  7.9 13.0 %collective-permute-start.4 = (bf16[2,256,256]{2,1,0:T(8,128)(2,1)}, bf16[2,256,256]{2,1,0:T(8,128)(2,1)S(1)}, u32[]{:S(2)}, u32[]{:S(2)}) collective-permute-start(bf16[2,256,256]{2,1,0:T(8,128)(2,1)} %get-tuple-element.67.refs_0_), channel_id=1, source_target_pairs={{8,0},{16,8},{24,16},{28,24},{20,28},{12,20},{4,12},{0,4},{9,1},{1... | collective-permute-start | bytes 786440 | tf_op jit(solution)/shard_map/ppermute | solution.py:400
  14.0 13.6 %collective-permute-start.7 = (bf16[2,256,256]{2,1,0:T(8,128)(2,1)S(1)}, bf16[2,256,256]{2,1,0:T(8,128)(2,1)S(1)}, u32[]{:S(2)}, u32[]{:S(2)}) collective-permute-start(bf16[2,256,256]{2,1,0:T(8,128)(2,1)S(1)} %collective-permute-done.3.refs_1_), channel_id=1, source_target_pairs={{8,0},{16,8},{24,16},{28,24},{20,28},{12,20},{4,12},{0,4},{9,1},{1... | collective-permute-start | bytes 786440 | tf_op jit(solution)/shard_map/ppermute | solution.py:400
  16.0 13.3 %collective-permute-start.1 = (bf16[2,256,256]{2,1,0:T(8,128)(2,1)S(1)}, bf16[2,256,256]{2,1,0:T(8,128)(2,1)S(1)}, u32[]{:S(2)}, u32[]{:S(2)}) collective-permute-start(bf16[2,256,256]{2,1,0:T(8,128)(2,1)S(1)} %collective-permute-done.refs_0_), channel_id=1, source_target_pairs={{0,8},{8,16},{16,24},{24,28},{28,20},{20,12},{12,4},{4,0},{1,9},{9... | collective-permute-start | bytes 786440 | tf_op jit(solution)/shard_map/ppermute | solution.py:400
  20.9 11.2 %collective-permute-start.6 = (bf16[2,256,256]{2,1,0:T(8,128)(2,1)S(1)}, bf16[2,256,256]{2,1,0:T(8,128)(2,1)S(1)}, u32[]{:S(2)}, u32[]{:S(2)}) collective-permute-start(bf16[2,256,256]{2,1,0:T(8,128)(2,1)S(1)} %collective-permute-done.2.refs_0_), channel_id=1, source_target_pairs={{0,8},{8,16},{16,24},{24,28},{28,20},{20,12},{12,4},{4,0},{1,9},{9... | collective-permute-start | bytes 786440 | tf_op jit(solution)/shard_map/ppermute | solution.py:400
  21.0 11.2 %collective-permute-start.8 = (bf16[2,256,256]{2,1,0:T(8,128)(2,1)S(1)}, bf16[2,256,256]{2,1,0:T(8,128)(2,1)S(1)}, u32[]{:S(2)}, u32[]{:S(2)}) collective-permute-start(bf16[2,256,256]{2,1,0:T(8,128)(2,1)S(1)} %collective-permute-done.4.refs_1_), channel_id=1, source_target_pairs={{8,0},{16,8},{24,16},{28,24},{20,28},{12,20},{4,12},{0,4},{9,1},{1... | collective-permute-start | bytes 786440 | tf_op jit(solution)/shard_map/ppermute | solution.py:400
  27.6 11.2 %collective-permute-start.10 = (bf16[2,256,256]{2,1,0:T(8,128)(2,1)S(1)}, bf16[2,256,256]{2,1,0:T(8,128)(2,1)S(1)}, u32[]{:S(2)}, u32[]{:S(2)}) collective-permute-start(bf16[2,256,256]{2,1,0:T(8,128)(2,1)S(1)} %collective-permute-done.7.refs_1_), channel_id=1, source_target_pairs={{8,0},{16,8},{24,16},{28,24},{20,28},{12,20},{4,12},{0,4},{9,1},{1... | collective-permute-start | bytes 786440 | tf_op jit(solution)/shard_map/ppermute | solution.py:400
  29.2 9.6 %collective-permute-start.5 = (bf16[2,256,256]{2,1,0:T(8,128)(2,1)S(1)}, bf16[2,256,256]{2,1,0:T(8,128)(2,1)S(1)}, u32[]{:S(2)}, u32[]{:S(2)}) collective-permute-start(bf16[2,256,256]{2,1,0:T(8,128)(2,1)S(1)} %collective-permute-done.1.refs_0_), channel_id=1, source_target_pairs={{0,8},{8,16},{16,24},{24,28},{28,20},{20,12},{12,4},{4,0},{1,9},{9... | collective-permute-start | bytes 786440 | tf_op jit(solution)/shard_map/ppermute | solution.py:400
  32.2 10.4 %collective-permute-start.13 = (bf16[2,256,256]{2,1,0:T(8,128)(2,1)S(1)}, bf16[2,256,256]{2,1,0:T(8,128)(2,1)S(1)}, u32[]{:S(2)}, u32[]{:S(2)}) collective-permute-start(bf16[2,256,256]{2,1,0:T(8,128)(2,1)S(1)} %collective-permute-done.8.refs_1_), channel_id=1, source_target_pairs={{8,0},{16,8},{24,16},{28,24},{20,28},{12,20},{4,12},{0,4},{9,1},{1... | collective-permute-start | bytes 786440 | tf_op jit(solution)/shard_map/ppermute | solution.py:400
  33.7 11.2 %collective-permute-start.12 = (bf16[2,256,256]{2,1,0:T(8,128)(2,1)S(1)}, bf16[2,256,256]{2,1,0:T(8,128)(2,1)S(1)}, u32[]{:S(2)}, u32[]{:S(2)}) collective-permute-start(bf16[2,256,256]{2,1,0:T(8,128)(2,1)S(1)} %collective-permute-done.6.refs_0_), channel_id=1, source_target_pairs={{0,8},{8,16},{16,24},{24,28},{28,20},{20,12},{12,4},{4,0},{1,9},{9... | collective-permute-start | bytes 786440 | tf_op jit(solution)/shard_map/ppermute | solution.py:400
  38.9 8.3 %collective-permute-start.11 = (bf16[2,256,256]{2,1,0:T(8,128)(2,1)S(1)}, bf16[2,256,256]{2,1,0:T(8,128)(2,1)S(1)}, u32[]{:S(2)}, u32[]{:S(2)}) collective-permute-start(bf16[2,256,256]{2,1,0:T(8,128)(2,1)S(1)} %collective-permute-done.10.refs_1_), channel_id=1, source_target_pairs={{8,0},{16,8},{24,16},{28,24},{20,28},{12,20},{4,12},{0,4},{9,1},{1... | collective-permute-start | bytes 786440 | tf_op jit(solution)/shard_map/ppermute | solution.py:412
  40.5 7.0 %collective-permute-start.9 = (bf16[2,256,256]{2,1,0:T(8,128)(2,1)S(1)}, bf16[2,256,256]{2,1,0:T(8,128)(2,1)S(1)}, u32[]{:S(2)}, u32[]{:S(2)}) collective-permute-start(bf16[2,256,256]{2,1,0:T(8,128)(2,1)S(1)} %collective-permute-done.5.refs_0_), channel_id=1, source_target_pairs={{0,8},{8,16},{16,24},{24,28},{28,20},{20,12},{12,4},{4,0},{1,9},{9... | collective-permute-start | bytes 786440 | tf_op jit(solution)/shard_map/ppermute | solution.py:411
  49.8 9.3 %collective-permute-start.17 = (bf16[64,2048]{1,0:T(8,128)(2,1)S(1)}, bf16[64,2048]{1,0:T(8,128)(2,1)S(1)}, u32[]{:S(2)}, u32[]{:S(2)}) collective-permute-start(bf16[64,2048]{1,0:T(8,128)(2,1)S(1)} %get-tuple-element.102.refs_1_), channel_id=1, source_target_pairs={{8,0},{16,8},{24,16},{28,24},{20,28},{12,20},{4,12},{0,4},{9,1},{1... | collective-permute-start | bytes 786440 | tf_op jit(solution)/shard_map/ppermute | solution.py:400
  51.4 9.2 %collective-permute-start.14 = (bf16[64,2048]{1,0:T(8,128)(2,1)S(1)}, bf16[64,2048]{1,0:T(8,128)(2,1)S(1)}, u32[]{:S(2)}, u32[]{:S(2)}) collective-permute-start(bf16[64,2048]{1,0:T(8,128)(2,1)S(1)} %get-tuple-element.101.refs_0_), channel_id=1, source_target_pairs={{0,8},{8,16},{16,24},{24,28},{28,20},{20,12},{12,4},{4,0},{1,9},{9... | collective-permute-start | bytes 786440 | tf_op jit(solution)/shard_map/ppermute | solution.py:400
  51.9 12.8 %collective-permute-start.16 = (bf16[64,2048]{1,0:T(8,128)(2,1)S(1)}, bf16[64,2048]{1,0:T(8,128)(2,1)S(1)}, u32[]{:S(2)}, u32[]{:S(2)}) collective-permute-start(bf16[64,2048]{1,0:T(8,128)(2,1)S(1)} %get-tuple-element.101.refs_0_), channel_id=1, source_target_pairs={{8,0},{16,8},{24,16},{28,24},{20,28},{12,20},{4,12},{0,4},{9,1},{1... | collective-permute-start | bytes 786440 | tf_op jit(solution)/shard_map/ppermute | solution.py:400
  53.5 12.8 %collective-permute-start.15 = (bf16[64,2048]{1,0:T(8,128)(2,1)S(1)}, bf16[64,2048]{1,0:T(8,128)(2,1)S(1)}, u32[]{:S(2)}, u32[]{:S(2)}) collective-permute-start(bf16[64,2048]{1,0:T(8,128)(2,1)S(1)} %get-tuple-element.102.refs_1_), channel_id=1, source_target_pairs={{0,8},{8,16},{16,24},{24,28},{28,20},{20,12},{12,4},{4,0},{1,9},{9... | collective-permute-start | bytes 786440 | tf_op jit(solution)/shard_map/ppermute | solution.py:400
  59.1 11.6 %collective-permute-start.21 = (bf16[64,2048]{1,0:T(8,128)(2,1)S(1)}, bf16[64,2048]{1,0:T(8,128)(2,1)S(1)}, u32[]{:S(2)}, u32[]{:S(2)}) collective-permute-start(bf16[64,2048]{1,0:T(8,128)(2,1)S(1)} %collective-permute-done.17.refs_5_), channel_id=1, source_target_pairs={{8,0},{16,8},{24,16},{28,24},{20,28},{12,20},{4,12},{0,4},{9,1},{1... | collective-permute-start | bytes 786440 | tf_op jit(solution)/shard_map/ppermute | solution.py:400
  60.7 11.6 %collective-permute-start.18 = (bf16[64,2048]{1,0:T(8,128)(2,1)S(1)}, bf16[64,2048]{1,0:T(8,128)(2,1)S(1)}, u32[]{:S(2)}, u32[]{:S(2)}) collective-permute-start(bf16[64,2048]{1,0:T(8,128)(2,1)S(1)} %collective-permute-done.14.refs_2_), channel_id=1, source_target_pairs={{0,8},{8,16},{16,24},{24,28},{28,20},{20,12},{12,4},{4,0},{1,9},{9... | collective-permute-start | bytes 786440 | tf_op jit(solution)/shard_map/ppermute | solution.py:400
  64.7 11.2 %collective-permute-start.20 = (bf16[64,2048]{1,0:T(8,128)(2,1)S(1)}, bf16[64,2048]{1,0:T(8,128)(2,1)S(1)}, u32[]{:S(2)}, u32[]{:S(2)}) collective-permute-start(bf16[64,2048]{1,0:T(8,128)(2,1)S(1)} %collective-permute-done.16.refs_4_), channel_id=1, source_target_pairs={{8,0},{16,8},{24,16},{28,24},{20,28},{12,20},{4,12},{0,4},{9,1},{1... | collective-permute-start | bytes 786440 | tf_op jit(solution)/shard_map/ppermute | solution.py:400
  66.3 11.2 %collective-permute-start.19 = (bf16[64,2048]{1,0:T(8,128)(2,1)S(1)}, bf16[64,2048]{1,0:T(8,128)(2,1)S(1)}, u32[]{:S(2)}, u32[]{:S(2)}) collective-permute-start(bf16[64,2048]{1,0:T(8,128)(2,1)S(1)} %collective-permute-done.15.refs_3_), channel_id=1, source_target_pairs={{0,8},{8,16},{16,24},{24,28},{28,20},{20,12},{12,4},{4,0},{1,9},{9... | collective-permute-start | bytes 786440 | tf_op jit(solution)/shard_map/ppermute | solution.py:400
  70.7 10.6 %collective-permute-start.25 = (bf16[64,2048]{1,0:T(8,128)(2,1)S(1)}, bf16[64,2048]{1,0:T(8,128)(2,1)S(1)}, u32[]{:S(2)}, u32[]{:S(2)}) collective-permute-start(bf16[64,2048]{1,0:T(8,128)(2,1)S(1)} %collective-permute-done.21.refs_3_), channel_id=1, source_target_pairs={{8,0},{16,8},{24,16},{28,24},{20,28},{12,20},{4,12},{0,4},{9,1},{1... | collective-permute-start | bytes 786440 | tf_op jit(solution)/shard_map/ppermute | solution.py:400
  72.3 10.2 %collective-permute-start.22 = (bf16[64,2048]{1,0:T(8,128)(2,1)S(1)}, bf16[64,2048]{1,0:T(8,128)(2,1)S(1)}, u32[]{:S(2)}, u32[]{:S(2)}) collective-permute-start(bf16[64,2048]{1,0:T(8,128)(2,1)S(1)} %collective-permute-done.18.refs_0_), channel_id=1, source_target_pairs={{0,8},{8,16},{16,24},{24,28},{28,20},{20,12},{12,4},{4,0},{1,9},{9... | collective-permute-start | bytes 786440 | tf_op jit(solution)/shard_map/ppermute | solution.py:400
  76.0 8.1 %collective-permute-start.24 = (bf16[64,2048]{1,0:T(8,128)(2,1)S(1)}, bf16[64,2048]{1,0:T(8,128)(2,1)S(1)}, u32[]{:S(2)}, u32[]{:S(2)}) collective-permute-start(bf16[64,2048]{1,0:T(8,128)(2,1)S(1)} %collective-permute-done.20.refs_2_), channel_id=1, source_target_pairs={{8,0},{16,8},{24,16},{28,24},{20,28},{12,20},{4,12},{0,4},{9,1},{1... | collective-permute-start | bytes 786440 | tf_op jit(solution)/shard_map/ppermute | solution.py:400
  77.5 7.8 %collective-permute-start.23 = (bf16[64,2048]{1,0:T(8,128)(2,1)S(1)}, bf16[64,2048]{1,0:T(8,128)(2,1)S(1)}, u32[]{:S(2)}, u32[]{:S(2)}) collective-permute-start(bf16[64,2048]{1,0:T(8,128)(2,1)S(1)} %collective-permute-done.19.refs_1_), channel_id=1, source_target_pairs={{0,8},{8,16},{16,24},{24,28},{28,20},{20,12},{12,4},{4,0},{1,9},{9... | collective-permute-start | bytes 786440 | tf_op jit(solution)/shard_map/ppermute | solution.py:400
  78.0 10.2 %collective-permute-start.26 = (bf16[1,64,1024]{2,1,0:T(8,128)(2,1)S(1)}, bf16[1,64,1024]{2,1,0:T(8,128)(2,1)S(1)}, u32[]{:S(2)}, u32[]{:S(2)}) collective-permute-start(bf16[1,64,1024]{2,1,0:T(8,128)(2,1)S(1)} %get-tuple-element.131), channel_id=1, source_target_pairs={{0,1},{1,0},{2,3},{3,2},{4,5},{5,4},{6,7},{7,6},{8,9},{9,8},{10,11... | collective-permute-start | bytes 393224 | tf_op jit(solution)/shard_map/ppermute | solution.py:438
  81.3 9.2 %collective-permute-start.27 = (bf16[1,64,1024]{2,1,0:T(8,128)(2,1)S(1)}, bf16[1,64,1024]{2,1,0:T(8,128)(2,1)S(1)}, u32[]{:S(2)}, u32[]{:S(2)}) collective-permute-start(bf16[1,64,1024]{2,1,0:T(8,128)(2,1)S(1)} %get-tuple-element.130), channel_id=1, source_target_pairs={{0,1},{1,0},{2,3},{3,2},{4,5},{5,4},{6,7},{7,6},{8,9},{9,8},{10,11... | collective-permute-start | bytes 393224 | tf_op jit(solution)/shard_map/ppermute | solution.py:438
  82.6 7.9 %collective-permute-start.28 = (bf16[1,64,1024]{2,1,0:T(8,128)(2,1)S(1)}, bf16[1,64,1024]{2,1,0:T(8,128)(2,1)S(1)}, u32[]{:S(2)}, u32[]{:S(2)}) collective-permute-start(bf16[1,64,1024]{2,1,0:T(8,128)(2,1)S(1)} %get-tuple-element.129), channel_id=1, source_target_pairs={{0,1},{1,0},{2,3},{3,2},{4,5},{5,4},{6,7},{7,6},{8,9},{9,8},{10,11... | collective-permute-start | bytes 393224 | tf_op jit(solution)/shard_map/ppermute | solution.py:438
  88.2 8.8 %collective-permute-start.35 = (bf16[64,2048]{1,0:T(8,128)(2,1)S(1)}, bf16[64,2048]{1,0:T(8,128)(2,1)S(1)}, u32[]{:S(2)}, u32[]{:S(2)}) collective-permute-start(bf16[64,2048]{1,0:T(8,128)(2,1)S(1)} %collective-permute-done.25.refs_3_), channel_id=1, source_target_pairs={{8,0},{16,8},{24,16},{28,24},{20,28},{12,20},{4,12},{0,4},{9,1},{1... | collective-permute-start | bytes 786440 | tf_op jit(solution)/shard_map/ppermute | solution.py:412
  90.4 8.5 %collective-permute-start.34 = (bf16[64,2048]{1,0:T(8,128)(2,1)S(1)}, bf16[64,2048]{1,0:T(8,128)(2,1)S(1)}, u32[]{:S(2)}, u32[]{:S(2)}) collective-permute-start(bf16[64,2048]{1,0:T(8,128)(2,1)S(1)} %collective-permute-done.22.refs_0_), channel_id=1, source_target_pairs={{0,8},{8,16},{16,24},{24,28},{28,20},{20,12},{12,4},{4,0},{1,9},{9... | collective-permute-start | bytes 786440 | tf_op jit(solution)/shard_map/ppermute | solution.py:411
  92.6 15.1 %collective-permute-start.33 = (bf16[3,64,1024]{2,1,0:T(8,128)(2,1)S(1)}, bf16[3,64,1024]{2,1,0:T(8,128)(2,1)S(1)}, u32[]{:S(2)}, u32[]{:S(2)}) collective-permute-start(bf16[3,64,1024]{2,1,0:T(8,128)(2,1)S(1)} %get-tuple-element.118), channel_id=1, source_target_pairs={{0,2},{1,3},{2,0},{3,1},{4,6},{5,7},{6,4},{7,5},{8,10},{9,11},{10,... | collective-permute-start | bytes 1179656 | tf_op jit(solution)/shard_map/ppermute | solution.py:449
  (13 other events, 91.7 us)

commit v4 on v1

--- a/solution.py
+++ b/solution.py
@@ -219,16 +219,8 @@
         for i in range(count):
             low = product[2 * i * half : (2 * i + 1) * half]
             high = product[(2 * i + 1) * half : (2 * i + 2) * half]
-
-            @pl.when(odd == 0)
-            def _():
-                keep_ref[i, :, at] = low
-                send_ref[i, :, at] = high
-
-            @pl.when(odd == 1)
-            def _():
-                keep_ref[i, :, at] = high
-                send_ref[i, :, at] = low
+            keep_ref[i, :, at] = jnp.where(odd == 0, low, high)
+            send_ref[i, :, at] = jnp.where(odd == 0, high, low)
 
 
 def project(arrays, out_weight):

time: 108 us -> 108 us (level)
  waiting for transfers between devices: 36.9 us -> 43.1 us
  Pallas kernels: 34.4 us -> 28.2 us
    pallas_call x4, Pallas kernels: 11.2 us -> 5.01 us  [project(): pl.pallas_call(functools.partial(project_kernel, count), out_shape=[jax.S...]
    ppermute x12, waiting for transfers between devices: 14.8 us -> 20.1 us  [send_both(): lax.ppermute(from_right, 'ctx', left)]
  transfers between devices with their start and end apart: 35 -> 35, of which waited for: 15 -> 16; matrix products, arithmetic and copies ran while one was open for 0% -> 0% of each run, Pallas kernels for 26% -> 20%
where the time goes in v4:
time: 108 us; the launch traced here: 107 us
  waiting for transfers between devices  43.1 us (40%)
  starting transfers between devices  32.1 us (30%)
  Pallas kernels  28.2 us (26%)
  local copies, waits for them, and re-layouts  3.6 us (3%)
    ppermute x12, waiting for transfers between devices, send_both(): lax.ppermute(from_right, 'ctx', left)  20.1 us
    ppermute x12, starting transfers between devices, send_both(): lax.ppermute(from_right, 'ctx', left)  19.7 us
    pallas_call x8, Pallas kernels, flash(): pl.pallas_call(functools.partial(flash_kernel, n, tok, pieces, not state,...  18.6 us
    ppermute x12, waiting for transfers between devices, send_both(): lax.ppermute(from_left, 'ctx', right)  8.58 us
    ppermute x2, waiting for transfers between devices, cross(): got = lax.ppermute(send, 'tp', [(t, t ^ 2) for t in range(n_tp)])  8.47 us
    ppermute x12, starting transfers between devices, send_both(): lax.ppermute(from_left, 'ctx', right)  5.89 us
    pallas_call x4, Pallas kernels, project(): pl.pallas_call(functools.partial(project_kernel, count), out_shape=[jax.S...  5.01 us
    unnamed x12, local copies, waits for them, and re-layouts  3.6 us
  transfers between devices with their start and end apart: 35, of which 16 were waited for; matrix products, arithmetic and copies ran while one was open for 0% of the time, Pallas kernels for 20%

profile of v4, /device:TPU:0, one launch (start us, length us, event | category | flops | bytes accessed | tf_op | source)
XLA Modules:
  0.0 107.1 jit_solution(12325245071675930461)
XLA Ops:
  0.0 2.8 %pick.1 = (bf16[2,256,256]{2,1,0:T(8,128)(2,1)}, bf16[2,256,256]{2,1,0:T(8,128)(2,1)}) custom-call(s32[1,3]{1,0:T(1,128)} %hit_slots.1, bf16[2,16,128,256]{3,2,1,0:T(8,128)(2,1)} %pool_ref.1, bf16[2,128,256]{2,1,0:T(8,128)(2,1)} %suffix_ref.1), custom_call_target="tpu_custom_call" | custom-call | tf_op jit(solution)/shard_map/pick/pallas_call | solution.py:63
  2.8 3.0 %collective-permute-start.3 = (bf16[2,256,256]{2,1,0:T(8,128)(2,1)}, bf16[2,256,256]{2,1,0:T(8,128)(2,1)S(1)}, u32[]{:S(2)}, u32[]{:S(2)}) collective-permute-start(bf16[2,256,256]{2,1,0:T(8,128)(2,1)} %get-tuple-element.69.refs_1_), channel_id=1, source_target_pairs={{8,0},{16,8},{24,16},{28,24},{20,28},{12,20},{4,12},{0,4},{9,1},{1... | collective-permute-start | bytes 786440 | tf_op jit(solution)/shard_map/ppermute | solution.py:386
  6.0 2.0 %collective-permute-start.2 = (bf16[2,256,256]{2,1,0:T(8,128)(2,1)}, bf16[2,256,256]{2,1,0:T(8,128)(2,1)S(1)}, u32[]{:S(2)}, u32[]{:S(2)}) collective-permute-start(bf16[2,256,256]{2,1,0:T(8,128)(2,1)} %get-tuple-element.69.refs_1_), channel_id=1, source_target_pairs={{0,8},{8,16},{16,24},{24,28},{28,20},{20,12},{12,4},{4,0},{1,9},{9... | collective-permute-start | bytes 786440 | tf_op jit(solution)/shard_map/ppermute | solution.py:386
  11.6 2.4 %flash.8 = (bf16[128,2048]{1,0:T(8,128)(2,1)S(1)}, f32[8,2048]{1,0:T(8,128)S(1)}, f32[8,2048]{1,0:T(8,128)S(1)}, f32[128,2048]{1,0:T(8,128)S(1)}) custom-call(s32[8]{0:T(128)S(1)} %copy-done.4, bf16[128,2048]{1,0:T(8,128)(2,1)S(1)} %copy-done.1, bf16[2,256,256]{2,1,0:T(8,128)(2,1)S(1)} %copy-done.2, bf16[2,256,256]{2,1,0:T(8,128)(2,1)S(1)} %copy-done.3), custom_call_target="tpu_custom_call" | custom-call | flops 1000 | bytes 1000 | tf_op jit(solution)/shard_map/flash/pallas_call | solution.py:196
  14.0 2.0 %collective-permute-start.7 = (bf16[2,256,256]{2,1,0:T(8,128)(2,1)S(1)}, bf16[2,256,256]{2,1,0:T(8,128)(2,1)S(1)}, u32[]{:S(2)}, u32[]{:S(2)}) collective-permute-start(bf16[2,256,256]{2,1,0:T(8,128)(2,1)S(1)} %collective-permute-done.3.refs_1_), channel_id=1, source_target_pairs={{8,0},{16,8},{24,16},{28,24},{20,28},{12,20},{4,12},{0,4},{9,1},{1... | collective-permute-start | bytes 786440 | tf_op jit(solution)/shard_map/ppermute | solution.py:386
  16.1 4.8 %collective-permute-done.2.refs_0_ = bf16[2,256,256]{2,1,0:T(8,128)(2,1)S(1)} collective-permute-done((bf16[2,256,256]{2,1,0:T(8,128)(2,1)}, bf16[2,256,256]{2,1,0:T(8,128)(2,1)S(1)}, u32[]{:S(2)}, u32[]{:S(2)}) %collective-permute-start.2) | collective-permute-done | bytes 262176 | tf_op jit(solution)/shard_map/ppermute | solution.py:386
  21.0 1.9 %collective-permute-start.8 = (bf16[2,256,256]{2,1,0:T(8,128)(2,1)S(1)}, bf16[2,256,256]{2,1,0:T(8,128)(2,1)S(1)}, u32[]{:S(2)}, u32[]{:S(2)}) collective-permute-start(bf16[2,256,256]{2,1,0:T(8,128)(2,1)S(1)} %collective-permute-done.4.refs_1_), channel_id=1, source_target_pairs={{8,0},{16,8},{24,16},{28,24},{20,28},{12,20},{4,12},{0,4},{9,1},{1... | collective-permute-start | bytes 786440 | tf_op jit(solution)/shard_map/ppermute | solution.py:386
  22.9 2.4 %flash.9 = (f32[8,2048]{1,0:T(8,128)S(1)}, f32[8,2048]{1,0:T(8,128)S(1)}, f32[128,2048]{1,0:T(8,128)S(1)}) custom-call(s32[8]{0:T(128)S(1)} %copy-done.4, bf16[128,2048]{1,0:T(8,128)(2,1)S(1)} %get-tuple-element.70.q_ref, bf16[2,256,256]{2,1,0:T(8,128)(2,1)S(1)} %collective-permute-done.refs_0_, ...), custom_call_target="tpu_custom_call", output_to_operand_aliasing={{0}: (4, {}), {1}: (5, {}), {2}: (6, {})} | custom-call | flops 1000 | bytes 1000 | tf_op jit(solution)/shard_map/flash/pallas_call | solution.py:196
  25.3 2.3 %flash.10 = (f32[8,2048]{1,0:T(8,128)S(1)}, f32[8,2048]{1,0:T(8,128)S(1)}, f32[128,2048]{1,0:T(8,128)S(1)}) custom-call(s32[8]{0:T(128)S(1)} %copy-done.4, bf16[128,2048]{1,0:T(8,128)(2,1)S(1)} %get-tuple-element.70.q_ref, bf16[2,256,256]{2,1,0:T(8,128)(2,1)S(1)} %collective-permute-done.2.refs_0_, ...), custom_call_target="tpu_custom_call", output_to_operand_aliasing={{0}: (4, {}), {1}: (5, {}), {2}: (6, {})} | custom-call | flops 1000 | bytes 1000 | tf_op jit(solution)/shard_map/flash/pallas_call | solution.py:196
  27.6 1.6 %collective-permute-start.10 = (bf16[2,256,256]{2,1,0:T(8,128)(2,1)S(1)}, bf16[2,256,256]{2,1,0:T(8,128)(2,1)S(1)}, u32[]{:S(2)}, u32[]{:S(2)}) collective-permute-start(bf16[2,256,256]{2,1,0:T(8,128)(2,1)S(1)} %collective-permute-done.7.refs_1_), channel_id=1, source_target_pairs={{8,0},{16,8},{24,16},{28,24},{20,28},{12,20},{4,12},{0,4},{9,1},{1... | collective-permute-start | bytes 786440 | tf_op jit(solution)/shard_map/ppermute | solution.py:386
  29.7 2.4 %collective-permute-done.6.refs_0_ = bf16[2,256,256]{2,1,0:T(8,128)(2,1)S(1)} collective-permute-done((bf16[2,256,256]{2,1,0:T(8,128)(2,1)S(1)}, bf16[2,256,256]{2,1,0:T(8,128)(2,1)S(1)}, u32[]{:S(2)}, u32[]{:S(2)}) %collective-permute-start.6) | collective-permute-done | bytes 262176 | tf_op jit(solution)/shard_map/ppermute | solution.py:386
  32.1 1.6 %collective-permute-start.13 = (bf16[2,256,256]{2,1,0:T(8,128)(2,1)S(1)}, bf16[2,256,256]{2,1,0:T(8,128)(2,1)S(1)}, u32[]{:S(2)}, u32[]{:S(2)}) collective-permute-start(bf16[2,256,256]{2,1,0:T(8,128)(2,1)S(1)} %collective-permute-done.8.refs_1_), channel_id=1, source_target_pairs={{8,0},{16,8},{24,16},{28,24},{20,28},{12,20},{4,12},{0,4},{9,1},{1... | collective-permute-start | bytes 786440 | tf_op jit(solution)/shard_map/ppermute | solution.py:386
  34.2 2.4 %flash.11 = (f32[8,2048]{1,0:T(8,128)S(1)}, f32[8,2048]{1,0:T(8,128)S(1)}, f32[128,2048]{1,0:T(8,128)S(1)}) custom-call(s32[8]{0:T(128)S(1)} %copy-done.5, bf16[128,2048]{1,0:T(8,128)(2,1)S(1)} %get-tuple-element.70.q_ref, bf16[2,256,256]{2,1,0:T(8,128)(2,1)S(1)} %collective-permute-done.1.refs_0_, ...), custom_call_target="tpu_custom_call", output_to_operand_aliasing={{0}: (4, {}), {1}: (5, {}), {2}: (6, {})} | custom-call | flops 1000 | bytes 1000 | tf_op jit(solution)/shard_map/flash/pallas_call | solution.py:196
  36.6 2.3 %flash.12 = (f32[8,2048]{1,0:T(8,128)S(1)}, f32[8,2048]{1,0:T(8,128)S(1)}, f32[128,2048]{1,0:T(8,128)S(1)}) custom-call(s32[8]{0:T(128)S(1)} %copy-done.5, bf16[128,2048]{1,0:T(8,128)(2,1)S(1)} %get-tuple-element.70.q_ref, bf16[2,256,256]{2,1,0:T(8,128)(2,1)S(1)} %collective-permute-done.6.refs_0_, ...), custom_call_target="tpu_custom_call", output_to_operand_aliasing={{0}: (4, {}), {1}: (5, {}), {2}: (6, {})} | custom-call | flops 1000 | bytes 1000 | tf_op jit(solution)/shard_map/flash/pallas_call | solution.py:196
  38.9 1.6 %collective-permute-start.11 = (bf16[2,256,256]{2,1,0:T(8,128)(2,1)S(1)}, bf16[2,256,256]{2,1,0:T(8,128)(2,1)S(1)}, u32[]{:S(2)}, u32[]{:S(2)}) collective-permute-start(bf16[2,256,256]{2,1,0:T(8,128)(2,1)S(1)} %collective-permute-done.10.refs_1_), channel_id=1, source_target_pairs={{8,0},{16,8},{24,16},{28,24},{20,28},{12,20},{4,12},{0,4},{9,1},{1... | collective-permute-start | bytes 786440 | tf_op jit(solution)/shard_map/ppermute | solution.py:398
  42.5 2.4 %flash.13 = (f32[8,2048]{1,0:T(8,128)S(1)}, f32[8,2048]{1,0:T(8,128)S(1)}, f32[128,2048]{1,0:T(8,128)S(1)}) custom-call(s32[8]{0:T(128)S(1)} %copy-done.5, bf16[128,2048]{1,0:T(8,128)(2,1)S(1)} %get-tuple-element.70.q_ref, bf16[2,256,256]{2,1,0:T(8,128)(2,1)S(1)} %collective-permute-done.5.refs_0_, ...), custom_call_target="tpu_custom_call", output_to_operand_aliasing={{0}: (4, {}), {1}: (5, {}), {2}: (6, {})} | custom-call | flops 1000 | bytes 1000 | tf_op jit(solution)/shard_map/flash/pallas_call | solution.py:196
  44.9 2.3 %flash.14 = (f32[8,2048]{1,0:T(8,128)S(1)}, f32[8,2048]{1,0:T(8,128)S(1)}, f32[128,2048]{1,0:T(8,128)S(1)}) custom-call(s32[8]{0:T(128)S(1)} %copy-done.5, bf16[128,2048]{1,0:T(8,128)(2,1)S(1)} %get-tuple-element.70.q_ref, bf16[2,256,256]{2,1,0:T(8,128)(2,1)S(1)} %collective-permute-done.12.refs_0_, ...), custom_call_target="tpu_custom_call", output_to_operand_aliasing={{0}: (4, {}), {1}: (5, {}), {2}: (6, {})} | custom-call | flops 1000 | bytes 1000 | tf_op jit(solution)/shard_map/flash/pallas_call | solution.py:196
  47.5 2.3 %flash.15 = (bf16[64,2048]{1,0:T(8,128)(2,1)S(1)}, bf16[64,2048]{1,0:T(8,128)(2,1)S(1)}) custom-call(s32[8]{0:T(128)S(1)} %copy-done.5, bf16[128,2048]{1,0:T(8,128)(2,1)S(1)} %get-tuple-element.70.q_ref, bf16[2,256,256]{2,1,0:T(8,128)(2,1)S(1)} %collective-permute-done.9.refs_0_, bf16[2,256,256]{2,1,0:T(8,128)(2,1)S(1)} %collective-permute-done.11.refs_1_, ...), custom_call_target="tpu_custom_call" | custom-call | flops 1000 | bytes 1000 | tf_op jit(solution)/shard_map/flash/pallas_call | solution.py:196
  49.8 1.6 %collective-permute-start.17 = (bf16[64,2048]{1,0:T(8,128)(2,1)S(1)}, bf16[64,2048]{1,0:T(8,128)(2,1)S(1)}, u32[]{:S(2)}, u32[]{:S(2)}) collective-permute-start(bf16[64,2048]{1,0:T(8,128)(2,1)S(1)} %get-tuple-element.103.refs_1_), channel_id=1, source_target_pairs={{8,0},{16,8},{24,16},{28,24},{20,28},{12,20},{4,12},{0,4},{9,1},{1... | collective-permute-start | bytes 786440 | tf_op jit(solution)/shard_map/ppermute | solution.py:386
  51.9 1.6 %collective-permute-start.16 = (bf16[64,2048]{1,0:T(8,128)(2,1)S(1)}, bf16[64,2048]{1,0:T(8,128)(2,1)S(1)}, u32[]{:S(2)}, u32[]{:S(2)}) collective-permute-start(bf16[64,2048]{1,0:T(8,128)(2,1)S(1)} %get-tuple-element.102.refs_0_), channel_id=1, source_target_pairs={{8,0},{16,8},{24,16},{28,24},{20,28},{12,20},{4,12},{0,4},{9,1},{1... | collective-permute-start | bytes 786440 | tf_op jit(solution)/shard_map/ppermute | solution.py:386
  53.9 5.2 %collective-permute-done.17.refs_5_ = bf16[64,2048]{1,0:T(8,128)(2,1)S(1)} collective-permute-done((bf16[64,2048]{1,0:T(8,128)(2,1)S(1)}, bf16[64,2048]{1,0:T(8,128)(2,1)S(1)}, u32[]{:S(2)}, u32[]{:S(2)}) %collective-permute-start.17) | collective-permute-done | bytes 262176 | tf_op jit(solution)/shard_map/ppermute | solution.py:386
  59.1 1.6 %collective-permute-start.22 = (bf16[64,2048]{1,0:T(8,128)(2,1)S(1)}, bf16[64,2048]{1,0:T(8,128)(2,1)S(1)}, u32[]{:S(2)}, u32[]{:S(2)}) collective-permute-start(bf16[64,2048]{1,0:T(8,128)(2,1)S(1)} %collective-permute-done.17.refs_5_), channel_id=1, source_target_pairs={{8,0},{16,8},{24,16},{28,24},{20,28},{12,20},{4,12},{0,4},{9,1},{1... | collective-permute-start | bytes 786440 | tf_op jit(solution)/shard_map/ppermute | solution.py:386
  61.1 3.6 %collective-permute-done.16.refs_4_ = bf16[64,2048]{1,0:T(8,128)(2,1)S(1)} collective-permute-done((bf16[64,2048]{1,0:T(8,128)(2,1)S(1)}, bf16[64,2048]{1,0:T(8,128)(2,1)S(1)}, u32[]{:S(2)}, u32[]{:S(2)}) %collective-permute-start.16) | collective-permute-done | bytes 262176 | tf_op jit(solution)/shard_map/ppermute | solution.py:386
  64.7 1.6 %collective-permute-start.21 = (bf16[64,2048]{1,0:T(8,128)(2,1)S(1)}, bf16[64,2048]{1,0:T(8,128)(2,1)S(1)}, u32[]{:S(2)}, u32[]{:S(2)}) collective-permute-start(bf16[64,2048]{1,0:T(8,128)(2,1)S(1)} %collective-permute-done.16.refs_4_), channel_id=1, source_target_pairs={{8,0},{16,8},{24,16},{28,24},{20,28},{12,20},{4,12},{0,4},{9,1},{1... | collective-permute-start | bytes 786440 | tf_op jit(solution)/shard_map/ppermute | solution.py:386
  66.7 1.8 %project.4 = (bf16[3,64,1024]{2,1,0:T(8,128)(2,1)S(1)}, bf16[3,64,1024]{2,1,0:T(8,128)(2,1)S(1)}) custom-call(bf16[64,2048]{1,0:T(8,128)(2,1)S(1)} %get-tuple-element.102.refs_0_, bf16[64,2048]{1,0:T(8,128)(2,1)S(1)} %get-tuple-element.103.refs_1_, bf16[64,2048]{1,0:T(8,128)(2,1)S(1)} %collective-permute-done.14.refs_2_, ...), custom_call_target="tpu_custom_call" | custom-call | flops 1000 | bytes 1000 | tf_op jit(solution)/shard_map/project/pallas_call | solution.py:230
  68.5 1.8 %collective-permute-done.22.refs_3_ = bf16[64,2048]{1,0:T(8,128)(2,1)S(1)} collective-permute-done((bf16[64,2048]{1,0:T(8,128)(2,1)S(1)}, bf16[64,2048]{1,0:T(8,128)(2,1)S(1)}, u32[]{:S(2)}, u32[]{:S(2)}) %collective-permute-start.22) | collective-permute-done | bytes 262176 | tf_op jit(solution)/shard_map/ppermute | solution.py:386
  70.3 1.6 %collective-permute-start.24 = (bf16[64,2048]{1,0:T(8,128)(2,1)S(1)}, bf16[64,2048]{1,0:T(8,128)(2,1)S(1)}, u32[]{:S(2)}, u32[]{:S(2)}) collective-permute-start(bf16[64,2048]{1,0:T(8,128)(2,1)S(1)} %collective-permute-done.22.refs_3_), channel_id=1, source_target_pairs={{8,0},{16,8},{24,16},{28,24},{20,28},{12,20},{4,12},{0,4},{9,1},{1... | collective-permute-start | bytes 786440 | tf_op jit(solution)/shard_map/ppermute | solution.py:386
  72.3 3.6 %collective-permute-done.21.refs_2_ = bf16[64,2048]{1,0:T(8,128)(2,1)S(1)} collective-permute-done((bf16[64,2048]{1,0:T(8,128)(2,1)S(1)}, bf16[64,2048]{1,0:T(8,128)(2,1)S(1)}, u32[]{:S(2)}, u32[]{:S(2)}) %collective-permute-start.21) | collective-permute-done | bytes 262176 | tf_op jit(solution)/shard_map/ppermute | solution.py:386
  79.2 2.0 %collective-permute-done.24.refs_3_ = bf16[64,2048]{1,0:T(8,128)(2,1)S(1)} collective-permute-done((bf16[64,2048]{1,0:T(8,128)(2,1)S(1)}, bf16[64,2048]{1,0:T(8,128)(2,1)S(1)}, u32[]{:S(2)}, u32[]{:S(2)}) %collective-permute-start.24) | collective-permute-done | bytes 262176 | tf_op jit(solution)/shard_map/ppermute | solution.py:386
  81.2 1.6 %collective-permute-start.25 = (bf16[64,2048]{1,0:T(8,128)(2,1)S(1)}, bf16[64,2048]{1,0:T(8,128)(2,1)S(1)}, u32[]{:S(2)}, u32[]{:S(2)}) collective-permute-start(bf16[64,2048]{1,0:T(8,128)(2,1)S(1)} %collective-permute-done.24.refs_3_), channel_id=1, source_target_pairs={{8,0},{16,8},{24,16},{28,24},{20,28},{12,20},{4,12},{0,4},{9,1},{1... | collective-permute-start | bytes 786440 | tf_op jit(solution)/shard_map/ppermute | solution.py:398
  83.3 2.4 %collective-permute-done.27.refs_2_ = bf16[64,2048]{1,0:T(8,128)(2,1)S(1)} collective-permute-done((bf16[64,2048]{1,0:T(8,128)(2,1)S(1)}, bf16[64,2048]{1,0:T(8,128)(2,1)S(1)}, u32[]{:S(2)}, u32[]{:S(2)}) %collective-permute-start.27) | collective-permute-done | bytes 262176 | tf_op jit(solution)/shard_map/ppermute | solution.py:386
  95.9 8.5 %collective-permute-done.33.refs_3_ = bf16[1,64,1024]{2,1,0:T(8,128)(2,1)S(1)} collective-permute-done((bf16[1,64,1024]{2,1,0:T(8,128)(2,1)S(1)}, bf16[1,64,1024]{2,1,0:T(8,128)(2,1)S(1)}, u32[]{:S(2)}, u32[]{:S(2)}) %collective-permute-start.33) | collective-permute-done | bytes 131104 | tf_op jit(solution)/shard_map/ppermute | solution.py:434
  (67 shorter events, 26.2 us)
Async XLA Ops:
  2.8 11.2 %collective-permute-start.3 = (bf16[2,256,256]{2,1,0:T(8,128)(2,1)}, bf16[2,256,256]{2,1,0:T(8,128)(2,1)S(1)}, u32[]{:S(2)}, u32[]{:S(2)}) collective-permute-start(bf16[2,256,256]{2,1,0:T(8,128)(2,1)} %get-tuple-element.69.refs_1_), channel_id=1, source_target_pairs={{8,0},{16,8},{24,16},{28,24},{20,28},{12,20},{4,12},{0,4},{9,1},{1... | collective-permute-start | bytes 786440 | tf_op jit(solution)/shard_map/ppermute | solution.py:386
  5.8 10.1 %collective-permute-start = (bf16[2,256,256]{2,1,0:T(8,128)(2,1)}, bf16[2,256,256]{2,1,0:T(8,128)(2,1)S(1)}, u32[]{:S(2)}, u32[]{:S(2)}) collective-permute-start(bf16[2,256,256]{2,1,0:T(8,128)(2,1)} %get-tuple-element.68.refs_0_), channel_id=1, source_target_pairs={{0,8},{8,16},{16,24},{24,28},{28,20},{20,12},{12,4},{4,0},{1,9},{9... | collective-permute-start | bytes 786440 | tf_op jit(solution)/shard_map/ppermute | solution.py:386
  6.0 14.9 %collective-permute-start.2 = (bf16[2,256,256]{2,1,0:T(8,128)(2,1)}, bf16[2,256,256]{2,1,0:T(8,128)(2,1)S(1)}, u32[]{:S(2)}, u32[]{:S(2)}) collective-permute-start(bf16[2,256,256]{2,1,0:T(8,128)(2,1)} %get-tuple-element.69.refs_1_), channel_id=1, source_target_pairs={{0,8},{8,16},{16,24},{24,28},{28,20},{20,12},{12,4},{4,0},{1,9},{9... | collective-permute-start | bytes 786440 | tf_op jit(solution)/shard_map/ppermute | solution.py:386
  7.9 13.0 %collective-permute-start.4 = (bf16[2,256,256]{2,1,0:T(8,128)(2,1)}, bf16[2,256,256]{2,1,0:T(8,128)(2,1)S(1)}, u32[]{:S(2)}, u32[]{:S(2)}) collective-permute-start(bf16[2,256,256]{2,1,0:T(8,128)(2,1)} %get-tuple-element.68.refs_0_), channel_id=1, source_target_pairs={{8,0},{16,8},{24,16},{28,24},{20,28},{12,20},{4,12},{0,4},{9,1},{1... | collective-permute-start | bytes 786440 | tf_op jit(solution)/shard_map/ppermute | solution.py:386
  14.0 13.6 %collective-permute-start.7 = (bf16[2,256,256]{2,1,0:T(8,128)(2,1)S(1)}, bf16[2,256,256]{2,1,0:T(8,128)(2,1)S(1)}, u32[]{:S(2)}, u32[]{:S(2)}) collective-permute-start(bf16[2,256,256]{2,1,0:T(8,128)(2,1)S(1)} %collective-permute-done.3.refs_1_), channel_id=1, source_target_pairs={{8,0},{16,8},{24,16},{28,24},{20,28},{12,20},{4,12},{0,4},{9,1},{1... | collective-permute-start | bytes 786440 | tf_op jit(solution)/shard_map/ppermute | solution.py:386
  16.0 13.3 %collective-permute-start.1 = (bf16[2,256,256]{2,1,0:T(8,128)(2,1)S(1)}, bf16[2,256,256]{2,1,0:T(8,128)(2,1)S(1)}, u32[]{:S(2)}, u32[]{:S(2)}) collective-permute-start(bf16[2,256,256]{2,1,0:T(8,128)(2,1)S(1)} %collective-permute-done.refs_0_), channel_id=1, source_target_pairs={{0,8},{8,16},{16,24},{24,28},{28,20},{20,12},{12,4},{4,0},{1,9},{9... | collective-permute-start | bytes 786440 | tf_op jit(solution)/shard_map/ppermute | solution.py:386
  20.9 11.2 %collective-permute-start.6 = (bf16[2,256,256]{2,1,0:T(8,128)(2,1)S(1)}, bf16[2,256,256]{2,1,0:T(8,128)(2,1)S(1)}, u32[]{:S(2)}, u32[]{:S(2)}) collective-permute-start(bf16[2,256,256]{2,1,0:T(8,128)(2,1)S(1)} %collective-permute-done.2.refs_0_), channel_id=1, source_target_pairs={{0,8},{8,16},{16,24},{24,28},{28,20},{20,12},{12,4},{4,0},{1,9},{9... | collective-permute-start | bytes 786440 | tf_op jit(solution)/shard_map/ppermute | solution.py:386
  21.0 11.2 %collective-permute-start.8 = (bf16[2,256,256]{2,1,0:T(8,128)(2,1)S(1)}, bf16[2,256,256]{2,1,0:T(8,128)(2,1)S(1)}, u32[]{:S(2)}, u32[]{:S(2)}) collective-permute-start(bf16[2,256,256]{2,1,0:T(8,128)(2,1)S(1)} %collective-permute-done.4.refs_1_), channel_id=1, source_target_pairs={{8,0},{16,8},{24,16},{28,24},{20,28},{12,20},{4,12},{0,4},{9,1},{1... | collective-permute-start | bytes 786440 | tf_op jit(solution)/shard_map/ppermute | solution.py:386
  27.6 11.2 %collective-permute-start.10 = (bf16[2,256,256]{2,1,0:T(8,128)(2,1)S(1)}, bf16[2,256,256]{2,1,0:T(8,128)(2,1)S(1)}, u32[]{:S(2)}, u32[]{:S(2)}) collective-permute-start(bf16[2,256,256]{2,1,0:T(8,128)(2,1)S(1)} %collective-permute-done.7.refs_1_), channel_id=1, source_target_pairs={{8,0},{16,8},{24,16},{28,24},{20,28},{12,20},{4,12},{0,4},{9,1},{1... | collective-permute-start | bytes 786440 | tf_op jit(solution)/shard_map/ppermute | solution.py:386
  29.2 9.6 %collective-permute-start.5 = (bf16[2,256,256]{2,1,0:T(8,128)(2,1)S(1)}, bf16[2,256,256]{2,1,0:T(8,128)(2,1)S(1)}, u32[]{:S(2)}, u32[]{:S(2)}) collective-permute-start(bf16[2,256,256]{2,1,0:T(8,128)(2,1)S(1)} %collective-permute-done.1.refs_0_), channel_id=1, source_target_pairs={{0,8},{8,16},{16,24},{24,28},{28,20},{20,12},{12,4},{4,0},{1,9},{9... | collective-permute-start | bytes 786440 | tf_op jit(solution)/shard_map/ppermute | solution.py:386
  32.1 10.4 %collective-permute-start.13 = (bf16[2,256,256]{2,1,0:T(8,128)(2,1)S(1)}, bf16[2,256,256]{2,1,0:T(8,128)(2,1)S(1)}, u32[]{:S(2)}, u32[]{:S(2)}) collective-permute-start(bf16[2,256,256]{2,1,0:T(8,128)(2,1)S(1)} %collective-permute-done.8.refs_1_), channel_id=1, source_target_pairs={{8,0},{16,8},{24,16},{28,24},{20,28},{12,20},{4,12},{0,4},{9,1},{1... | collective-permute-start | bytes 786440 | tf_op jit(solution)/shard_map/ppermute | solution.py:386
  33.7 11.2 %collective-permute-start.12 = (bf16[2,256,256]{2,1,0:T(8,128)(2,1)S(1)}, bf16[2,256,256]{2,1,0:T(8,128)(2,1)S(1)}, u32[]{:S(2)}, u32[]{:S(2)}) collective-permute-start(bf16[2,256,256]{2,1,0:T(8,128)(2,1)S(1)} %collective-permute-done.6.refs_0_), channel_id=1, source_target_pairs={{0,8},{8,16},{16,24},{24,28},{28,20},{20,12},{12,4},{4,0},{1,9},{9... | collective-permute-start | bytes 786440 | tf_op jit(solution)/shard_map/ppermute | solution.py:386
  38.9 8.3 %collective-permute-start.11 = (bf16[2,256,256]{2,1,0:T(8,128)(2,1)S(1)}, bf16[2,256,256]{2,1,0:T(8,128)(2,1)S(1)}, u32[]{:S(2)}, u32[]{:S(2)}) collective-permute-start(bf16[2,256,256]{2,1,0:T(8,128)(2,1)S(1)} %collective-permute-done.10.refs_1_), channel_id=1, source_target_pairs={{8,0},{16,8},{24,16},{28,24},{20,28},{12,20},{4,12},{0,4},{9,1},{1... | collective-permute-start | bytes 786440 | tf_op jit(solution)/shard_map/ppermute | solution.py:398
  40.5 7.0 %collective-permute-start.9 = (bf16[2,256,256]{2,1,0:T(8,128)(2,1)S(1)}, bf16[2,256,256]{2,1,0:T(8,128)(2,1)S(1)}, u32[]{:S(2)}, u32[]{:S(2)}) collective-permute-start(bf16[2,256,256]{2,1,0:T(8,128)(2,1)S(1)} %collective-permute-done.5.refs_0_), channel_id=1, source_target_pairs={{0,8},{8,16},{16,24},{24,28},{28,20},{20,12},{12,4},{4,0},{1,9},{9... | collective-permute-start | bytes 786440 | tf_op jit(solution)/shard_map/ppermute | solution.py:397
  49.8 9.3 %collective-permute-start.17 = (bf16[64,2048]{1,0:T(8,128)(2,1)S(1)}, bf16[64,2048]{1,0:T(8,128)(2,1)S(1)}, u32[]{:S(2)}, u32[]{:S(2)}) collective-permute-start(bf16[64,2048]{1,0:T(8,128)(2,1)S(1)} %get-tuple-element.103.refs_1_), channel_id=1, source_target_pairs={{8,0},{16,8},{24,16},{28,24},{20,28},{12,20},{4,12},{0,4},{9,1},{1... | collective-permute-start | bytes 786440 | tf_op jit(solution)/shard_map/ppermute | solution.py:386
  51.4 9.2 %collective-permute-start.14 = (bf16[64,2048]{1,0:T(8,128)(2,1)S(1)}, bf16[64,2048]{1,0:T(8,128)(2,1)S(1)}, u32[]{:S(2)}, u32[]{:S(2)}) collective-permute-start(bf16[64,2048]{1,0:T(8,128)(2,1)S(1)} %get-tuple-element.102.refs_0_), channel_id=1, source_target_pairs={{0,8},{8,16},{16,24},{24,28},{28,20},{20,12},{12,4},{4,0},{1,9},{9... | collective-permute-start | bytes 786440 | tf_op jit(solution)/shard_map/ppermute | solution.py:386
  51.9 12.8 %collective-permute-start.16 = (bf16[64,2048]{1,0:T(8,128)(2,1)S(1)}, bf16[64,2048]{1,0:T(8,128)(2,1)S(1)}, u32[]{:S(2)}, u32[]{:S(2)}) collective-permute-start(bf16[64,2048]{1,0:T(8,128)(2,1)S(1)} %get-tuple-element.102.refs_0_), channel_id=1, source_target_pairs={{8,0},{16,8},{24,16},{28,24},{20,28},{12,20},{4,12},{0,4},{9,1},{1... | collective-permute-start | bytes 786440 | tf_op jit(solution)/shard_map/ppermute | solution.py:386
  53.4 12.8 %collective-permute-start.15 = (bf16[64,2048]{1,0:T(8,128)(2,1)S(1)}, bf16[64,2048]{1,0:T(8,128)(2,1)S(1)}, u32[]{:S(2)}, u32[]{:S(2)}) collective-permute-start(bf16[64,2048]{1,0:T(8,128)(2,1)S(1)} %get-tuple-element.103.refs_1_), channel_id=1, source_target_pairs={{0,8},{8,16},{16,24},{24,28},{28,20},{20,12},{12,4},{4,0},{1,9},{9... | collective-permute-start | bytes 786440 | tf_op jit(solution)/shard_map/ppermute | solution.py:386
  59.1 11.2 %collective-permute-start.22 = (bf16[64,2048]{1,0:T(8,128)(2,1)S(1)}, bf16[64,2048]{1,0:T(8,128)(2,1)S(1)}, u32[]{:S(2)}, u32[]{:S(2)}) collective-permute-start(bf16[64,2048]{1,0:T(8,128)(2,1)S(1)} %collective-permute-done.17.refs_5_), channel_id=1, source_target_pairs={{8,0},{16,8},{24,16},{28,24},{20,28},{12,20},{4,12},{0,4},{9,1},{1... | collective-permute-start | bytes 786440 | tf_op jit(solution)/shard_map/ppermute | solution.py:386
  60.7 11.2 %collective-permute-start.18 = (bf16[64,2048]{1,0:T(8,128)(2,1)S(1)}, bf16[64,2048]{1,0:T(8,128)(2,1)S(1)}, u32[]{:S(2)}, u32[]{:S(2)}) collective-permute-start(bf16[64,2048]{1,0:T(8,128)(2,1)S(1)} %collective-permute-done.14.refs_2_), channel_id=1, source_target_pairs={{0,8},{8,16},{16,24},{24,28},{28,20},{20,12},{12,4},{4,0},{1,9},{9... | collective-permute-start | bytes 786440 | tf_op jit(solution)/shard_map/ppermute | solution.py:386
  64.7 11.2 %collective-permute-start.21 = (bf16[64,2048]{1,0:T(8,128)(2,1)S(1)}, bf16[64,2048]{1,0:T(8,128)(2,1)S(1)}, u32[]{:S(2)}, u32[]{:S(2)}) collective-permute-start(bf16[64,2048]{1,0:T(8,128)(2,1)S(1)} %collective-permute-done.16.refs_4_), channel_id=1, source_target_pairs={{8,0},{16,8},{24,16},{28,24},{20,28},{12,20},{4,12},{0,4},{9,1},{1... | collective-permute-start | bytes 786440 | tf_op jit(solution)/shard_map/ppermute | solution.py:386
  66.3 11.2 %collective-permute-start.20 = (bf16[64,2048]{1,0:T(8,128)(2,1)S(1)}, bf16[64,2048]{1,0:T(8,128)(2,1)S(1)}, u32[]{:S(2)}, u32[]{:S(2)}) collective-permute-start(bf16[64,2048]{1,0:T(8,128)(2,1)S(1)} %collective-permute-done.15.refs_3_), channel_id=1, source_target_pairs={{0,8},{8,16},{16,24},{24,28},{28,20},{20,12},{12,4},{4,0},{1,9},{9... | collective-permute-start | bytes 786440 | tf_op jit(solution)/shard_map/ppermute | solution.py:386
  70.3 10.9 %collective-permute-start.24 = (bf16[64,2048]{1,0:T(8,128)(2,1)S(1)}, bf16[64,2048]{1,0:T(8,128)(2,1)S(1)}, u32[]{:S(2)}, u32[]{:S(2)}) collective-permute-start(bf16[64,2048]{1,0:T(8,128)(2,1)S(1)} %collective-permute-done.22.refs_3_), channel_id=1, source_target_pairs={{8,0},{16,8},{24,16},{28,24},{20,28},{12,20},{4,12},{0,4},{9,1},{1... | collective-permute-start | bytes 786440 | tf_op jit(solution)/shard_map/ppermute | solution.py:386
  71.9 10.9 %collective-permute-start.19 = (bf16[64,2048]{1,0:T(8,128)(2,1)S(1)}, bf16[64,2048]{1,0:T(8,128)(2,1)S(1)}, u32[]{:S(2)}, u32[]{:S(2)}) collective-permute-start(bf16[64,2048]{1,0:T(8,128)(2,1)S(1)} %collective-permute-done.18.refs_0_), channel_id=1, source_target_pairs={{0,8},{8,16},{16,24},{24,28},{28,20},{20,12},{12,4},{4,0},{1,9},{9... | collective-permute-start | bytes 786440 | tf_op jit(solution)/shard_map/ppermute | solution.py:386
  75.9 9.7 %collective-permute-start.27 = (bf16[64,2048]{1,0:T(8,128)(2,1)S(1)}, bf16[64,2048]{1,0:T(8,128)(2,1)S(1)}, u32[]{:S(2)}, u32[]{:S(2)}) collective-permute-start(bf16[64,2048]{1,0:T(8,128)(2,1)S(1)} %collective-permute-done.21.refs_2_), channel_id=1, source_target_pairs={{8,0},{16,8},{24,16},{28,24},{20,28},{12,20},{4,12},{0,4},{9,1},{1... | collective-permute-start | bytes 786440 | tf_op jit(solution)/shard_map/ppermute | solution.py:386
  77.5 9.4 %collective-permute-start.26 = (bf16[64,2048]{1,0:T(8,128)(2,1)S(1)}, bf16[64,2048]{1,0:T(8,128)(2,1)S(1)}, u32[]{:S(2)}, u32[]{:S(2)}) collective-permute-start(bf16[64,2048]{1,0:T(8,128)(2,1)S(1)} %collective-permute-done.20.refs_1_), channel_id=1, source_target_pairs={{0,8},{8,16},{16,24},{24,28},{28,20},{20,12},{12,4},{4,0},{1,9},{9... | collective-permute-start | bytes 786440 | tf_op jit(solution)/shard_map/ppermute | solution.py:386
  78.0 13.0 %collective-permute-start.28 = (bf16[3,64,1024]{2,1,0:T(8,128)(2,1)S(1)}, bf16[3,64,1024]{2,1,0:T(8,128)(2,1)S(1)}, u32[]{:S(2)}, u32[]{:S(2)}) collective-permute-start(bf16[3,64,1024]{2,1,0:T(8,128)(2,1)S(1)} %get-tuple-element.106), channel_id=1, source_target_pairs={{0,1},{1,0},{2,3},{3,2},{4,5},{5,4},{6,7},{7,6},{8,9},{9,8},{10,11... | collective-permute-start | bytes 1179656 | tf_op jit(solution)/shard_map/ppermute | solution.py:423
  81.2 8.4 %collective-permute-start.25 = (bf16[64,2048]{1,0:T(8,128)(2,1)S(1)}, bf16[64,2048]{1,0:T(8,128)(2,1)S(1)}, u32[]{:S(2)}, u32[]{:S(2)}) collective-permute-start(bf16[64,2048]{1,0:T(8,128)(2,1)S(1)} %collective-permute-done.24.refs_3_), channel_id=1, source_target_pairs={{8,0},{16,8},{24,16},{28,24},{20,28},{12,20},{4,12},{0,4},{9,1},{1... | collective-permute-start | bytes 786440 | tf_op jit(solution)/shard_map/ppermute | solution.py:398
  82.8 8.1 %collective-permute-start.23 = (bf16[64,2048]{1,0:T(8,128)(2,1)S(1)}, bf16[64,2048]{1,0:T(8,128)(2,1)S(1)}, u32[]{:S(2)}, u32[]{:S(2)}) collective-permute-start(bf16[64,2048]{1,0:T(8,128)(2,1)S(1)} %collective-permute-done.19.refs_0_), channel_id=1, source_target_pairs={{0,8},{8,16},{16,24},{24,28},{28,20},{20,12},{12,4},{4,0},{1,9},{9... | collective-permute-start | bytes 786440 | tf_op jit(solution)/shard_map/ppermute | solution.py:397
  85.6 5.3 %collective-permute-start.29 = (bf16[2,64,1024]{2,1,0:T(8,128)(2,1)S(1)}, bf16[2,64,1024]{2,1,0:T(8,128)(2,1)S(1)}, u32[]{:S(2)}, u32[]{:S(2)}) collective-permute-start(bf16[2,64,1024]{2,1,0:T(8,128)(2,1)S(1)} %get-tuple-element.111), channel_id=1, source_target_pairs={{0,1},{1,0},{2,3},{3,2},{4,5},{5,4},{6,7},{7,6},{8,9},{9,8},{10,11... | collective-permute-start | bytes 786440 | tf_op jit(solution)/shard_map/ppermute | solution.py:423
  91.5 12.9 %collective-permute-start.31 = (bf16[3,64,1024]{2,1,0:T(8,128)(2,1)S(1)}, bf16[3,64,1024]{2,1,0:T(8,128)(2,1)S(1)}, u32[]{:S(2)}, u32[]{:S(2)}) collective-permute-start(bf16[3,64,1024]{2,1,0:T(8,128)(2,1)S(1)} %get-tuple-element.122), channel_id=1, source_target_pairs={{0,2},{1,3},{2,0},{3,1},{4,6},{5,7},{6,4},{7,5},{8,10},{9,11},{10,... | collective-permute-start | bytes 1179656 | tf_op jit(solution)/shard_map/ppermute | solution.py:434
  95.3 9.1 %collective-permute-start.33 = (bf16[1,64,1024]{2,1,0:T(8,128)(2,1)S(1)}, bf16[1,64,1024]{2,1,0:T(8,128)(2,1)S(1)}, u32[]{:S(2)}, u32[]{:S(2)}) collective-permute-start(bf16[1,64,1024]{2,1,0:T(8,128)(2,1)S(1)} %get-tuple-element.128), channel_id=1, source_target_pairs={{0,2},{1,3},{2,0},{3,1},{4,6},{5,7},{6,4},{7,5},{8,10},{9,11},{10,... | collective-permute-start | bytes 393224 | tf_op jit(solution)/shard_map/ppermute | solution.py:434
  (9 other events, 73.7 us)

commit v5 on v4

--- a/solution.py
+++ b/solution.py
@@ -256,34 +256,33 @@
     return a.astype(jnp.float32) + b.astype(jnp.float32)
 
 
-def sort_kernel(n, n_tp, steps, *refs):
-    *refs, stay_ref, send_ref, last_stay_ref, last_send_ref = refs
+def sort_kernel(n, n_tp, steps, side, *refs):
+    *refs, out, last = refs
     count = len(refs) // 2
     places = [(a, b, i) for a, b in zip(refs[:count], refs[count:]) for i in range(a.shape[0])]
-    full = stay_ref.shape[0]
+    full = out.shape[0]
     for (a, b, i), (_, away, rank) in zip(places, sides(n, n_tp, steps)):
         total = added(a[i], b[i]).astype(jnp.bfloat16)
-        for side, out, last in ((0, stay_ref, last_stay_ref), (1, send_ref, last_send_ref)):
-
-            @pl.when((away == side) & (rank < full))
-            def _():
-                out[rank] = total
-
-            @pl.when((away == side) & (rank == full))
-            def _():
-                last[0] = total
-
-
-def sort(n, n_tp, steps, sums):
+
+        @pl.when((away == side) & (rank < full))
+        def _():
+            out[rank] = total
+
+        @pl.when((away == side) & (rank == full))
+        def _():
+            last[0] = total
+
+
+def sort(n, n_tp, steps, side, sums):
     keeps, gots = zip(*sums)
     half, wide = keeps[0].shape[1:]
     many = jax.ShapeDtypeStruct((n // 2 - 1, half, wide), jnp.bfloat16)
     one = jax.ShapeDtypeStruct((1, half, wide), jnp.bfloat16)
     return pl.pallas_call(
-        functools.partial(sort_kernel, n, n_tp, steps),
-        out_shape=[many, many, one, one],
+        functools.partial(sort_kernel, n, n_tp, steps, side),
+        out_shape=[many, one],
         in_specs=[vmem] * (2 * len(sums)),
-        out_specs=[vmem] * 4,
+        out_specs=[vmem] * 2,
         compiler_params=params,
         cost_estimate=light,
         name="sort",
@@ -342,17 +341,18 @@
     )(*arrays)
 
 
-def join_kernel(mine_ref, got_ref, out_ref):
+def join_kernel(mine_ref, got_ref, out_ref, sems):
     odd = lax.axis_index("tp") % 2
     count, half, _ = mine_ref.shape
-    for low in range(2):
-        first, second = (mine_ref, got_ref) if low == 0 else (got_ref, mine_ref)
-
-        @pl.when(odd == low)
-        def _():
-            for i in range(count):
-                out_ref[2 * i * half : (2 * i + 1) * half] = first[i]
-                out_ref[(2 * i + 1) * half : (2 * i + 2) * half] = second[i]
+    copies = []
+    for k, (ref, place) in enumerate(((mine_ref, odd), (got_ref, 1 - odd))):
+        for i in range(count):
+            at = pl.ds(pl.multiple_of((2 * i + place) * half, half), half)
+            copies.append(pltpu.make_async_copy(ref.at[i], out_ref.at[at, :], sems.at[k, i]))
+    for copy in copies:
+        copy.start()
+    for copy in copies:
+        copy.wait()
 
 
 def join(mine, got):
@@ -361,7 +361,8 @@
         join_kernel,
         out_shape=jax.ShapeDtypeStruct((2 * count * half, wide), jnp.bfloat16),
         in_specs=[vmem, vmem],
-        out_specs=vmem,
+        out_specs=hbm,
+        scratch_shapes=[pltpu.SemaphoreType.DMA((2, count))],
         compiler_params=params,
         name="join",
     )(mine, got)
@@ -442,7 +443,9 @@
     far, _ = ring(attention, spread, None)
     steps = [0] + [s * d for d in range(1, half) for s in (-1, 1)] + [half]
     sums[0] = (after(sums[0][0], far), sums[0][1])
-    stay, send, last_stay, last_send = sort(n, n_tp, steps[:-1], sums)
+    send, last_send = sort(n, n_tp, steps[:-1], 1, sums)
+    kept = [(after(sums[0][0], send), sums[0][1])] + sums[1:]
+    stay, last_stay = sort(n, n_tp, steps[:-1], 0, kept)
     stay, got = cross(stay, send)
     reduce(far)
     last_stay, last_send = place_last(n, n_tp, *sums[-1], last_stay, last_send)

time: 108 us -> 108 us (level)
  no operation moved by 1% of the time
where the time goes in v5:
time: 108 us; the launch traced here: 107 us
  waiting for transfers between devices  42.6 us (39%)
  starting transfers between devices  32.1 us (30%)
  Pallas kernels  28.5 us (26%)
  local copies, waits for them, and re-layouts  3.6 us (3%)
    ppermute x12, waiting for transfers between devices, send_both(): lax.ppermute(from_right, 'ctx', left)  20.1 us
    ppermute x12, starting transfers between devices, send_both(): lax.ppermute(from_right, 'ctx', left)  19.7 us
    pallas_call x8, Pallas kernels, flash(): pl.pallas_call(functools.partial(flash_kernel, n, tok, pieces, not state,...  18.6 us
    ppermute x12, waiting for transfers between devices, send_both(): lax.ppermute(from_left, 'ctx', right)  8.58 us
    ppermute x2, waiting for transfers between devices, cross(): got = lax.ppermute(send, 'tp', [(t, t ^ 2) for t in range(n_tp)])  8.47 us
    ppermute x12, starting transfers between devices, send_both(): lax.ppermute(from_left, 'ctx', right)  5.89 us
    pallas_call x4, Pallas kernels, project(): pl.pallas_call(functools.partial(project_kernel, count), out_shape=[jax.S...  5.01 us
    unnamed x12, local copies, waits for them, and re-layouts  3.6 us
  transfers between devices with their start and end apart: 35, of which 16 were waited for; matrix products, arithmetic and copies ran while one was open for 0% of the time, Pallas kernels for 20%

profile of v5, /device:TPU:0, one launch (start us, length us, event | category | flops | bytes accessed | tf_op | source)
XLA Modules:
  0.0 107.2 jit_solution(8985552492066934187)
XLA Ops:
  0.0 2.8 %pick.1 = (bf16[2,256,256]{2,1,0:T(8,128)(2,1)}, bf16[2,256,256]{2,1,0:T(8,128)(2,1)}) custom-call(s32[1,3]{1,0:T(1,128)} %hit_slots.1, bf16[2,16,128,256]{3,2,1,0:T(8,128)(2,1)} %pool_ref.1, bf16[2,128,256]{2,1,0:T(8,128)(2,1)} %suffix_ref.1), custom_call_target="tpu_custom_call" | custom-call | tf_op jit(solution)/shard_map/pick/pallas_call | solution.py:63
  2.8 3.0 %collective-permute-start.3 = (bf16[2,256,256]{2,1,0:T(8,128)(2,1)}, bf16[2,256,256]{2,1,0:T(8,128)(2,1)S(1)}, u32[]{:S(2)}, u32[]{:S(2)}) collective-permute-start(bf16[2,256,256]{2,1,0:T(8,128)(2,1)} %get-tuple-element.70.refs_1_), channel_id=1, source_target_pairs={{8,0},{16,8},{24,16},{28,24},{20,28},{12,20},{4,12},{0,4},{9,1},{1... | collective-permute-start | bytes 786440 | tf_op jit(solution)/shard_map/ppermute | solution.py:387
  5.9 2.0 %collective-permute-start.2 = (bf16[2,256,256]{2,1,0:T(8,128)(2,1)}, bf16[2,256,256]{2,1,0:T(8,128)(2,1)S(1)}, u32[]{:S(2)}, u32[]{:S(2)}) collective-permute-start(bf16[2,256,256]{2,1,0:T(8,128)(2,1)} %get-tuple-element.70.refs_1_), channel_id=1, source_target_pairs={{0,8},{8,16},{16,24},{24,28},{28,20},{20,12},{12,4},{4,0},{1,9},{9... | collective-permute-start | bytes 786440 | tf_op jit(solution)/shard_map/ppermute | solution.py:387
  11.6 2.4 %flash.8 = (bf16[128,2048]{1,0:T(8,128)(2,1)S(1)}, f32[8,2048]{1,0:T(8,128)S(1)}, f32[8,2048]{1,0:T(8,128)S(1)}, f32[128,2048]{1,0:T(8,128)S(1)}) custom-call(s32[8]{0:T(128)S(1)} %copy-done.4, bf16[128,2048]{1,0:T(8,128)(2,1)S(1)} %copy-done.1, bf16[2,256,256]{2,1,0:T(8,128)(2,1)S(1)} %copy-done.2, bf16[2,256,256]{2,1,0:T(8,128)(2,1)S(1)} %copy-done.3), custom_call_target="tpu_custom_call" | custom-call | flops 1000 | bytes 1000 | tf_op jit(solution)/shard_map/flash/pallas_call | solution.py:196
  14.0 2.0 %collective-permute-start.7 = (bf16[2,256,256]{2,1,0:T(8,128)(2,1)S(1)}, bf16[2,256,256]{2,1,0:T(8,128)(2,1)S(1)}, u32[]{:S(2)}, u32[]{:S(2)}) collective-permute-start(bf16[2,256,256]{2,1,0:T(8,128)(2,1)S(1)} %collective-permute-done.3.refs_1_), channel_id=1, source_target_pairs={{8,0},{16,8},{24,16},{28,24},{20,28},{12,20},{4,12},{0,4},{9,1},{1... | collective-permute-start | bytes 786440 | tf_op jit(solution)/shard_map/ppermute | solution.py:387
  16.1 4.8 %collective-permute-done.2.refs_0_ = bf16[2,256,256]{2,1,0:T(8,128)(2,1)S(1)} collective-permute-done((bf16[2,256,256]{2,1,0:T(8,128)(2,1)}, bf16[2,256,256]{2,1,0:T(8,128)(2,1)S(1)}, u32[]{:S(2)}, u32[]{:S(2)}) %collective-permute-start.2) | collective-permute-done | bytes 262176 | tf_op jit(solution)/shard_map/ppermute | solution.py:387
  21.0 1.9 %collective-permute-start.8 = (bf16[2,256,256]{2,1,0:T(8,128)(2,1)S(1)}, bf16[2,256,256]{2,1,0:T(8,128)(2,1)S(1)}, u32[]{:S(2)}, u32[]{:S(2)}) collective-permute-start(bf16[2,256,256]{2,1,0:T(8,128)(2,1)S(1)} %collective-permute-done.4.refs_1_), channel_id=1, source_target_pairs={{8,0},{16,8},{24,16},{28,24},{20,28},{12,20},{4,12},{0,4},{9,1},{1... | collective-permute-start | bytes 786440 | tf_op jit(solution)/shard_map/ppermute | solution.py:387
  22.9 2.4 %flash.9 = (f32[8,2048]{1,0:T(8,128)S(1)}, f32[8,2048]{1,0:T(8,128)S(1)}, f32[128,2048]{1,0:T(8,128)S(1)}) custom-call(s32[8]{0:T(128)S(1)} %copy-done.4, bf16[128,2048]{1,0:T(8,128)(2,1)S(1)} %get-tuple-element.71.q_ref, bf16[2,256,256]{2,1,0:T(8,128)(2,1)S(1)} %collective-permute-done.refs_0_, ...), custom_call_target="tpu_custom_call", output_to_operand_aliasing={{0}: (4, {}), {1}: (5, {}), {2}: (6, {})} | custom-call | flops 1000 | bytes 1000 | tf_op jit(solution)/shard_map/flash/pallas_call | solution.py:196
  25.3 2.3 %flash.10 = (f32[8,2048]{1,0:T(8,128)S(1)}, f32[8,2048]{1,0:T(8,128)S(1)}, f32[128,2048]{1,0:T(8,128)S(1)}) custom-call(s32[8]{0:T(128)S(1)} %copy-done.4, bf16[128,2048]{1,0:T(8,128)(2,1)S(1)} %get-tuple-element.71.q_ref, bf16[2,256,256]{2,1,0:T(8,128)(2,1)S(1)} %collective-permute-done.2.refs_0_, ...), custom_call_target="tpu_custom_call", output_to_operand_aliasing={{0}: (4, {}), {1}: (5, {}), {2}: (6, {})} | custom-call | flops 1000 | bytes 1000 | tf_op jit(solution)/shard_map/flash/pallas_call | solution.py:196
  27.6 1.6 %collective-permute-start.10 = (bf16[2,256,256]{2,1,0:T(8,128)(2,1)S(1)}, bf16[2,256,256]{2,1,0:T(8,128)(2,1)S(1)}, u32[]{:S(2)}, u32[]{:S(2)}) collective-permute-start(bf16[2,256,256]{2,1,0:T(8,128)(2,1)S(1)} %collective-permute-done.7.refs_1_), channel_id=1, source_target_pairs={{8,0},{16,8},{24,16},{28,24},{20,28},{12,20},{4,12},{0,4},{9,1},{1... | collective-permute-start | bytes 786440 | tf_op jit(solution)/shard_map/ppermute | solution.py:387
  29.7 2.4 %collective-permute-done.6.refs_0_ = bf16[2,256,256]{2,1,0:T(8,128)(2,1)S(1)} collective-permute-done((bf16[2,256,256]{2,1,0:T(8,128)(2,1)S(1)}, bf16[2,256,256]{2,1,0:T(8,128)(2,1)S(1)}, u32[]{:S(2)}, u32[]{:S(2)}) %collective-permute-start.6) | collective-permute-done | bytes 262176 | tf_op jit(solution)/shard_map/ppermute | solution.py:387
  32.1 1.6 %collective-permute-start.13 = (bf16[2,256,256]{2,1,0:T(8,128)(2,1)S(1)}, bf16[2,256,256]{2,1,0:T(8,128)(2,1)S(1)}, u32[]{:S(2)}, u32[]{:S(2)}) collective-permute-start(bf16[2,256,256]{2,1,0:T(8,128)(2,1)S(1)} %collective-permute-done.8.refs_1_), channel_id=1, source_target_pairs={{8,0},{16,8},{24,16},{28,24},{20,28},{12,20},{4,12},{0,4},{9,1},{1... | collective-permute-start | bytes 786440 | tf_op jit(solution)/shard_map/ppermute | solution.py:387
  34.2 2.4 %flash.11 = (f32[8,2048]{1,0:T(8,128)S(1)}, f32[8,2048]{1,0:T(8,128)S(1)}, f32[128,2048]{1,0:T(8,128)S(1)}) custom-call(s32[8]{0:T(128)S(1)} %copy-done.5, bf16[128,2048]{1,0:T(8,128)(2,1)S(1)} %get-tuple-element.71.q_ref, bf16[2,256,256]{2,1,0:T(8,128)(2,1)S(1)} %collective-permute-done.1.refs_0_, ...), custom_call_target="tpu_custom_call", output_to_operand_aliasing={{0}: (4, {}), {1}: (5, {}), {2}: (6, {})} | custom-call | flops 1000 | bytes 1000 | tf_op jit(solution)/shard_map/flash/pallas_call | solution.py:196
  36.5 2.3 %flash.12 = (f32[8,2048]{1,0:T(8,128)S(1)}, f32[8,2048]{1,0:T(8,128)S(1)}, f32[128,2048]{1,0:T(8,128)S(1)}) custom-call(s32[8]{0:T(128)S(1)} %copy-done.5, bf16[128,2048]{1,0:T(8,128)(2,1)S(1)} %get-tuple-element.71.q_ref, bf16[2,256,256]{2,1,0:T(8,128)(2,1)S(1)} %collective-permute-done.6.refs_0_, ...), custom_call_target="tpu_custom_call", output_to_operand_aliasing={{0}: (4, {}), {1}: (5, {}), {2}: (6, {})} | custom-call | flops 1000 | bytes 1000 | tf_op jit(solution)/shard_map/flash/pallas_call | solution.py:196
  38.8 1.6 %collective-permute-start.11 = (bf16[2,256,256]{2,1,0:T(8,128)(2,1)S(1)}, bf16[2,256,256]{2,1,0:T(8,128)(2,1)S(1)}, u32[]{:S(2)}, u32[]{:S(2)}) collective-permute-start(bf16[2,256,256]{2,1,0:T(8,128)(2,1)S(1)} %collective-permute-done.10.refs_1_), channel_id=1, source_target_pairs={{8,0},{16,8},{24,16},{28,24},{20,28},{12,20},{4,12},{0,4},{9,1},{1... | collective-permute-start | bytes 786440 | tf_op jit(solution)/shard_map/ppermute | solution.py:399
  40.9 1.6 %collective-permute-done.13.refs_1_ = bf16[2,256,256]{2,1,0:T(8,128)(2,1)S(1)} collective-permute-done((bf16[2,256,256]{2,1,0:T(8,128)(2,1)S(1)}, bf16[2,256,256]{2,1,0:T(8,128)(2,1)S(1)}, u32[]{:S(2)}, u32[]{:S(2)}) %collective-permute-start.13) | collective-permute-done | bytes 262176 | tf_op jit(solution)/shard_map/ppermute | solution.py:387
  42.5 2.4 %flash.13 = (f32[8,2048]{1,0:T(8,128)S(1)}, f32[8,2048]{1,0:T(8,128)S(1)}, f32[128,2048]{1,0:T(8,128)S(1)}) custom-call(s32[8]{0:T(128)S(1)} %copy-done.5, bf16[128,2048]{1,0:T(8,128)(2,1)S(1)} %get-tuple-element.71.q_ref, bf16[2,256,256]{2,1,0:T(8,128)(2,1)S(1)} %collective-permute-done.5.refs_0_, ...), custom_call_target="tpu_custom_call", output_to_operand_aliasing={{0}: (4, {}), {1}: (5, {}), {2}: (6, {})} | custom-call | flops 1000 | bytes 1000 | tf_op jit(solution)/shard_map/flash/pallas_call | solution.py:196
  44.9 2.3 %flash.14 = (f32[8,2048]{1,0:T(8,128)S(1)}, f32[8,2048]{1,0:T(8,128)S(1)}, f32[128,2048]{1,0:T(8,128)S(1)}) custom-call(s32[8]{0:T(128)S(1)} %copy-done.5, bf16[128,2048]{1,0:T(8,128)(2,1)S(1)} %get-tuple-element.71.q_ref, bf16[2,256,256]{2,1,0:T(8,128)(2,1)S(1)} %collective-permute-done.12.refs_0_, ...), custom_call_target="tpu_custom_call", output_to_operand_aliasing={{0}: (4, {}), {1}: (5, {}), {2}: (6, {})} | custom-call | flops 1000 | bytes 1000 | tf_op jit(solution)/shard_map/flash/pallas_call | solution.py:196
  47.5 2.3 %flash.15 = (bf16[64,2048]{1,0:T(8,128)(2,1)S(1)}, bf16[64,2048]{1,0:T(8,128)(2,1)S(1)}) custom-call(s32[8]{0:T(128)S(1)} %copy-done.5, bf16[128,2048]{1,0:T(8,128)(2,1)S(1)} %get-tuple-element.71.q_ref, bf16[2,256,256]{2,1,0:T(8,128)(2,1)S(1)} %collective-permute-done.9.refs_0_, bf16[2,256,256]{2,1,0:T(8,128)(2,1)S(1)} %collective-permute-done.11.refs_1_, ...), custom_call_target="tpu_custom_call" | custom-call | flops 1000 | bytes 1000 | tf_op jit(solution)/shard_map/flash/pallas_call | solution.py:196
  49.8 1.6 %collective-permute-start.17 = (bf16[64,2048]{1,0:T(8,128)(2,1)S(1)}, bf16[64,2048]{1,0:T(8,128)(2,1)S(1)}, u32[]{:S(2)}, u32[]{:S(2)}) collective-permute-start(bf16[64,2048]{1,0:T(8,128)(2,1)S(1)} %get-tuple-element.104.refs_1_), channel_id=1, source_target_pairs={{8,0},{16,8},{24,16},{28,24},{20,28},{12,20},{4,12},{0,4},{9,1},{1... | collective-permute-start | bytes 786440 | tf_op jit(solution)/shard_map/ppermute | solution.py:387
  51.9 1.6 %collective-permute-start.16 = (bf16[64,2048]{1,0:T(8,128)(2,1)S(1)}, bf16[64,2048]{1,0:T(8,128)(2,1)S(1)}, u32[]{:S(2)}, u32[]{:S(2)}) collective-permute-start(bf16[64,2048]{1,0:T(8,128)(2,1)S(1)} %get-tuple-element.103.refs_0_), channel_id=1, source_target_pairs={{8,0},{16,8},{24,16},{28,24},{20,28},{12,20},{4,12},{0,4},{9,1},{1... | collective-permute-start | bytes 786440 | tf_op jit(solution)/shard_map/ppermute | solution.py:387
  53.9 5.2 %collective-permute-done.17.refs_5_ = bf16[64,2048]{1,0:T(8,128)(2,1)S(1)} collective-permute-done((bf16[64,2048]{1,0:T(8,128)(2,1)S(1)}, bf16[64,2048]{1,0:T(8,128)(2,1)S(1)}, u32[]{:S(2)}, u32[]{:S(2)}) %collective-permute-start.17) | collective-permute-done | bytes 262176 | tf_op jit(solution)/shard_map/ppermute | solution.py:387
  59.1 1.6 %collective-permute-start.22 = (bf16[64,2048]{1,0:T(8,128)(2,1)S(1)}, bf16[64,2048]{1,0:T(8,128)(2,1)S(1)}, u32[]{:S(2)}, u32[]{:S(2)}) collective-permute-start(bf16[64,2048]{1,0:T(8,128)(2,1)S(1)} %collective-permute-done.17.refs_5_), channel_id=1, source_target_pairs={{8,0},{16,8},{24,16},{28,24},{20,28},{12,20},{4,12},{0,4},{9,1},{1... | collective-permute-start | bytes 786440 | tf_op jit(solution)/shard_map/ppermute | solution.py:387
  61.1 3.6 %collective-permute-done.16.refs_4_ = bf16[64,2048]{1,0:T(8,128)(2,1)S(1)} collective-permute-done((bf16[64,2048]{1,0:T(8,128)(2,1)S(1)}, bf16[64,2048]{1,0:T(8,128)(2,1)S(1)}, u32[]{:S(2)}, u32[]{:S(2)}) %collective-permute-start.16) | collective-permute-done | bytes 262176 | tf_op jit(solution)/shard_map/ppermute | solution.py:387
  64.7 1.6 %collective-permute-start.21 = (bf16[64,2048]{1,0:T(8,128)(2,1)S(1)}, bf16[64,2048]{1,0:T(8,128)(2,1)S(1)}, u32[]{:S(2)}, u32[]{:S(2)}) collective-permute-start(bf16[64,2048]{1,0:T(8,128)(2,1)S(1)} %collective-permute-done.16.refs_4_), channel_id=1, source_target_pairs={{8,0},{16,8},{24,16},{28,24},{20,28},{12,20},{4,12},{0,4},{9,1},{1... | collective-permute-start | bytes 786440 | tf_op jit(solution)/shard_map/ppermute | solution.py:387
  66.7 1.8 %project.4 = (bf16[3,64,1024]{2,1,0:T(8,128)(2,1)S(1)}, bf16[3,64,1024]{2,1,0:T(8,128)(2,1)S(1)}) custom-call(bf16[64,2048]{1,0:T(8,128)(2,1)S(1)} %get-tuple-element.103.refs_0_, bf16[64,2048]{1,0:T(8,128)(2,1)S(1)} %get-tuple-element.104.refs_1_, bf16[64,2048]{1,0:T(8,128)(2,1)S(1)} %collective-permute-done.14.refs_2_, ...), custom_call_target="tpu_custom_call" | custom-call | flops 1000 | bytes 1000 | tf_op jit(solution)/shard_map/project/pallas_call | solution.py:230
  68.5 1.8 %collective-permute-done.22.refs_3_ = bf16[64,2048]{1,0:T(8,128)(2,1)S(1)} collective-permute-done((bf16[64,2048]{1,0:T(8,128)(2,1)S(1)}, bf16[64,2048]{1,0:T(8,128)(2,1)S(1)}, u32[]{:S(2)}, u32[]{:S(2)}) %collective-permute-start.22) | collective-permute-done | bytes 262176 | tf_op jit(solution)/shard_map/ppermute | solution.py:387
  72.3 3.6 %collective-permute-done.21.refs_2_ = bf16[64,2048]{1,0:T(8,128)(2,1)S(1)} collective-permute-done((bf16[64,2048]{1,0:T(8,128)(2,1)S(1)}, bf16[64,2048]{1,0:T(8,128)(2,1)S(1)}, u32[]{:S(2)}, u32[]{:S(2)}) %collective-permute-start.21) | collective-permute-done | bytes 262176 | tf_op jit(solution)/shard_map/ppermute | solution.py:387
  75.9 1.6 %collective-permute-start.27 = (bf16[64,2048]{1,0:T(8,128)(2,1)S(1)}, bf16[64,2048]{1,0:T(8,128)(2,1)S(1)}, u32[]{:S(2)}, u32[]{:S(2)}) collective-permute-start(bf16[64,2048]{1,0:T(8,128)(2,1)S(1)} %collective-permute-done.21.refs_2_), channel_id=1, source_target_pairs={{8,0},{16,8},{24,16},{28,24},{20,28},{12,20},{4,12},{0,4},{9,1},{1... | collective-permute-start | bytes 786440 | tf_op jit(solution)/shard_map/ppermute | solution.py:387
  79.2 2.0 %collective-permute-done.24.refs_3_ = bf16[64,2048]{1,0:T(8,128)(2,1)S(1)} collective-permute-done((bf16[64,2048]{1,0:T(8,128)(2,1)S(1)}, bf16[64,2048]{1,0:T(8,128)(2,1)S(1)}, u32[]{:S(2)}, u32[]{:S(2)}) %collective-permute-start.24) | collective-permute-done | bytes 262176 | tf_op jit(solution)/shard_map/ppermute | solution.py:387
  83.3 2.4 %collective-permute-done.27.refs_2_ = bf16[64,2048]{1,0:T(8,128)(2,1)S(1)} collective-permute-done((bf16[64,2048]{1,0:T(8,128)(2,1)S(1)}, bf16[64,2048]{1,0:T(8,128)(2,1)S(1)}, u32[]{:S(2)}, u32[]{:S(2)}) %collective-permute-start.27) | collective-permute-done | bytes 262176 | tf_op jit(solution)/shard_map/ppermute | solution.py:387
  95.8 8.5 %collective-permute-done.33.refs_3_ = bf16[1,64,1024]{2,1,0:T(8,128)(2,1)S(1)} collective-permute-done((bf16[1,64,1024]{2,1,0:T(8,128)(2,1)S(1)}, bf16[1,64,1024]{2,1,0:T(8,128)(2,1)S(1)}, u32[]{:S(2)}, u32[]{:S(2)}) %collective-permute-start.33) | collective-permute-done | bytes 131104 | tf_op jit(solution)/shard_map/ppermute | solution.py:435
  (68 shorter events, 26.1 us)
Async XLA Ops:
  2.8 11.2 %collective-permute-start.3 = (bf16[2,256,256]{2,1,0:T(8,128)(2,1)}, bf16[2,256,256]{2,1,0:T(8,128)(2,1)S(1)}, u32[]{:S(2)}, u32[]{:S(2)}) collective-permute-start(bf16[2,256,256]{2,1,0:T(8,128)(2,1)} %get-tuple-element.70.refs_1_), channel_id=1, source_target_pairs={{8,0},{16,8},{24,16},{28,24},{20,28},{12,20},{4,12},{0,4},{9,1},{1... | collective-permute-start | bytes 786440 | tf_op jit(solution)/shard_map/ppermute | solution.py:387
  5.8 10.1 %collective-permute-start = (bf16[2,256,256]{2,1,0:T(8,128)(2,1)}, bf16[2,256,256]{2,1,0:T(8,128)(2,1)S(1)}, u32[]{:S(2)}, u32[]{:S(2)}) collective-permute-start(bf16[2,256,256]{2,1,0:T(8,128)(2,1)} %get-tuple-element.69.refs_0_), channel_id=1, source_target_pairs={{0,8},{8,16},{16,24},{24,28},{28,20},{20,12},{12,4},{4,0},{1,9},{9... | collective-permute-start | bytes 786440 | tf_op jit(solution)/shard_map/ppermute | solution.py:387
  5.9 14.9 %collective-permute-start.2 = (bf16[2,256,256]{2,1,0:T(8,128)(2,1)}, bf16[2,256,256]{2,1,0:T(8,128)(2,1)S(1)}, u32[]{:S(2)}, u32[]{:S(2)}) collective-permute-start(bf16[2,256,256]{2,1,0:T(8,128)(2,1)} %get-tuple-element.70.refs_1_), channel_id=1, source_target_pairs={{0,8},{8,16},{16,24},{24,28},{28,20},{20,12},{12,4},{4,0},{1,9},{9... | collective-permute-start | bytes 786440 | tf_op jit(solution)/shard_map/ppermute | solution.py:387
  7.9 13.0 %collective-permute-start.4 = (bf16[2,256,256]{2,1,0:T(8,128)(2,1)}, bf16[2,256,256]{2,1,0:T(8,128)(2,1)S(1)}, u32[]{:S(2)}, u32[]{:S(2)}) collective-permute-start(bf16[2,256,256]{2,1,0:T(8,128)(2,1)} %get-tuple-element.69.refs_0_), channel_id=1, source_target_pairs={{8,0},{16,8},{24,16},{28,24},{20,28},{12,20},{4,12},{0,4},{9,1},{1... | collective-permute-start | bytes 786440 | tf_op jit(solution)/shard_map/ppermute | solution.py:387
  14.0 13.6 %collective-permute-start.7 = (bf16[2,256,256]{2,1,0:T(8,128)(2,1)S(1)}, bf16[2,256,256]{2,1,0:T(8,128)(2,1)S(1)}, u32[]{:S(2)}, u32[]{:S(2)}) collective-permute-start(bf16[2,256,256]{2,1,0:T(8,128)(2,1)S(1)} %collective-permute-done.3.refs_1_), channel_id=1, source_target_pairs={{8,0},{16,8},{24,16},{28,24},{20,28},{12,20},{4,12},{0,4},{9,1},{1... | collective-permute-start | bytes 786440 | tf_op jit(solution)/shard_map/ppermute | solution.py:387
  15.9 13.3 %collective-permute-start.1 = (bf16[2,256,256]{2,1,0:T(8,128)(2,1)S(1)}, bf16[2,256,256]{2,1,0:T(8,128)(2,1)S(1)}, u32[]{:S(2)}, u32[]{:S(2)}) collective-permute-start(bf16[2,256,256]{2,1,0:T(8,128)(2,1)S(1)} %collective-permute-done.refs_0_), channel_id=1, source_target_pairs={{0,8},{8,16},{16,24},{24,28},{28,20},{20,12},{12,4},{4,0},{1,9},{9... | collective-permute-start | bytes 786440 | tf_op jit(solution)/shard_map/ppermute | solution.py:387
  20.9 11.2 %collective-permute-start.6 = (bf16[2,256,256]{2,1,0:T(8,128)(2,1)S(1)}, bf16[2,256,256]{2,1,0:T(8,128)(2,1)S(1)}, u32[]{:S(2)}, u32[]{:S(2)}) collective-permute-start(bf16[2,256,256]{2,1,0:T(8,128)(2,1)S(1)} %collective-permute-done.2.refs_0_), channel_id=1, source_target_pairs={{0,8},{8,16},{16,24},{24,28},{28,20},{20,12},{12,4},{4,0},{1,9},{9... | collective-permute-start | bytes 786440 | tf_op jit(solution)/shard_map/ppermute | solution.py:387
  21.0 11.2 %collective-permute-start.8 = (bf16[2,256,256]{2,1,0:T(8,128)(2,1)S(1)}, bf16[2,256,256]{2,1,0:T(8,128)(2,1)S(1)}, u32[]{:S(2)}, u32[]{:S(2)}) collective-permute-start(bf16[2,256,256]{2,1,0:T(8,128)(2,1)S(1)} %collective-permute-done.4.refs_1_), channel_id=1, source_target_pairs={{8,0},{16,8},{24,16},{28,24},{20,28},{12,20},{4,12},{0,4},{9,1},{1... | collective-permute-start | bytes 786440 | tf_op jit(solution)/shard_map/ppermute | solution.py:387
  27.6 11.2 %collective-permute-start.10 = (bf16[2,256,256]{2,1,0:T(8,128)(2,1)S(1)}, bf16[2,256,256]{2,1,0:T(8,128)(2,1)S(1)}, u32[]{:S(2)}, u32[]{:S(2)}) collective-permute-start(bf16[2,256,256]{2,1,0:T(8,128)(2,1)S(1)} %collective-permute-done.7.refs_1_), channel_id=1, source_target_pairs={{8,0},{16,8},{24,16},{28,24},{20,28},{12,20},{4,12},{0,4},{9,1},{1... | collective-permute-start | bytes 786440 | tf_op jit(solution)/shard_map/ppermute | solution.py:387
  29.2 9.6 %collective-permute-start.5 = (bf16[2,256,256]{2,1,0:T(8,128)(2,1)S(1)}, bf16[2,256,256]{2,1,0:T(8,128)(2,1)S(1)}, u32[]{:S(2)}, u32[]{:S(2)}) collective-permute-start(bf16[2,256,256]{2,1,0:T(8,128)(2,1)S(1)} %collective-permute-done.1.refs_0_), channel_id=1, source_target_pairs={{0,8},{8,16},{16,24},{24,28},{28,20},{20,12},{12,4},{4,0},{1,9},{9... | collective-permute-start | bytes 786440 | tf_op jit(solution)/shard_map/ppermute | solution.py:387
  32.1 10.4 %collective-permute-start.13 = (bf16[2,256,256]{2,1,0:T(8,128)(2,1)S(1)}, bf16[2,256,256]{2,1,0:T(8,128)(2,1)S(1)}, u32[]{:S(2)}, u32[]{:S(2)}) collective-permute-start(bf16[2,256,256]{2,1,0:T(8,128)(2,1)S(1)} %collective-permute-done.8.refs_1_), channel_id=1, source_target_pairs={{8,0},{16,8},{24,16},{28,24},{20,28},{12,20},{4,12},{0,4},{9,1},{1... | collective-permute-start | bytes 786440 | tf_op jit(solution)/shard_map/ppermute | solution.py:387
  33.7 11.2 %collective-permute-start.12 = (bf16[2,256,256]{2,1,0:T(8,128)(2,1)S(1)}, bf16[2,256,256]{2,1,0:T(8,128)(2,1)S(1)}, u32[]{:S(2)}, u32[]{:S(2)}) collective-permute-start(bf16[2,256,256]{2,1,0:T(8,128)(2,1)S(1)} %collective-permute-done.6.refs_0_), channel_id=1, source_target_pairs={{0,8},{8,16},{16,24},{24,28},{28,20},{20,12},{12,4},{4,0},{1,9},{9... | collective-permute-start | bytes 786440 | tf_op jit(solution)/shard_map/ppermute | solution.py:387
  38.8 8.3 %collective-permute-start.11 = (bf16[2,256,256]{2,1,0:T(8,128)(2,1)S(1)}, bf16[2,256,256]{2,1,0:T(8,128)(2,1)S(1)}, u32[]{:S(2)}, u32[]{:S(2)}) collective-permute-start(bf16[2,256,256]{2,1,0:T(8,128)(2,1)S(1)} %collective-permute-done.10.refs_1_), channel_id=1, source_target_pairs={{8,0},{16,8},{24,16},{28,24},{20,28},{12,20},{4,12},{0,4},{9,1},{1... | collective-permute-start | bytes 786440 | tf_op jit(solution)/shard_map/ppermute | solution.py:399
  40.5 7.0 %collective-permute-start.9 = (bf16[2,256,256]{2,1,0:T(8,128)(2,1)S(1)}, bf16[2,256,256]{2,1,0:T(8,128)(2,1)S(1)}, u32[]{:S(2)}, u32[]{:S(2)}) collective-permute-start(bf16[2,256,256]{2,1,0:T(8,128)(2,1)S(1)} %collective-permute-done.5.refs_0_), channel_id=1, source_target_pairs={{0,8},{8,16},{16,24},{24,28},{28,20},{20,12},{12,4},{4,0},{1,9},{9... | collective-permute-start | bytes 786440 | tf_op jit(solution)/shard_map/ppermute | solution.py:398
  49.8 9.3 %collective-permute-start.17 = (bf16[64,2048]{1,0:T(8,128)(2,1)S(1)}, bf16[64,2048]{1,0:T(8,128)(2,1)S(1)}, u32[]{:S(2)}, u32[]{:S(2)}) collective-permute-start(bf16[64,2048]{1,0:T(8,128)(2,1)S(1)} %get-tuple-element.104.refs_1_), channel_id=1, source_target_pairs={{8,0},{16,8},{24,16},{28,24},{20,28},{12,20},{4,12},{0,4},{9,1},{1... | collective-permute-start | bytes 786440 | tf_op jit(solution)/shard_map/ppermute | solution.py:387
  51.4 9.2 %collective-permute-start.14 = (bf16[64,2048]{1,0:T(8,128)(2,1)S(1)}, bf16[64,2048]{1,0:T(8,128)(2,1)S(1)}, u32[]{:S(2)}, u32[]{:S(2)}) collective-permute-start(bf16[64,2048]{1,0:T(8,128)(2,1)S(1)} %get-tuple-element.103.refs_0_), channel_id=1, source_target_pairs={{0,8},{8,16},{16,24},{24,28},{28,20},{20,12},{12,4},{4,0},{1,9},{9... | collective-permute-start | bytes 786440 | tf_op jit(solution)/shard_map/ppermute | solution.py:387
  51.9 12.8 %collective-permute-start.16 = (bf16[64,2048]{1,0:T(8,128)(2,1)S(1)}, bf16[64,2048]{1,0:T(8,128)(2,1)S(1)}, u32[]{:S(2)}, u32[]{:S(2)}) collective-permute-start(bf16[64,2048]{1,0:T(8,128)(2,1)S(1)} %get-tuple-element.103.refs_0_), channel_id=1, source_target_pairs={{8,0},{16,8},{24,16},{28,24},{20,28},{12,20},{4,12},{0,4},{9,1},{1... | collective-permute-start | bytes 786440 | tf_op jit(solution)/shard_map/ppermute | solution.py:387
  53.4 12.8 %collective-permute-start.15 = (bf16[64,2048]{1,0:T(8,128)(2,1)S(1)}, bf16[64,2048]{1,0:T(8,128)(2,1)S(1)}, u32[]{:S(2)}, u32[]{:S(2)}) collective-permute-start(bf16[64,2048]{1,0:T(8,128)(2,1)S(1)} %get-tuple-element.104.refs_1_), channel_id=1, source_target_pairs={{0,8},{8,16},{16,24},{24,28},{28,20},{20,12},{12,4},{4,0},{1,9},{9... | collective-permute-start | bytes 786440 | tf_op jit(solution)/shard_map/ppermute | solution.py:387
  59.1 11.2 %collective-permute-start.22 = (bf16[64,2048]{1,0:T(8,128)(2,1)S(1)}, bf16[64,2048]{1,0:T(8,128)(2,1)S(1)}, u32[]{:S(2)}, u32[]{:S(2)}) collective-permute-start(bf16[64,2048]{1,0:T(8,128)(2,1)S(1)} %collective-permute-done.17.refs_5_), channel_id=1, source_target_pairs={{8,0},{16,8},{24,16},{28,24},{20,28},{12,20},{4,12},{0,4},{9,1},{1... | collective-permute-start | bytes 786440 | tf_op jit(solution)/shard_map/ppermute | solution.py:387
  60.7 11.2 %collective-permute-start.18 = (bf16[64,2048]{1,0:T(8,128)(2,1)S(1)}, bf16[64,2048]{1,0:T(8,128)(2,1)S(1)}, u32[]{:S(2)}, u32[]{:S(2)}) collective-permute-start(bf16[64,2048]{1,0:T(8,128)(2,1)S(1)} %collective-permute-done.14.refs_2_), channel_id=1, source_target_pairs={{0,8},{8,16},{16,24},{24,28},{28,20},{20,12},{12,4},{4,0},{1,9},{9... | collective-permute-start | bytes 786440 | tf_op jit(solution)/shard_map/ppermute | solution.py:387
  64.7 11.2 %collective-permute-start.21 = (bf16[64,2048]{1,0:T(8,128)(2,1)S(1)}, bf16[64,2048]{1,0:T(8,128)(2,1)S(1)}, u32[]{:S(2)}, u32[]{:S(2)}) collective-permute-start(bf16[64,2048]{1,0:T(8,128)(2,1)S(1)} %collective-permute-done.16.refs_4_), channel_id=1, source_target_pairs={{8,0},{16,8},{24,16},{28,24},{20,28},{12,20},{4,12},{0,4},{9,1},{1... | collective-permute-start | bytes 786440 | tf_op jit(solution)/shard_map/ppermute | solution.py:387
  66.3 11.2 %collective-permute-start.20 = (bf16[64,2048]{1,0:T(8,128)(2,1)S(1)}, bf16[64,2048]{1,0:T(8,128)(2,1)S(1)}, u32[]{:S(2)}, u32[]{:S(2)}) collective-permute-start(bf16[64,2048]{1,0:T(8,128)(2,1)S(1)} %collective-permute-done.15.refs_3_), channel_id=1, source_target_pairs={{0,8},{8,16},{16,24},{24,28},{28,20},{20,12},{12,4},{4,0},{1,9},{9... | collective-permute-start | bytes 786440 | tf_op jit(solution)/shard_map/ppermute | solution.py:387
  70.3 10.9 %collective-permute-start.24 = (bf16[64,2048]{1,0:T(8,128)(2,1)S(1)}, bf16[64,2048]{1,0:T(8,128)(2,1)S(1)}, u32[]{:S(2)}, u32[]{:S(2)}) collective-permute-start(bf16[64,2048]{1,0:T(8,128)(2,1)S(1)} %collective-permute-done.22.refs_3_), channel_id=1, source_target_pairs={{8,0},{16,8},{24,16},{28,24},{20,28},{12,20},{4,12},{0,4},{9,1},{1... | collective-permute-start | bytes 786440 | tf_op jit(solution)/shard_map/ppermute | solution.py:387
  71.9 10.9 %collective-permute-start.19 = (bf16[64,2048]{1,0:T(8,128)(2,1)S(1)}, bf16[64,2048]{1,0:T(8,128)(2,1)S(1)}, u32[]{:S(2)}, u32[]{:S(2)}) collective-permute-start(bf16[64,2048]{1,0:T(8,128)(2,1)S(1)} %collective-permute-done.18.refs_0_), channel_id=1, source_target_pairs={{0,8},{8,16},{16,24},{24,28},{28,20},{20,12},{12,4},{4,0},{1,9},{9... | collective-permute-start | bytes 786440 | tf_op jit(solution)/shard_map/ppermute | solution.py:387
  75.9 9.7 %collective-permute-start.27 = (bf16[64,2048]{1,0:T(8,128)(2,1)S(1)}, bf16[64,2048]{1,0:T(8,128)(2,1)S(1)}, u32[]{:S(2)}, u32[]{:S(2)}) collective-permute-start(bf16[64,2048]{1,0:T(8,128)(2,1)S(1)} %collective-permute-done.21.refs_2_), channel_id=1, source_target_pairs={{8,0},{16,8},{24,16},{28,24},{20,28},{12,20},{4,12},{0,4},{9,1},{1... | collective-permute-start | bytes 786440 | tf_op jit(solution)/shard_map/ppermute | solution.py:387
  77.5 9.4 %collective-permute-start.26 = (bf16[64,2048]{1,0:T(8,128)(2,1)S(1)}, bf16[64,2048]{1,0:T(8,128)(2,1)S(1)}, u32[]{:S(2)}, u32[]{:S(2)}) collective-permute-start(bf16[64,2048]{1,0:T(8,128)(2,1)S(1)} %collective-permute-done.20.refs_1_), channel_id=1, source_target_pairs={{0,8},{8,16},{16,24},{24,28},{28,20},{20,12},{12,4},{4,0},{1,9},{9... | collective-permute-start | bytes 786440 | tf_op jit(solution)/shard_map/ppermute | solution.py:387
  78.0 13.0 %collective-permute-start.28 = (bf16[3,64,1024]{2,1,0:T(8,128)(2,1)S(1)}, bf16[3,64,1024]{2,1,0:T(8,128)(2,1)S(1)}, u32[]{:S(2)}, u32[]{:S(2)}) collective-permute-start(bf16[3,64,1024]{2,1,0:T(8,128)(2,1)S(1)} %get-tuple-element.107), channel_id=1, source_target_pairs={{0,1},{1,0},{2,3},{3,2},{4,5},{5,4},{6,7},{7,6},{8,9},{9,8},{10,11... | collective-permute-start | bytes 1179656 | tf_op jit(solution)/shard_map/ppermute | solution.py:424
  81.2 8.4 %collective-permute-start.25 = (bf16[64,2048]{1,0:T(8,128)(2,1)S(1)}, bf16[64,2048]{1,0:T(8,128)(2,1)S(1)}, u32[]{:S(2)}, u32[]{:S(2)}) collective-permute-start(bf16[64,2048]{1,0:T(8,128)(2,1)S(1)} %collective-permute-done.24.refs_3_), channel_id=1, source_target_pairs={{8,0},{16,8},{24,16},{28,24},{20,28},{12,20},{4,12},{0,4},{9,1},{1... | collective-permute-start | bytes 786440 | tf_op jit(solution)/shard_map/ppermute | solution.py:399
  82.8 8.1 %collective-permute-start.23 = (bf16[64,2048]{1,0:T(8,128)(2,1)S(1)}, bf16[64,2048]{1,0:T(8,128)(2,1)S(1)}, u32[]{:S(2)}, u32[]{:S(2)}) collective-permute-start(bf16[64,2048]{1,0:T(8,128)(2,1)S(1)} %collective-permute-done.19.refs_0_), channel_id=1, source_target_pairs={{0,8},{8,16},{16,24},{24,28},{28,20},{20,12},{12,4},{4,0},{1,9},{9... | collective-permute-start | bytes 786440 | tf_op jit(solution)/shard_map/ppermute | solution.py:398
  85.6 5.3 %collective-permute-start.29 = (bf16[2,64,1024]{2,1,0:T(8,128)(2,1)S(1)}, bf16[2,64,1024]{2,1,0:T(8,128)(2,1)S(1)}, u32[]{:S(2)}, u32[]{:S(2)}) collective-permute-start(bf16[2,64,1024]{2,1,0:T(8,128)(2,1)S(1)} %get-tuple-element.112), channel_id=1, source_target_pairs={{0,1},{1,0},{2,3},{3,2},{4,5},{5,4},{6,7},{7,6},{8,9},{9,8},{10,11... | collective-permute-start | bytes 786440 | tf_op jit(solution)/shard_map/ppermute | solution.py:424
  91.4 12.9 %collective-permute-start.31 = (bf16[3,64,1024]{2,1,0:T(8,128)(2,1)S(1)}, bf16[3,64,1024]{2,1,0:T(8,128)(2,1)S(1)}, u32[]{:S(2)}, u32[]{:S(2)}) collective-permute-start(bf16[3,64,1024]{2,1,0:T(8,128)(2,1)S(1)} %get-tuple-element.122), channel_id=1, source_target_pairs={{0,2},{1,3},{2,0},{3,1},{4,6},{5,7},{6,4},{7,5},{8,10},{9,11},{10,... | collective-permute-start | bytes 1179656 | tf_op jit(solution)/shard_map/ppermute | solution.py:435
  95.2 9.1 %collective-permute-start.33 = (bf16[1,64,1024]{2,1,0:T(8,128)(2,1)S(1)}, bf16[1,64,1024]{2,1,0:T(8,128)(2,1)S(1)}, u32[]{:S(2)}, u32[]{:S(2)}) collective-permute-start(bf16[1,64,1024]{2,1,0:T(8,128)(2,1)S(1)} %get-tuple-element.130), channel_id=1, source_target_pairs={{0,2},{1,3},{2,0},{3,1},{4,6},{5,7},{6,4},{7,5},{8,10},{9,11},{10,... | collective-permute-start | bytes 393224 | tf_op jit(solution)/shard_map/ppermute | solution.py:435
  (9 other events, 73.7 us)

commit v6 on v4

--- a/solution.py
+++ b/solution.py
@@ -391,7 +391,7 @@
             token = visit(step - 1, arrived if step > 1 else None, token)
             arrived = held
             if step < half - 1:
-                held = [send_both(arrived[k], k, token) for k in range(2)]
+                held = [send_both(arrived[k], k, token if step > 1 else None) for k in range(2)]
             else:
                 held = (
                     lax.ppermute(after(arrived[0][0], token), "ctx", right),

time: 108 us -> 107 us (level)
    ppermute x12, waiting for transfers between devices: 8.58 us -> 3.77 us  [send_both(): lax.ppermute(from_left, 'ctx', right)]
    ppermute x12, waiting for transfers between devices: 20.1 us -> 24.4 us  [send_both(): lax.ppermute(from_right, 'ctx', left)]
    ppermute x12, starting transfers between devices: 5.89 us -> 7.85 us  [send_both(): lax.ppermute(from_left, 'ctx', right)]
    ppermute x12, starting transfers between devices: 19.7 us -> 18.1 us  [send_both(): lax.ppermute(from_right, 'ctx', left)]
where the time goes in v6:
time: 107 us
  waiting for transfers between devices  42.5 us (40%)
  starting transfers between devices  32.3 us (30%)
  Pallas kernels  28.2 us (26%)
  local copies, waits for them, and re-layouts  3.6 us (3%)
    ppermute x12, waiting for transfers between devices, send_both(): lax.ppermute(from_right, 'ctx', left)  24.4 us
    pallas_call x8, Pallas kernels, flash(): pl.pallas_call(functools.partial(flash_kernel, n, tok, pieces, not state,...  18.6 us
    ppermute x12, starting transfers between devices, send_both(): lax.ppermute(from_right, 'ctx', left)  18.1 us
    ppermute x2, waiting for transfers between devices, cross(): got = lax.ppermute(send, 'tp', [(t, t ^ 2) for t in range(n_tp)])  8.44 us
    ppermute x12, starting transfers between devices, send_both(): lax.ppermute(from_left, 'ctx', right)  7.85 us
    pallas_call x4, Pallas kernels, project(): pl.pallas_call(functools.partial(project_kernel, count), out_shape=[jax.S...  5.01 us
    ppermute x12, waiting for transfers between devices, send_both(): lax.ppermute(from_left, 'ctx', right)  3.77 us
    unnamed x12, local copies, waits for them, and re-layouts  3.6 us
  transfers between devices with their start and end apart: 35, of which 16 were waited for; matrix products, arithmetic and copies ran while one was open for 0% of the time, Pallas kernels for 20%

profile of v6, /device:TPU:0, one launch (start us, length us, event | category | flops | bytes accessed | tf_op | source)
XLA Modules:
  0.0 106.9 jit_solution(14947727089920752190)
XLA Ops:
  0.0 2.8 %pick.1 = (bf16[2,256,256]{2,1,0:T(8,128)(2,1)}, bf16[2,256,256]{2,1,0:T(8,128)(2,1)}) custom-call(s32[1,3]{1,0:T(1,128)} %hit_slots.1, bf16[2,16,128,256]{3,2,1,0:T(8,128)(2,1)} %pool_ref.1, bf16[2,128,256]{2,1,0:T(8,128)(2,1)} %suffix_ref.1), custom_call_target="tpu_custom_call" | custom-call | tf_op jit(solution)/shard_map/pick/pallas_call | solution.py:63
  2.8 3.0 %collective-permute-start.3 = (bf16[2,256,256]{2,1,0:T(8,128)(2,1)}, bf16[2,256,256]{2,1,0:T(8,128)(2,1)S(1)}, u32[]{:S(2)}, u32[]{:S(2)}) collective-permute-start(bf16[2,256,256]{2,1,0:T(8,128)(2,1)} %get-tuple-element.61.refs_1_), channel_id=1, source_target_pairs={{8,0},{16,8},{24,16},{28,24},{20,28},{12,20},{4,12},{0,4},{9,1},{1... | collective-permute-start | bytes 786440 | tf_op jit(solution)/shard_map/ppermute | solution.py:386
  6.0 2.0 %collective-permute-start.2 = (bf16[2,256,256]{2,1,0:T(8,128)(2,1)}, bf16[2,256,256]{2,1,0:T(8,128)(2,1)S(1)}, u32[]{:S(2)}, u32[]{:S(2)}) collective-permute-start(bf16[2,256,256]{2,1,0:T(8,128)(2,1)} %get-tuple-element.61.refs_1_), channel_id=1, source_target_pairs={{0,8},{8,16},{16,24},{24,28},{28,20},{20,12},{12,4},{4,0},{1,9},{9... | collective-permute-start | bytes 786440 | tf_op jit(solution)/shard_map/ppermute | solution.py:386
  8.0 5.3 %collective-permute-done.3.refs_1_ = bf16[2,256,256]{2,1,0:T(8,128)(2,1)S(1)} collective-permute-done((bf16[2,256,256]{2,1,0:T(8,128)(2,1)}, bf16[2,256,256]{2,1,0:T(8,128)(2,1)S(1)}, u32[]{:S(2)}, u32[]{:S(2)}) %collective-permute-start.3) | collective-permute-done | bytes 262176 | tf_op jit(solution)/shard_map/ppermute | solution.py:386
  13.2 2.0 %collective-permute-start.7 = (bf16[2,256,256]{2,1,0:T(8,128)(2,1)S(1)}, bf16[2,256,256]{2,1,0:T(8,128)(2,1)S(1)}, u32[]{:S(2)}, u32[]{:S(2)}) collective-permute-start(bf16[2,256,256]{2,1,0:T(8,128)(2,1)S(1)} %collective-permute-done.3.refs_1_), channel_id=1, source_target_pairs={{8,0},{16,8},{24,16},{28,24},{20,28},{12,20},{4,12},{0,4},{9,1},{1... | collective-permute-start | bytes 786440 | tf_op jit(solution)/shard_map/ppermute | solution.py:386
  19.0 2.4 %flash.8 = (bf16[128,2048]{1,0:T(8,128)(2,1)S(1)}, f32[8,2048]{1,0:T(8,128)S(1)}, f32[8,2048]{1,0:T(8,128)S(1)}, f32[128,2048]{1,0:T(8,128)S(1)}) custom-call(s32[8]{0:T(128)S(1)} %copy-done.4, bf16[128,2048]{1,0:T(8,128)(2,1)S(1)} %copy-done.1, bf16[2,256,256]{2,1,0:T(8,128)(2,1)S(1)} %copy-done.2, bf16[2,256,256]{2,1,0:T(8,128)(2,1)S(1)} %copy-done.3), custom_call_target="tpu_custom_call" | custom-call | flops 1000 | bytes 1000 | tf_op jit(solution)/shard_map/flash/pallas_call | solution.py:196
  21.4 2.1 %collective-permute-start.6 = (bf16[2,256,256]{2,1,0:T(8,128)(2,1)S(1)}, bf16[2,256,256]{2,1,0:T(8,128)(2,1)S(1)}, u32[]{:S(2)}, u32[]{:S(2)}) collective-permute-start(bf16[2,256,256]{2,1,0:T(8,128)(2,1)S(1)} %collective-permute-done.2.refs_0_), channel_id=1, source_target_pairs={{0,8},{8,16},{16,24},{24,28},{28,20},{20,12},{12,4},{4,0},{1,9},{9... | collective-permute-start | bytes 786440 | tf_op jit(solution)/shard_map/ppermute | solution.py:386
  23.5 2.4 %flash.9 = (f32[8,2048]{1,0:T(8,128)S(1)}, f32[8,2048]{1,0:T(8,128)S(1)}, f32[128,2048]{1,0:T(8,128)S(1)}) custom-call(s32[8]{0:T(128)S(1)} %copy-done.4, bf16[128,2048]{1,0:T(8,128)(2,1)S(1)} %get-tuple-element.62.q_ref, bf16[2,256,256]{2,1,0:T(8,128)(2,1)S(1)} %collective-permute-done.refs_0_, ...), custom_call_target="tpu_custom_call", output_to_operand_aliasing={{0}: (4, {}), {1}: (5, {}), {2}: (6, {})} | custom-call | flops 1000 | bytes 1000 | tf_op jit(solution)/shard_map/flash/pallas_call | solution.py:196
  25.8 2.3 %flash.10 = (f32[8,2048]{1,0:T(8,128)S(1)}, f32[8,2048]{1,0:T(8,128)S(1)}, f32[128,2048]{1,0:T(8,128)S(1)}) custom-call(s32[8]{0:T(128)S(1)} %copy-done.4, bf16[128,2048]{1,0:T(8,128)(2,1)S(1)} %get-tuple-element.62.q_ref, bf16[2,256,256]{2,1,0:T(8,128)(2,1)S(1)} %collective-permute-done.2.refs_0_, ...), custom_call_target="tpu_custom_call", output_to_operand_aliasing={{0}: (4, {}), {1}: (5, {}), {2}: (6, {})} | custom-call | flops 1000 | bytes 1000 | tf_op jit(solution)/shard_map/flash/pallas_call | solution.py:196
  28.1 2.0 %collective-permute-start.10 = (bf16[2,256,256]{2,1,0:T(8,128)(2,1)S(1)}, bf16[2,256,256]{2,1,0:T(8,128)(2,1)S(1)}, u32[]{:S(2)}, u32[]{:S(2)}) collective-permute-start(bf16[2,256,256]{2,1,0:T(8,128)(2,1)S(1)} %collective-permute-done.7.refs_1_), channel_id=1, source_target_pairs={{8,0},{16,8},{24,16},{28,24},{20,28},{12,20},{4,12},{0,4},{9,1},{1... | collective-permute-start | bytes 786440 | tf_op jit(solution)/shard_map/ppermute | solution.py:386
  30.3 1.9 %collective-permute-done.6.refs_0_ = bf16[2,256,256]{2,1,0:T(8,128)(2,1)S(1)} collective-permute-done((bf16[2,256,256]{2,1,0:T(8,128)(2,1)S(1)}, bf16[2,256,256]{2,1,0:T(8,128)(2,1)S(1)}, u32[]{:S(2)}, u32[]{:S(2)}) %collective-permute-start.6) | collective-permute-done | bytes 262176 | tf_op jit(solution)/shard_map/ppermute | solution.py:386
  32.1 1.6 %collective-permute-start.13 = (bf16[2,256,256]{2,1,0:T(8,128)(2,1)S(1)}, bf16[2,256,256]{2,1,0:T(8,128)(2,1)S(1)}, u32[]{:S(2)}, u32[]{:S(2)}) collective-permute-start(bf16[2,256,256]{2,1,0:T(8,128)(2,1)S(1)} %collective-permute-done.8.refs_1_), channel_id=1, source_target_pairs={{8,0},{16,8},{24,16},{28,24},{20,28},{12,20},{4,12},{0,4},{9,1},{1... | collective-permute-start | bytes 786440 | tf_op jit(solution)/shard_map/ppermute | solution.py:386
  34.2 2.4 %flash.11 = (f32[8,2048]{1,0:T(8,128)S(1)}, f32[8,2048]{1,0:T(8,128)S(1)}, f32[128,2048]{1,0:T(8,128)S(1)}) custom-call(s32[8]{0:T(128)S(1)} %copy-done.5, bf16[128,2048]{1,0:T(8,128)(2,1)S(1)} %get-tuple-element.62.q_ref, bf16[2,256,256]{2,1,0:T(8,128)(2,1)S(1)} %collective-permute-done.1.refs_0_, ...), custom_call_target="tpu_custom_call", output_to_operand_aliasing={{0}: (4, {}), {1}: (5, {}), {2}: (6, {})} | custom-call | flops 1000 | bytes 1000 | tf_op jit(solution)/shard_map/flash/pallas_call | solution.py:196
  36.6 2.3 %flash.12 = (f32[8,2048]{1,0:T(8,128)S(1)}, f32[8,2048]{1,0:T(8,128)S(1)}, f32[128,2048]{1,0:T(8,128)S(1)}) custom-call(s32[8]{0:T(128)S(1)} %copy-done.5, bf16[128,2048]{1,0:T(8,128)(2,1)S(1)} %get-tuple-element.62.q_ref, bf16[2,256,256]{2,1,0:T(8,128)(2,1)S(1)} %collective-permute-done.6.refs_0_, ...), custom_call_target="tpu_custom_call", output_to_operand_aliasing={{0}: (4, {}), {1}: (5, {}), {2}: (6, {})} | custom-call | flops 1000 | bytes 1000 | tf_op jit(solution)/shard_map/flash/pallas_call | solution.py:196
  39.1 1.6 %collective-permute-start.11 = (bf16[2,256,256]{2,1,0:T(8,128)(2,1)S(1)}, bf16[2,256,256]{2,1,0:T(8,128)(2,1)S(1)}, u32[]{:S(2)}, u32[]{:S(2)}) collective-permute-start(bf16[2,256,256]{2,1,0:T(8,128)(2,1)S(1)} %collective-permute-done.10.refs_1_), channel_id=1, source_target_pairs={{8,0},{16,8},{24,16},{28,24},{20,28},{12,20},{4,12},{0,4},{9,1},{1... | collective-permute-start | bytes 786440 | tf_op jit(solution)/shard_map/ppermute | solution.py:398
  41.1 1.9 %collective-permute-done.13.refs_1_ = bf16[2,256,256]{2,1,0:T(8,128)(2,1)S(1)} collective-permute-done((bf16[2,256,256]{2,1,0:T(8,128)(2,1)S(1)}, bf16[2,256,256]{2,1,0:T(8,128)(2,1)S(1)}, u32[]{:S(2)}, u32[]{:S(2)}) %collective-permute-start.13) | collective-permute-done | bytes 262176 | tf_op jit(solution)/shard_map/ppermute | solution.py:386
  43.0 2.4 %flash.13 = (f32[8,2048]{1,0:T(8,128)S(1)}, f32[8,2048]{1,0:T(8,128)S(1)}, f32[128,2048]{1,0:T(8,128)S(1)}) custom-call(s32[8]{0:T(128)S(1)} %copy-done.5, bf16[128,2048]{1,0:T(8,128)(2,1)S(1)} %get-tuple-element.62.q_ref, bf16[2,256,256]{2,1,0:T(8,128)(2,1)S(1)} %collective-permute-done.5.refs_0_, ...), custom_call_target="tpu_custom_call", output_to_operand_aliasing={{0}: (4, {}), {1}: (5, {}), {2}: (6, {})} | custom-call | flops 1000 | bytes 1000 | tf_op jit(solution)/shard_map/flash/pallas_call | solution.py:196
  45.4 2.3 %flash.14 = (f32[8,2048]{1,0:T(8,128)S(1)}, f32[8,2048]{1,0:T(8,128)S(1)}, f32[128,2048]{1,0:T(8,128)S(1)}) custom-call(s32[8]{0:T(128)S(1)} %copy-done.5, bf16[128,2048]{1,0:T(8,128)(2,1)S(1)} %get-tuple-element.62.q_ref, bf16[2,256,256]{2,1,0:T(8,128)(2,1)S(1)} %collective-permute-done.12.refs_0_, ...), custom_call_target="tpu_custom_call", output_to_operand_aliasing={{0}: (4, {}), {1}: (5, {}), {2}: (6, {})} | custom-call | flops 1000 | bytes 1000 | tf_op jit(solution)/shard_map/flash/pallas_call | solution.py:196
  47.7 2.3 %flash.15 = (bf16[64,2048]{1,0:T(8,128)(2,1)S(1)}, bf16[64,2048]{1,0:T(8,128)(2,1)S(1)}) custom-call(s32[8]{0:T(128)S(1)} %copy-done.5, bf16[128,2048]{1,0:T(8,128)(2,1)S(1)} %get-tuple-element.62.q_ref, bf16[2,256,256]{2,1,0:T(8,128)(2,1)S(1)} %collective-permute-done.9.refs_0_, bf16[2,256,256]{2,1,0:T(8,128)(2,1)S(1)} %collective-permute-done.11.refs_1_, ...), custom_call_target="tpu_custom_call" | custom-call | flops 1000 | bytes 1000 | tf_op jit(solution)/shard_map/flash/pallas_call | solution.py:196
  50.0 1.6 %collective-permute-start.17 = (bf16[64,2048]{1,0:T(8,128)(2,1)S(1)}, bf16[64,2048]{1,0:T(8,128)(2,1)S(1)}, u32[]{:S(2)}, u32[]{:S(2)}) collective-permute-start(bf16[64,2048]{1,0:T(8,128)(2,1)S(1)} %get-tuple-element.91.refs_1_), channel_id=1, source_target_pairs={{8,0},{16,8},{24,16},{28,24},{20,28},{12,20},{4,12},{0,4},{9,1},{1... | collective-permute-start | bytes 786440 | tf_op jit(solution)/shard_map/ppermute | solution.py:386
  54.2 5.1 %collective-permute-done.17.refs_5_ = bf16[64,2048]{1,0:T(8,128)(2,1)S(1)} collective-permute-done((bf16[64,2048]{1,0:T(8,128)(2,1)S(1)}, bf16[64,2048]{1,0:T(8,128)(2,1)S(1)}, u32[]{:S(2)}, u32[]{:S(2)}) %collective-permute-start.17) | collective-permute-done | bytes 262176 | tf_op jit(solution)/shard_map/ppermute | solution.py:386
  59.3 1.6 %collective-permute-start.22 = (bf16[64,2048]{1,0:T(8,128)(2,1)S(1)}, bf16[64,2048]{1,0:T(8,128)(2,1)S(1)}, u32[]{:S(2)}, u32[]{:S(2)}) collective-permute-start(bf16[64,2048]{1,0:T(8,128)(2,1)S(1)} %collective-permute-done.17.refs_5_), channel_id=1, source_target_pairs={{8,0},{16,8},{24,16},{28,24},{20,28},{12,20},{4,12},{0,4},{9,1},{1... | collective-permute-start | bytes 786440 | tf_op jit(solution)/shard_map/ppermute | solution.py:386
  61.4 3.5 %collective-permute-done.16.refs_4_ = bf16[64,2048]{1,0:T(8,128)(2,1)S(1)} collective-permute-done((bf16[64,2048]{1,0:T(8,128)(2,1)S(1)}, bf16[64,2048]{1,0:T(8,128)(2,1)S(1)}, u32[]{:S(2)}, u32[]{:S(2)}) %collective-permute-start.16) | collective-permute-done | bytes 262176 | tf_op jit(solution)/shard_map/ppermute | solution.py:386
  67.0 1.8 %project.4 = (bf16[3,64,1024]{2,1,0:T(8,128)(2,1)S(1)}, bf16[3,64,1024]{2,1,0:T(8,128)(2,1)S(1)}) custom-call(bf16[64,2048]{1,0:T(8,128)(2,1)S(1)} %get-tuple-element.90.refs_0_, bf16[64,2048]{1,0:T(8,128)(2,1)S(1)} %get-tuple-element.91.refs_1_, bf16[64,2048]{1,0:T(8,128)(2,1)S(1)} %collective-permute-done.14.refs_2_, ...), custom_call_target="tpu_custom_call" | custom-call | flops 1000 | bytes 1000 | tf_op jit(solution)/shard_map/project/pallas_call | solution.py:230
  68.8 1.7 %collective-permute-done.22.refs_3_ = bf16[64,2048]{1,0:T(8,128)(2,1)S(1)} collective-permute-done((bf16[64,2048]{1,0:T(8,128)(2,1)S(1)}, bf16[64,2048]{1,0:T(8,128)(2,1)S(1)}, u32[]{:S(2)}, u32[]{:S(2)}) %collective-permute-start.22) | collective-permute-done | bytes 262176 | tf_op jit(solution)/shard_map/ppermute | solution.py:386
  70.5 1.6 %collective-permute-start.24 = (bf16[64,2048]{1,0:T(8,128)(2,1)S(1)}, bf16[64,2048]{1,0:T(8,128)(2,1)S(1)}, u32[]{:S(2)}, u32[]{:S(2)}) collective-permute-start(bf16[64,2048]{1,0:T(8,128)(2,1)S(1)} %collective-permute-done.22.refs_3_), channel_id=1, source_target_pairs={{8,0},{16,8},{24,16},{28,24},{20,28},{12,20},{4,12},{0,4},{9,1},{1... | collective-permute-start | bytes 786440 | tf_op jit(solution)/shard_map/ppermute | solution.py:386
  72.6 3.5 %collective-permute-done.21.refs_2_ = bf16[64,2048]{1,0:T(8,128)(2,1)S(1)} collective-permute-done((bf16[64,2048]{1,0:T(8,128)(2,1)S(1)}, bf16[64,2048]{1,0:T(8,128)(2,1)S(1)}, u32[]{:S(2)}, u32[]{:S(2)}) %collective-permute-start.21) | collective-permute-done | bytes 262176 | tf_op jit(solution)/shard_map/ppermute | solution.py:386
  81.0 1.6 %collective-permute-start.25 = (bf16[64,2048]{1,0:T(8,128)(2,1)S(1)}, bf16[64,2048]{1,0:T(8,128)(2,1)S(1)}, u32[]{:S(2)}, u32[]{:S(2)}) collective-permute-start(bf16[64,2048]{1,0:T(8,128)(2,1)S(1)} %collective-permute-done.24.refs_3_), channel_id=1, source_target_pairs={{8,0},{16,8},{24,16},{28,24},{20,28},{12,20},{4,12},{0,4},{9,1},{1... | collective-permute-start | bytes 786440 | tf_op jit(solution)/shard_map/ppermute | solution.py:398
  83.1 1.7 %collective-permute-done.27.refs_2_ = bf16[64,2048]{1,0:T(8,128)(2,1)S(1)} collective-permute-done((bf16[64,2048]{1,0:T(8,128)(2,1)S(1)}, bf16[64,2048]{1,0:T(8,128)(2,1)S(1)}, u32[]{:S(2)}, u32[]{:S(2)}) %collective-permute-start.27) | collective-permute-done | bytes 262176 | tf_op jit(solution)/shard_map/ppermute | solution.py:386
  84.7 1.6 %collective-permute-done.26.refs_1_ = bf16[64,2048]{1,0:T(8,128)(2,1)S(1)} collective-permute-done((bf16[64,2048]{1,0:T(8,128)(2,1)S(1)}, bf16[64,2048]{1,0:T(8,128)(2,1)S(1)}, u32[]{:S(2)}, u32[]{:S(2)}) %collective-permute-start.26) | collective-permute-done | bytes 262176 | tf_op jit(solution)/shard_map/ppermute | solution.py:386
  87.7 1.8 %collective-permute-done.25.refs_1_ = bf16[64,2048]{1,0:T(8,128)(2,1)S(1)} collective-permute-done((bf16[64,2048]{1,0:T(8,128)(2,1)S(1)}, bf16[64,2048]{1,0:T(8,128)(2,1)S(1)}, u32[]{:S(2)}, u32[]{:S(2)}) %collective-permute-start.25) | collective-permute-done | bytes 262176 | tf_op jit(solution)/shard_map/ppermute | solution.py:398
  95.7 8.4 %collective-permute-done.33.refs_3_ = bf16[1,64,1024]{2,1,0:T(8,128)(2,1)S(1)} collective-permute-done((bf16[1,64,1024]{2,1,0:T(8,128)(2,1)S(1)}, bf16[1,64,1024]{2,1,0:T(8,128)(2,1)S(1)}, u32[]{:S(2)}, u32[]{:S(2)}) %collective-permute-start.33) | collective-permute-done | bytes 131104 | tf_op jit(solution)/shard_map/ppermute | solution.py:434
  (67 shorter events, 26.4 us)
Async XLA Ops:
  2.8 10.4 %collective-permute-start.3 = (bf16[2,256,256]{2,1,0:T(8,128)(2,1)}, bf16[2,256,256]{2,1,0:T(8,128)(2,1)S(1)}, u32[]{:S(2)}, u32[]{:S(2)}) collective-permute-start(bf16[2,256,256]{2,1,0:T(8,128)(2,1)} %get-tuple-element.61.refs_1_), channel_id=1, source_target_pairs={{8,0},{16,8},{24,16},{28,24},{20,28},{12,20},{4,12},{0,4},{9,1},{1... | collective-permute-start | bytes 786440 | tf_op jit(solution)/shard_map/ppermute | solution.py:386
  5.8 9.4 %collective-permute-start = (bf16[2,256,256]{2,1,0:T(8,128)(2,1)}, bf16[2,256,256]{2,1,0:T(8,128)(2,1)S(1)}, u32[]{:S(2)}, u32[]{:S(2)}) collective-permute-start(bf16[2,256,256]{2,1,0:T(8,128)(2,1)} %get-tuple-element.60.refs_0_), channel_id=1, source_target_pairs={{0,8},{8,16},{16,24},{24,28},{28,20},{20,12},{12,4},{4,0},{1,9},{9... | collective-permute-start | bytes 786440 | tf_op jit(solution)/shard_map/ppermute | solution.py:386
  6.0 15.4 %collective-permute-start.2 = (bf16[2,256,256]{2,1,0:T(8,128)(2,1)}, bf16[2,256,256]{2,1,0:T(8,128)(2,1)S(1)}, u32[]{:S(2)}, u32[]{:S(2)}) collective-permute-start(bf16[2,256,256]{2,1,0:T(8,128)(2,1)} %get-tuple-element.61.refs_1_), channel_id=1, source_target_pairs={{0,8},{8,16},{16,24},{24,28},{28,20},{20,12},{12,4},{4,0},{1,9},{9... | collective-permute-start | bytes 786440 | tf_op jit(solution)/shard_map/ppermute | solution.py:386
  7.9 15.5 %collective-permute-start.4 = (bf16[2,256,256]{2,1,0:T(8,128)(2,1)}, bf16[2,256,256]{2,1,0:T(8,128)(2,1)S(1)}, u32[]{:S(2)}, u32[]{:S(2)}) collective-permute-start(bf16[2,256,256]{2,1,0:T(8,128)(2,1)} %get-tuple-element.60.refs_0_), channel_id=1, source_target_pairs={{8,0},{16,8},{24,16},{28,24},{20,28},{12,20},{4,12},{0,4},{9,1},{1... | collective-permute-start | bytes 786440 | tf_op jit(solution)/shard_map/ppermute | solution.py:386
  13.2 14.9 %collective-permute-start.7 = (bf16[2,256,256]{2,1,0:T(8,128)(2,1)S(1)}, bf16[2,256,256]{2,1,0:T(8,128)(2,1)S(1)}, u32[]{:S(2)}, u32[]{:S(2)}) collective-permute-start(bf16[2,256,256]{2,1,0:T(8,128)(2,1)S(1)} %collective-permute-done.3.refs_1_), channel_id=1, source_target_pairs={{8,0},{16,8},{24,16},{28,24},{20,28},{12,20},{4,12},{0,4},{9,1},{1... | collective-permute-start | bytes 786440 | tf_op jit(solution)/shard_map/ppermute | solution.py:386
  15.3 14.8 %collective-permute-start.1 = (bf16[2,256,256]{2,1,0:T(8,128)(2,1)S(1)}, bf16[2,256,256]{2,1,0:T(8,128)(2,1)S(1)}, u32[]{:S(2)}, u32[]{:S(2)}) collective-permute-start(bf16[2,256,256]{2,1,0:T(8,128)(2,1)S(1)} %collective-permute-done.refs_0_), channel_id=1, source_target_pairs={{0,8},{8,16},{16,24},{24,28},{28,20},{20,12},{12,4},{4,0},{1,9},{9... | collective-permute-start | bytes 786440 | tf_op jit(solution)/shard_map/ppermute | solution.py:386
  21.4 10.8 %collective-permute-start.6 = (bf16[2,256,256]{2,1,0:T(8,128)(2,1)S(1)}, bf16[2,256,256]{2,1,0:T(8,128)(2,1)S(1)}, u32[]{:S(2)}, u32[]{:S(2)}) collective-permute-start(bf16[2,256,256]{2,1,0:T(8,128)(2,1)S(1)} %collective-permute-done.2.refs_0_), channel_id=1, source_target_pairs={{0,8},{8,16},{16,24},{24,28},{28,20},{20,12},{12,4},{4,0},{1,9},{9... | collective-permute-start | bytes 786440 | tf_op jit(solution)/shard_map/ppermute | solution.py:386
  23.4 8.7 %collective-permute-start.8 = (bf16[2,256,256]{2,1,0:T(8,128)(2,1)S(1)}, bf16[2,256,256]{2,1,0:T(8,128)(2,1)S(1)}, u32[]{:S(2)}, u32[]{:S(2)}) collective-permute-start(bf16[2,256,256]{2,1,0:T(8,128)(2,1)S(1)} %collective-permute-done.4.refs_1_), channel_id=1, source_target_pairs={{8,0},{16,8},{24,16},{28,24},{20,28},{12,20},{4,12},{0,4},{9,1},{1... | collective-permute-start | bytes 786440 | tf_op jit(solution)/shard_map/ppermute | solution.py:386
  28.1 10.7 %collective-permute-start.10 = (bf16[2,256,256]{2,1,0:T(8,128)(2,1)S(1)}, bf16[2,256,256]{2,1,0:T(8,128)(2,1)S(1)}, u32[]{:S(2)}, u32[]{:S(2)}) collective-permute-start(bf16[2,256,256]{2,1,0:T(8,128)(2,1)S(1)} %collective-permute-done.7.refs_1_), channel_id=1, source_target_pairs={{8,0},{16,8},{24,16},{28,24},{20,28},{12,20},{4,12},{0,4},{9,1},{1... | collective-permute-start | bytes 786440 | tf_op jit(solution)/shard_map/ppermute | solution.py:386
  30.1 9.0 %collective-permute-start.5 = (bf16[2,256,256]{2,1,0:T(8,128)(2,1)S(1)}, bf16[2,256,256]{2,1,0:T(8,128)(2,1)S(1)}, u32[]{:S(2)}, u32[]{:S(2)}) collective-permute-start(bf16[2,256,256]{2,1,0:T(8,128)(2,1)S(1)} %collective-permute-done.1.refs_0_), channel_id=1, source_target_pairs={{0,8},{8,16},{16,24},{24,28},{28,20},{20,12},{12,4},{4,0},{1,9},{9... | collective-permute-start | bytes 786440 | tf_op jit(solution)/shard_map/ppermute | solution.py:386
  32.1 10.9 %collective-permute-start.13 = (bf16[2,256,256]{2,1,0:T(8,128)(2,1)S(1)}, bf16[2,256,256]{2,1,0:T(8,128)(2,1)S(1)}, u32[]{:S(2)}, u32[]{:S(2)}) collective-permute-start(bf16[2,256,256]{2,1,0:T(8,128)(2,1)S(1)} %collective-permute-done.8.refs_1_), channel_id=1, source_target_pairs={{8,0},{16,8},{24,16},{28,24},{20,28},{12,20},{4,12},{0,4},{9,1},{1... | collective-permute-start | bytes 786440 | tf_op jit(solution)/shard_map/ppermute | solution.py:386
  33.7 11.7 %collective-permute-start.12 = (bf16[2,256,256]{2,1,0:T(8,128)(2,1)S(1)}, bf16[2,256,256]{2,1,0:T(8,128)(2,1)S(1)}, u32[]{:S(2)}, u32[]{:S(2)}) collective-permute-start(bf16[2,256,256]{2,1,0:T(8,128)(2,1)S(1)} %collective-permute-done.6.refs_0_), channel_id=1, source_target_pairs={{0,8},{8,16},{16,24},{24,28},{28,20},{20,12},{12,4},{4,0},{1,9},{9... | collective-permute-start | bytes 786440 | tf_op jit(solution)/shard_map/ppermute | solution.py:386
  39.1 8.6 %collective-permute-start.11 = (bf16[2,256,256]{2,1,0:T(8,128)(2,1)S(1)}, bf16[2,256,256]{2,1,0:T(8,128)(2,1)S(1)}, u32[]{:S(2)}, u32[]{:S(2)}) collective-permute-start(bf16[2,256,256]{2,1,0:T(8,128)(2,1)S(1)} %collective-permute-done.10.refs_1_), channel_id=1, source_target_pairs={{8,0},{16,8},{24,16},{28,24},{20,28},{12,20},{4,12},{0,4},{9,1},{1... | collective-permute-start | bytes 786440 | tf_op jit(solution)/shard_map/ppermute | solution.py:398
  40.7 7.0 %collective-permute-start.9 = (bf16[2,256,256]{2,1,0:T(8,128)(2,1)S(1)}, bf16[2,256,256]{2,1,0:T(8,128)(2,1)S(1)}, u32[]{:S(2)}, u32[]{:S(2)}) collective-permute-start(bf16[2,256,256]{2,1,0:T(8,128)(2,1)S(1)} %collective-permute-done.5.refs_0_), channel_id=1, source_target_pairs={{0,8},{8,16},{16,24},{24,28},{28,20},{20,12},{12,4},{4,0},{1,9},{9... | collective-permute-start | bytes 786440 | tf_op jit(solution)/shard_map/ppermute | solution.py:397
  50.0 9.3 %collective-permute-start.17 = (bf16[64,2048]{1,0:T(8,128)(2,1)S(1)}, bf16[64,2048]{1,0:T(8,128)(2,1)S(1)}, u32[]{:S(2)}, u32[]{:S(2)}) collective-permute-start(bf16[64,2048]{1,0:T(8,128)(2,1)S(1)} %get-tuple-element.91.refs_1_), channel_id=1, source_target_pairs={{8,0},{16,8},{24,16},{28,24},{20,28},{12,20},{4,12},{0,4},{9,1},{1... | collective-permute-start | bytes 786440 | tf_op jit(solution)/shard_map/ppermute | solution.py:386
  51.6 9.2 %collective-permute-start.14 = (bf16[64,2048]{1,0:T(8,128)(2,1)S(1)}, bf16[64,2048]{1,0:T(8,128)(2,1)S(1)}, u32[]{:S(2)}, u32[]{:S(2)}) collective-permute-start(bf16[64,2048]{1,0:T(8,128)(2,1)S(1)} %get-tuple-element.90.refs_0_), channel_id=1, source_target_pairs={{0,8},{8,16},{16,24},{24,28},{28,20},{20,12},{12,4},{4,0},{1,9},{9... | collective-permute-start | bytes 786440 | tf_op jit(solution)/shard_map/ppermute | solution.py:386
  52.1 12.8 %collective-permute-start.16 = (bf16[64,2048]{1,0:T(8,128)(2,1)S(1)}, bf16[64,2048]{1,0:T(8,128)(2,1)S(1)}, u32[]{:S(2)}, u32[]{:S(2)}) collective-permute-start(bf16[64,2048]{1,0:T(8,128)(2,1)S(1)} %get-tuple-element.90.refs_0_), channel_id=1, source_target_pairs={{8,0},{16,8},{24,16},{28,24},{20,28},{12,20},{4,12},{0,4},{9,1},{1... | collective-permute-start | bytes 786440 | tf_op jit(solution)/shard_map/ppermute | solution.py:386
  53.6 12.8 %collective-permute-start.15 = (bf16[64,2048]{1,0:T(8,128)(2,1)S(1)}, bf16[64,2048]{1,0:T(8,128)(2,1)S(1)}, u32[]{:S(2)}, u32[]{:S(2)}) collective-permute-start(bf16[64,2048]{1,0:T(8,128)(2,1)S(1)} %get-tuple-element.91.refs_1_), channel_id=1, source_target_pairs={{0,8},{8,16},{16,24},{24,28},{28,20},{20,12},{12,4},{4,0},{1,9},{9... | collective-permute-start | bytes 786440 | tf_op jit(solution)/shard_map/ppermute | solution.py:386
  59.3 11.2 %collective-permute-start.22 = (bf16[64,2048]{1,0:T(8,128)(2,1)S(1)}, bf16[64,2048]{1,0:T(8,128)(2,1)S(1)}, u32[]{:S(2)}, u32[]{:S(2)}) collective-permute-start(bf16[64,2048]{1,0:T(8,128)(2,1)S(1)} %collective-permute-done.17.refs_5_), channel_id=1, source_target_pairs={{8,0},{16,8},{24,16},{28,24},{20,28},{12,20},{4,12},{0,4},{9,1},{1... | collective-permute-start | bytes 786440 | tf_op jit(solution)/shard_map/ppermute | solution.py:386
  60.9 11.2 %collective-permute-start.18 = (bf16[64,2048]{1,0:T(8,128)(2,1)S(1)}, bf16[64,2048]{1,0:T(8,128)(2,1)S(1)}, u32[]{:S(2)}, u32[]{:S(2)}) collective-permute-start(bf16[64,2048]{1,0:T(8,128)(2,1)S(1)} %collective-permute-done.14.refs_2_), channel_id=1, source_target_pairs={{0,8},{8,16},{16,24},{24,28},{28,20},{20,12},{12,4},{4,0},{1,9},{9... | collective-permute-start | bytes 786440 | tf_op jit(solution)/shard_map/ppermute | solution.py:386
  64.9 11.2 %collective-permute-start.21 = (bf16[64,2048]{1,0:T(8,128)(2,1)S(1)}, bf16[64,2048]{1,0:T(8,128)(2,1)S(1)}, u32[]{:S(2)}, u32[]{:S(2)}) collective-permute-start(bf16[64,2048]{1,0:T(8,128)(2,1)S(1)} %collective-permute-done.16.refs_4_), channel_id=1, source_target_pairs={{8,0},{16,8},{24,16},{28,24},{20,28},{12,20},{4,12},{0,4},{9,1},{1... | collective-permute-start | bytes 786440 | tf_op jit(solution)/shard_map/ppermute | solution.py:386
  66.5 11.2 %collective-permute-start.20 = (bf16[64,2048]{1,0:T(8,128)(2,1)S(1)}, bf16[64,2048]{1,0:T(8,128)(2,1)S(1)}, u32[]{:S(2)}, u32[]{:S(2)}) collective-permute-start(bf16[64,2048]{1,0:T(8,128)(2,1)S(1)} %collective-permute-done.15.refs_3_), channel_id=1, source_target_pairs={{0,8},{8,16},{16,24},{24,28},{28,20},{20,12},{12,4},{4,0},{1,9},{9... | collective-permute-start | bytes 786440 | tf_op jit(solution)/shard_map/ppermute | solution.py:386
  70.5 10.5 %collective-permute-start.24 = (bf16[64,2048]{1,0:T(8,128)(2,1)S(1)}, bf16[64,2048]{1,0:T(8,128)(2,1)S(1)}, u32[]{:S(2)}, u32[]{:S(2)}) collective-permute-start(bf16[64,2048]{1,0:T(8,128)(2,1)S(1)} %collective-permute-done.22.refs_3_), channel_id=1, source_target_pairs={{8,0},{16,8},{24,16},{28,24},{20,28},{12,20},{4,12},{0,4},{9,1},{1... | collective-permute-start | bytes 786440 | tf_op jit(solution)/shard_map/ppermute | solution.py:386
  72.1 10.5 %collective-permute-start.19 = (bf16[64,2048]{1,0:T(8,128)(2,1)S(1)}, bf16[64,2048]{1,0:T(8,128)(2,1)S(1)}, u32[]{:S(2)}, u32[]{:S(2)}) collective-permute-start(bf16[64,2048]{1,0:T(8,128)(2,1)S(1)} %collective-permute-done.18.refs_0_), channel_id=1, source_target_pairs={{0,8},{8,16},{16,24},{24,28},{28,20},{20,12},{12,4},{4,0},{1,9},{9... | collective-permute-start | bytes 786440 | tf_op jit(solution)/shard_map/ppermute | solution.py:386
  76.1 8.6 %collective-permute-start.27 = (bf16[64,2048]{1,0:T(8,128)(2,1)S(1)}, bf16[64,2048]{1,0:T(8,128)(2,1)S(1)}, u32[]{:S(2)}, u32[]{:S(2)}) collective-permute-start(bf16[64,2048]{1,0:T(8,128)(2,1)S(1)} %collective-permute-done.21.refs_2_), channel_id=1, source_target_pairs={{8,0},{16,8},{24,16},{28,24},{20,28},{12,20},{4,12},{0,4},{9,1},{1... | collective-permute-start | bytes 786440 | tf_op jit(solution)/shard_map/ppermute | solution.py:386
  77.7 8.6 %collective-permute-start.26 = (bf16[64,2048]{1,0:T(8,128)(2,1)S(1)}, bf16[64,2048]{1,0:T(8,128)(2,1)S(1)}, u32[]{:S(2)}, u32[]{:S(2)}) collective-permute-start(bf16[64,2048]{1,0:T(8,128)(2,1)S(1)} %collective-permute-done.20.refs_1_), channel_id=1, source_target_pairs={{0,8},{8,16},{16,24},{24,28},{28,20},{20,12},{12,4},{4,0},{1,9},{9... | collective-permute-start | bytes 786440 | tf_op jit(solution)/shard_map/ppermute | solution.py:386
  78.2 12.5 %collective-permute-start.28 = (bf16[3,64,1024]{2,1,0:T(8,128)(2,1)S(1)}, bf16[3,64,1024]{2,1,0:T(8,128)(2,1)S(1)}, u32[]{:S(2)}, u32[]{:S(2)}) collective-permute-start(bf16[3,64,1024]{2,1,0:T(8,128)(2,1)S(1)} %get-tuple-element.93), channel_id=1, source_target_pairs={{0,1},{1,0},{2,3},{3,2},{4,5},{5,4},{6,7},{7,6},{8,9},{9,8},{10,11... | collective-permute-start | bytes 1179656 | tf_op jit(solution)/shard_map/ppermute | solution.py:423
  81.0 8.4 %collective-permute-start.25 = (bf16[64,2048]{1,0:T(8,128)(2,1)S(1)}, bf16[64,2048]{1,0:T(8,128)(2,1)S(1)}, u32[]{:S(2)}, u32[]{:S(2)}) collective-permute-start(bf16[64,2048]{1,0:T(8,128)(2,1)S(1)} %collective-permute-done.24.refs_3_), channel_id=1, source_target_pairs={{8,0},{16,8},{24,16},{28,24},{20,28},{12,20},{4,12},{0,4},{9,1},{1... | collective-permute-start | bytes 786440 | tf_op jit(solution)/shard_map/ppermute | solution.py:398
  82.6 8.1 %collective-permute-start.23 = (bf16[64,2048]{1,0:T(8,128)(2,1)S(1)}, bf16[64,2048]{1,0:T(8,128)(2,1)S(1)}, u32[]{:S(2)}, u32[]{:S(2)}) collective-permute-start(bf16[64,2048]{1,0:T(8,128)(2,1)S(1)} %collective-permute-done.19.refs_0_), channel_id=1, source_target_pairs={{0,8},{8,16},{16,24},{24,28},{28,20},{20,12},{12,4},{4,0},{1,9},{9... | collective-permute-start | bytes 786440 | tf_op jit(solution)/shard_map/ppermute | solution.py:397
  84.7 6.0 %collective-permute-start.29 = (bf16[2,64,1024]{2,1,0:T(8,128)(2,1)S(1)}, bf16[2,64,1024]{2,1,0:T(8,128)(2,1)S(1)}, u32[]{:S(2)}, u32[]{:S(2)}) collective-permute-start(bf16[2,64,1024]{2,1,0:T(8,128)(2,1)S(1)} %get-tuple-element.95), channel_id=1, source_target_pairs={{0,1},{1,0},{2,3},{3,2},{4,5},{5,4},{6,7},{7,6},{8,9},{9,8},{10,11... | collective-permute-start | bytes 786440 | tf_op jit(solution)/shard_map/ppermute | solution.py:423
  91.3 12.8 %collective-permute-start.31 = (bf16[3,64,1024]{2,1,0:T(8,128)(2,1)S(1)}, bf16[3,64,1024]{2,1,0:T(8,128)(2,1)S(1)}, u32[]{:S(2)}, u32[]{:S(2)}) collective-permute-start(bf16[3,64,1024]{2,1,0:T(8,128)(2,1)S(1)} %get-tuple-element.106), channel_id=1, source_target_pairs={{0,2},{1,3},{2,0},{3,1},{4,6},{5,7},{6,4},{7,5},{8,10},{9,11},{10,... | collective-permute-start | bytes 1179656 | tf_op jit(solution)/shard_map/ppermute | solution.py:434
  95.1 9.0 %collective-permute-start.33 = (bf16[1,64,1024]{2,1,0:T(8,128)(2,1)S(1)}, bf16[1,64,1024]{2,1,0:T(8,128)(2,1)S(1)}, u32[]{:S(2)}, u32[]{:S(2)}) collective-permute-start(bf16[1,64,1024]{2,1,0:T(8,128)(2,1)S(1)} %get-tuple-element.112), channel_id=1, source_target_pairs={{0,2},{1,3},{2,0},{3,1},{4,6},{5,7},{6,4},{7,5},{8,10},{9,11},{10,... | collective-permute-start | bytes 393224 | tf_op jit(solution)/shard_map/ppermute | solution.py:434
  (9 other events, 74.4 us)
